TPU v7x, 128 devices: a whole 4x4x4 slice. The times are simulated.
128 devices in a mesh: dev: 128 (over x, z, y, core).
Axes of the slice: x: 4, y: 4, z: 4, core: 2. Of those that a mesh axis runs over, the one named last changes fastest.
Arguments:
- entity_table: float32 [131072, 400], P('dev'), may hold values from -2.1 to 2.1
- entity_state: float32 [131072], P('dev'), may hold values from 0.01 to 1
- relation_table: float32 [7424, 400], P('dev'), may hold values from -3.6 to 3.6
- relation_state: float32 [7424], P('dev'), may hold values from 0.01 to 1
- heads: int32 [262144], P('dev'), may hold values from 0 to 1023
- relations: int32 [262144], P('dev'), may hold values from 0 to 7423
- tails: int32 [262144], P('dev'), may hold values from 0 to 3071, as said below
- pull_lists: int32 [16384, 16], P('dev'), may hold values from 0 to 1023, as said below
- negatives: int32 [1024], P('dev'), may hold values from 0 to 1023
Outputs:
- new_entity_table: float32 [131072, 400], P('dev')
- new_entity_state: float32 [131072], P('dev')
- new_relation_table: float32 [7424, 400], P('dev')
- new_relation_state: float32 [7424], P('dev')
Inputs may be any that keep to these rules, and one draw needn't show every extreme that they name: `pull_lists`: for partitions q != p, the first c entries of row q * 128 + p are distinct rows that q needs, 1 <= c <= 16; the last partition and a partition drawn from the seed (possibly the same one) are asked for exactly 16 rows by every other partition; row q * 128 + q asks for nothing; entries past c are valid rows that no edge names. `tails`: A value below 1024 is a row of the edge's own partition; a value 1024 + p * 16 + j names entry j of the edge's partition's pull list to partition p, only entries in its first c; every such entry is named by some edge of that partition.
All inputs are finite; a program needn't handle non-finite values.
Results may differ from a plain program's by a relative error of at most 0.0001.
Values sent between devices are 32-bit elements; how exact they have to be, the bound alone decides.
No kernel may reach another device: no remote copies, remote signals or barrier semaphores. Data moves between devices by JAX's collectives and lax.ppermute only.
A program may use at most 192 MiB of HBM per device.

v0:
```python
import jax
import jax.numpy as jnp
from jax import lax
from jax.sharding import PartitionSpec as P

highest = lax.Precision.HIGHEST
rate = 0.1


def complex_product(left, right):
    half = left.shape[1] // 2
    left_re, left_im = (left[:, :half], left[:, half:])
    right_re, right_im = (right[:, :half], right[:, half:])
    return jnp.concatenate(
        [left_re * right_re - left_im * right_im, left_re * right_im + left_im * right_re], axis=1
    )


def conj_product(grads, other):
    half = grads.shape[1] // 2
    grad_re, grad_im = (grads[:, :half], grads[:, half:])
    other_re, other_im = (other[:, :half], other[:, half:])
    return jnp.concatenate(
        [grad_re * other_re + grad_im * other_im, grad_im * other_re - grad_re * other_im], axis=1
    )


def edge_terms(head_rows, rel_rows, tail_rows, neg_rows):
    query = complex_product(head_rows, rel_rows)
    positive = jnp.sum(query * tail_rows, axis=1)
    negative = lax.dot_general(
        query,
        neg_rows,
        (((1,), (1,)), ((), ())),
        precision=highest,
        preferred_element_type=jnp.float32,
    )
    pos_grad = jax.nn.sigmoid(positive) - 1.0
    neg_grad = jax.nn.sigmoid(negative) / neg_rows.shape[0]
    query_grad = pos_grad[:, None] * tail_rows + jnp.dot(
        neg_grad, neg_rows, precision=highest, preferred_element_type=jnp.float32
    )
    tail_grad = pos_grad[:, None] * query
    negs_grad = lax.dot_general(
        neg_grad,
        query,
        (((0,), (0,)), ((), ())),
        precision=highest,
        preferred_element_type=jnp.float32,
    )
    head_grad = conj_product(query_grad, rel_rows)
    rel_grad = conj_product(query_grad, head_rows)
    return (head_grad, rel_grad, tail_grad, negs_grad)


def adagrad(rows, state, grads):
    new_state = state + jnp.mean(grads * grads, axis=1)
    return (rows - rate * grads / (jnp.sqrt(new_state)[:, None] + 1e-10), new_state)


def local(
    entity_table,
    entity_state,
    relation_table,
    relation_state,
    heads,
    relations,
    tails,
    pull_lists,
    negatives,
):
    ent_rows = entity_table.shape[0]
    width = entity_table.shape[1]
    neg_local = entity_table[negatives]
    relation_full, neg_rows = (
        lax.all_gather(relation_table, "dev", axis=0, tiled=True),
        lax.all_gather(neg_local, "dev", axis=0, tiled=True),
    )
    asked = lax.all_to_all(pull_lists, "dev", split_axis=0, concat_axis=0, tiled=True)
    rows_out = entity_table[asked]
    fetched = lax.all_to_all(rows_out, "dev", split_axis=0, concat_axis=0, tiled=True)
    slots_total = fetched.shape[0] * fetched.shape[1]
    extended = jnp.concatenate([entity_table, fetched.reshape(slots_total, width)], axis=0)
    head_grad, rel_grad, tail_grad, negs_grad = edge_terms(
        entity_table[heads], relation_full[relations], extended[tails], neg_rows
    )
    extended_grad = jnp.zeros(extended.shape, jnp.float32).at[tails].add(tail_grad)
    local_grad = extended_grad[:ent_rows].at[heads].add(head_grad)
    outgoing = extended_grad[ent_rows:].reshape(fetched.shape)
    returned = lax.all_to_all(outgoing, "dev", split_axis=0, concat_axis=0, tiled=True)
    local_grad = local_grad.at[asked.reshape(slots_total)].add(returned.reshape(slots_total, width))
    relation_grad = jnp.zeros(relation_full.shape, jnp.float32).at[relations].add(rel_grad)
    neg_share, rel_share = (
        lax.psum_scatter(negs_grad, "dev", scatter_dimension=0, tiled=True),
        lax.psum_scatter(relation_grad, "dev", scatter_dimension=0, tiled=True),
    )
    local_grad = local_grad.at[negatives].add(neg_share)
    new_entity_table, new_entity_state = adagrad(entity_table, entity_state, local_grad)
    new_relation_table, new_relation_state = adagrad(relation_table, relation_state, rel_share)
    return (new_entity_table, new_entity_state, new_relation_table, new_relation_state)


def solution(mesh):
    in_specs = (
        P("dev", None),
        P("dev"),
        P("dev", None),
        P("dev"),
        P("dev"),
        P("dev"),
        P("dev"),
        P("dev", None),
        P("dev"),
    )
    out_specs = (P("dev", None), P("dev"), P("dev", None), P("dev"))
    return jax.shard_map(local, mesh=mesh, in_specs=in_specs, out_specs=out_specs, check_vma=False)
```

profile of v0, /device:TPU:0, one launch (start us, length us, event | category | flops | bytes accessed | tf_op | source)
XLA Modules:
  0.0 957.7 jit_solution(1438659487644742655)
XLA Ops:
  9.3 11.1 %all-to-all-start = ((s32[128,1,16]{2,1,0:T(1,128)}), s32[128,1,16]{2,1,0:T(1,128)S(1)}, u32[]{:S(2)}, u32[]{:S(2)}) async-start(s32[128,1,16]{2,1,0:T(1,128)} %bitcast.1), calls=%async_computation | async-start | bytes 131072 | tf_op jit(solution)/shard_map/all_to_all | solution.py:79
  20.5 1.8 copy.53
  22.3 7.4 all-to-all-done
  29.8 8.9 gather_fusion.2
  38.7 6.0 all-to-all-start.1
  46.0 8.9 gather_fusion
  54.9 5.2 fusion.9
  60.1 2.9 copy.56
  63.0 2.8 copy.58
  65.8 37.0 %all-to-all-done.1 = f32[128,16,400]{2,1,0:T(8,128)} async-done(((f32[128,16,400]{2,1,0:T(8,128)}), f32[128,16,400]{2,1,0:T(8,128)}, u32[]{:S(2)}, u32[]{:S(2)}) %all-to-all-start.1) | async-done | bytes 3276832 | tf_op jit(solution)/shard_map/all_to_all | solution.py:81
  102.9 5.8 pad_maximum_fusion
  108.7 12.4 %gather_fusion.3 = f32[2048,400]{1,0:T(8,128)} fusion(f32[3072,400]{1,0:T(8,128)} %pad_maximum_fusion, s32[2048]{0:T(1024)S(1)} %get-tuple-element.32), kind=kCustom, calls=%fused_computation.3 | custom fusion | bytes 6561792 | tf_op jit(solution)/shard_map/gather | solution.py:85
  121.1 5.4 copy.48
  126.5 7.7 all-gather.7.cloned.1.call-done
  134.2 15.5 %reshape.185 = f32[7424,400]{1,0:T(8,128)} reshape(f32[128,58,400]{2,1,0:T(8,128)} %all-gather.7.cloned.1.call-done) | data formatting | bytes 23756800
  149.7 14.9 %gather_fusion.1 = f32[2048,400]{1,0:T(8,128)} fusion(f32[7424,400]{1,0:T(8,128)} %reshape.185, s32[2048]{0:T(1024)S(1)} %get-tuple-element.29), kind=kCustom, calls=%fused_computation.1 | custom fusion | bytes 6561792 | tf_op jit(solution)/shard_map/gather | solution.py:85
  164.5 5.2 fusion.8
  169.7 2.9 copy.59
  172.6 2.8 copy.57
  175.4 3.7 multiply_subtract_fusion.2
  180.8 2.1 broadcast_multiply_fusion
  182.9 5.0 copy.49
  187.8 16.2 %scatter_custom_fusion = f32[3072,400]{1,0:T(8,128)} fusion(s32[2048]{0:T(1024)S(1)} %get-tuple-element.33, f32[2048,400]{1,0:T(8,128)} %copy.49, f32[]{:T(128)} %constant.11.clone.1), kind=kCustom, calls=%fused_computation.19 | custom fusion | flops 819200 | bytes 4915712 | tf_op jit(solution)/shard_map/scatter-add | solution.py:87
  204.0 4.7 slice.55
  208.7 8.7 all-to-all-start.2
  217.6 30.7 %divide_multiply_fusion = f32[2048,1024]{1,0:T(8,128)S(1)} fusion(f32[1024,400]{1,0:T(8,128)} %all-gather.5.cloned.1.call-done, f32[2048,200]{0,1:T(8,128)} %copy-done.5, f32[2048,200]{0,1:T(8,128)} %copy-done.3), kind=kOutput, calls=%fused_computation.10 | convolution fusion | flops 10075537408 | bytes 13303808 | tf_op jit(solution)/shard_map/dot_general | solution.py:31
  248.3 3.2 copy-done.2
  251.5 27.9 %fusion.5 = f32[1024,400]{1,0:T(8,128)} fusion(f32[2048,1024]{1,0:T(8,128)S(1)} %divide_multiply_fusion, f32[2048,200]{0,1:T(8,128)S(1)} %copy-done.6, f32[2048,200]{0,1:T(8,128)S(1)} %copy-done.4), kind=kOutput, calls=%fused_computation.30 | convolution fusion | flops 10067148800 | bytes 13303808 | tf_op jit(solution)/shard_map/dot_general | solution.py:44
  279.5 14.4 %multiply_add_fusion = f32[2048,400]{0,1:T(8,128)S(1)} fusion(f32[2048,400]{0,1:T(8,128)} %copy.48, f32[2048,1024]{1,0:T(8,128)} %copy-done.2, f32[1024,400]{1,0:T(8,128)} %all-gather.5.cloned.1.call-done, f32[2048]{0:T(1024)S(1)} %divide_add_fusion), kind=kOutput, calls=%fused_computation.17 | convolution fusion | flops 10067968000 | bytes 16588800 | tf_op jit(solution)/shard_map/dot_general | solution.py:40
  293.9 4.0 multiply_add_fusion.1
  298.0 6.4 pad_maximum_fusion.2
  304.4 5.0 copy.54
  309.4 19.8 %scatter_custom_fusion.4 = f32[7424,400]{1,0:T(8,128)} fusion(s32[2048]{0:T(1024)S(1)} %get-tuple-element.28, f32[2048,400]{1,0:T(8,128)} %copy.54, f32[]{:T(128)} %constant.11.clone.1), kind=kCustom, calls=%fused_computation.11 | custom fusion | flops 819200 | bytes 11878912 | tf_op jit(solution)/shard_map/scatter-add | solution.py:92
  329.1 367.3 %fusion = f32[64,400]{1,0:T(8,128)S(1)} fusion(f32[7424,400]{1,0:T(8,128)} %scatter_custom_fusion.4), kind=kCustom, calls=%all-reduce-scatter | all-reduce-scatter fusion | flops 3276801 | bytes 11980800
  707.0 7.4 collective-permute-start.4
  715.8 4.4 collective-permute-start.2
  720.1 2.5 collective-permute-start.1
  722.6 2.4 collective-permute-start
  725.1 3.1 slice.52
  728.1 5.0 copy.52
  733.1 16.1 %scatter_fusion = f32[1024,400]{1,0:T(8,128)} fusion(f32[1024,400]{1,0:T(8,128)} %slice.52, s32[2048]{0:T(1024)S(1)} %get-tuple-element.30, f32[2048,400]{1,0:T(8,128)} %copy.52), kind=kCustom, calls=%fused_computation.6 | custom fusion | flops 819200 | bytes 9838592 | tf_op jit(solution)/shard_map/scatter-add | solution.py:88
  749.2 18.6 %concatenate.16 = f32[826,400]{1,0:T(8,128)} concatenate(f32[58,400]{1,0:T(8,128)S(1)} %collective-permute-done.11, f32[64,400]{1,0:T(8,128)S(1)} %collective-permute-done.10, f32[64,400]{1,0:T(8,128)S(1)} %collective-permute-done.9, f32[64,400]{1,0:T(8,128)S(1)} %collective-permute-done.8, f32[64,400]{1,0:T(8,128)S(1)} %collective-permute-done.7, ...), dimensions={0} | concatenate | bytes 2643200
  771.0 16.1 %scatter_fusion.1 = f32[1024,400]{1,0:T(8,128)} fusion(f32[1024,400]{1,0:T(8,128)} %scatter_fusion, s32[2048]{0:T(1024)S(1)} %bitcast.18, f32[2048,400]{1,0:T(8,128)} %bitcast.7), kind=kCustom, calls=%fused_computation.7 | custom fusion | flops 819200 | bytes 9838592 | tf_op jit(solution)/shard_map/scatter-add | solution.py:91
  787.1 152.8 %reduce-scatter.4.cloned.1.call-done = f32[8,400]{1,0:T(8,128)} async-done(((f32[1024,400]{1,0:T(8,128)}), f32[8,400]{1,0:T(8,128)}) %reduce-scatter.4.cloned.1.call-update) | async-done | bytes 12816 | tf_op jit(solution)/shard_map/reduce_scatter | solution.py:94
  940.0 3.7 scatter_fusion.2
  943.6 2.0 multiply_reduce_fusion.1
  946.2 1.8 divide_subtract_fusion
  947.9 2.7 copy.55
  (88 shorter events, 21.0 us)
Async XLA Ops:
  7.2 127.0 %all-gather.7.cloned.1.call-start = ((), (), s32[]{:S(2)}) async-start(), calls=%async_computation.6 | async-start | bytes 16908288 | tf_op jit(solution)/shard_map/all_gather | solution.py:76
  9.3 20.4 %all-to-all-start = ((s32[128,1,16]{2,1,0:T(1,128)}), s32[128,1,16]{2,1,0:T(1,128)S(1)}, u32[]{:S(2)}, u32[]{:S(2)}) async-start(s32[128,1,16]{2,1,0:T(1,128)} %bitcast.1), calls=%async_computation | async-start | bytes 131072 | tf_op jit(solution)/shard_map/all_to_all | solution.py:79
  38.7 6.0 copy-start.19
  38.7 7.3 copy-start.12
  38.7 64.1 %all-to-all-start.1 = ((f32[128,16,400]{2,1,0:T(8,128)}), f32[128,16,400]{2,1,0:T(8,128)}, u32[]{:S(2)}, u32[]{:S(2)}) async-start(f32[128,16,400]{2,1,0:T(8,128)} %bitcast.14), calls=%async_computation.1 | async-start | bytes 8388608 | tf_op jit(solution)/shard_map/all_to_all | solution.py:81
  44.7 172.8 %all-gather.5.cloned.1.call-start = ((), (), s32[]{:S(2)}) async-start(), calls=%async_computation.5 | async-start | bytes 2113536 | tf_op jit(solution)/shard_map/all_gather | solution.py:77
  44.8 1.2 copy-start.16
  60.1 5.7 copy-start.13
  60.1 5.7 copy-start.14
  175.4 3.9 copy-start.1
  179.1 1.2 copy-start.3
  179.1 1.7 copy-start.5
  208.7 562.3 %all-to-all-start.2 = ((f32[128,16,400]{2,1,0:T(8,128)}), f32[128,16,400]{2,1,0:T(8,128)}, u32[]{:S(2)}, u32[]{:S(2)}) async-start(f32[128,16,400]{2,1,0:T(8,128)} %bitcast.15), calls=%async_computation.2 | async-start | bytes 8388608 | tf_op jit(solution)/shard_map/all_to_all | solution.py:90
  217.5 722.5 %reduce-scatter.4.cloned.1.call-start = ((), (), s32[]{:S(2)}) async-start(), calls=%async_computation.4 | async-start | bytes 2113536 | tf_op jit(solution)/shard_map/reduce_scatter | solution.py:94
  217.5 34.0 %copy-start.4 = (f32[2048,200]{0,1:T(8,128)S(1)}, f32[2048,200]{0,1:T(8,128)}, u32[]{:S(2)}) copy-start(f32[2048,200]{0,1:T(8,128)} %copy-done.3) | copy-start | bytes 4915204
  217.6 34.0 %copy-start.6 = (f32[2048,200]{0,1:T(8,128)S(1)}, f32[2048,200]{0,1:T(8,128)}, u32[]{:S(2)}) copy-start(f32[2048,200]{0,1:T(8,128)} %copy-done.5) | copy-start | bytes 4915204
  248.3 3.2 copy-start.2
  279.4 14.4 %copy-start.7 = (f32[2048,200]{0,1:T(8,128)S(1)}, f32[2048,200]{0,1:T(8,128)}, u32[]{:S(2)}) copy-start(f32[2048,200]{0,1:T(8,128)} %copy.56) | copy-start | bytes 4915204
  279.4 14.4 %copy-start.8 = (f32[2048,200]{0,1:T(8,128)S(1)}, f32[2048,200]{0,1:T(8,128)}, u32[]{:S(2)}) copy-start(f32[2048,200]{0,1:T(8,128)} %copy.58) | copy-start | bytes 4915204
  279.5 14.4 %copy-start.9 = (f32[2048,200]{0,1:T(8,128)S(1)}, f32[2048,200]{0,1:T(8,128)}, u32[]{:S(2)}) copy-start(f32[2048,200]{0,1:T(8,128)} %copy.59) | copy-start | bytes 4915204
  279.5 14.4 %copy-start.10 = (f32[2048,200]{0,1:T(8,128)S(1)}, f32[2048,200]{0,1:T(8,128)}, u32[]{:S(2)}) copy-start(f32[2048,200]{0,1:T(8,128)} %copy.57) | copy-start | bytes 4915204
  696.4 7.9 collective-permute-start.10
  697.7 5.2 collective-permute-start.11
  699.0 8.0 collective-permute-start.9
  700.3 14.1 %collective-permute-start.8 = (f32[64,400]{1,0:T(8,128)S(1)}, f32[64,400]{1,0:T(8,128)S(1)}, u32[]{:S(2)}, u32[]{:S(2)}) collective-permute-start(f32[64,400]{1,0:T(8,128)S(1)} %fusion), channel_id=1, source_target_pairs={{0,9},{1,10},{2,11},{3,12},{4,13},{5,14},{6,15},{7,16},{8,17},{9,1... | collective-permute-start | bytes 307208
  701.6 14.1 %collective-permute-start.7 = (f32[64,400]{1,0:T(8,128)S(1)}, f32[64,400]{1,0:T(8,128)S(1)}, u32[]{:S(2)}, u32[]{:S(2)}) collective-permute-start(f32[64,400]{1,0:T(8,128)S(1)} %fusion), channel_id=1, source_target_pairs={{0,8},{1,9},{2,10},{3,11},{4,12},{5,13},{6,14},{7,15},{8,16},{9,17... | collective-permute-start | bytes 307208
  703.0 17.2 %collective-permute-start.6 = (f32[64,400]{1,0:T(8,128)S(1)}, f32[64,400]{1,0:T(8,128)S(1)}, u32[]{:S(2)}, u32[]{:S(2)}) collective-permute-start(f32[64,400]{1,0:T(8,128)S(1)} %fusion), channel_id=1, source_target_pairs={{0,7},{1,8},{2,9},{3,10},{4,11},{5,12},{6,13},{7,14},{8,15},{9,16}... | collective-permute-start | bytes 307208
  704.3 18.4 %collective-permute-start.5 = (f32[64,400]{1,0:T(8,128)S(1)}, f32[64,400]{1,0:T(8,128)S(1)}, u32[]{:S(2)}, u32[]{:S(2)}) collective-permute-start(f32[64,400]{1,0:T(8,128)S(1)} %fusion), channel_id=1, source_target_pairs={{0,6},{1,7},{2,8},{3,9},{4,10},{5,11},{6,12},{7,13},{8,14},{9,15},... | collective-permute-start | bytes 307208
  707.0 42.2 %collective-permute-start.4 = (f32[64,400]{1,0:T(8,128)S(1)}, f32[64,400]{1,0:T(8,128)S(1)}, u32[]{:S(2)}, u32[]{:S(2)}) collective-permute-start(f32[64,400]{1,0:T(8,128)S(1)} %fusion), channel_id=1, source_target_pairs={{0,5},{1,6},{2,7},{3,8},{4,9},{5,10},{6,11},{7,12},{8,13},{9,14},{... | collective-permute-start | bytes 307208
  714.5 34.7 %collective-permute-start.3 = (f32[64,400]{1,0:T(8,128)S(1)}, f32[64,400]{1,0:T(8,128)S(1)}, u32[]{:S(2)}, u32[]{:S(2)}) collective-permute-start(f32[64,400]{1,0:T(8,128)S(1)} %fusion), channel_id=1, source_target_pairs={{0,4},{1,5},{2,6},{3,7},{4,8},{5,9},{6,10},{7,11},{8,12},{9,13},{1... | collective-permute-start | bytes 307208
  715.8 33.4 %collective-permute-start.2 = (f32[64,400]{1,0:T(8,128)S(1)}, f32[64,400]{1,0:T(8,128)}, u32[]{:S(2)}, u32[]{:S(2)}) collective-permute-start(f32[64,400]{1,0:T(8,128)S(1)} %fusion), channel_id=1, source_target_pairs={{0,3},{1,4},{2,5},{3,6},{4,7},{5,8},{6,9},{7,10},{8,11},{9,12},{10... | collective-permute-start | bytes 307208
  720.1 29.1 %collective-permute-start.1 = (f32[64,400]{1,0:T(8,128)S(1)}, f32[64,400]{1,0:T(8,128)}, u32[]{:S(2)}, u32[]{:S(2)}) collective-permute-start(f32[64,400]{1,0:T(8,128)S(1)} %fusion), channel_id=1, source_target_pairs={{0,2},{1,3},{2,4},{3,5},{4,6},{5,7},{6,8},{7,9},{8,10},{9,11},{10,... | collective-permute-start | bytes 307208
  722.6 26.6 %collective-permute-start = (f32[64,400]{1,0:T(8,128)S(1)}, f32[64,400]{1,0:T(8,128)}, u32[]{:S(2)}, u32[]{:S(2)}) collective-permute-start(f32[64,400]{1,0:T(8,128)S(1)} %fusion), channel_id=1, source_target_pairs={{0,1},{1,2},{2,3},{3,4},{4,5},{5,6},{6,7},{7,8},{8,9},{9,10},{10,1... | collective-permute-start | bytes 307208
  749.2 19.7 %copy-start.18 = (f32[58]{0:T(128)S(1)}, f32[58]{0:T(128)}, u32[]{:S(2)}) copy-start(f32[58]{0:T(128)} %param.12) | copy-start | bytes 700
  749.2 20.2 %copy-start.11 = (f32[58,400]{1,0:T(8,128)S(1)}, f32[58,400]{1,0:T(8,128)}, u32[]{:S(2)}) copy-start(f32[58,400]{1,0:T(8,128)} %param.11) | copy-start | bytes 278404
  771.0 168.9 %copy-start.17 = (s32[8]{0:T(128)S(1)}, s32[8]{0:T(128)}, u32[]{:S(2)}) copy-start(s32[8]{0:T(128)} %copy-done.16) | copy-start | bytes 100
  771.0 174.6 %copy-start.15 = (f32[1024]{0:T(1024)S(1)}, f32[1024]{0:T(1024)}, u32[]{:S(2)}) copy-start(f32[1024]{0:T(1024)} %param.10) | copy-start | bytes 12292
  943.6 2.6 copy-start
Sparse Core Ops, SparseCore 0:
  11.1 122.9 all-gather.6
  137.9 64.7 all-gather.4
  298.1 641.8 reduce-scatter.3
where the time goes:
time: 970 us; the launch traced here: 958 us
  blocking collectives  367 us (38%)
  waiting for transfers between devices  206 us (21%)
  local copies, waits for them, and re-layouts  141 us (15%)
  other arithmetic  103 us (11%)
  matrix products  73 us (8%)
  starting transfers between devices  53 us (5%)
  between operations  14.7 us (2%)
    unnamed x1, blocking collectives  367 us
    reduce_scatter x1, waiting for transfers between devices, local(): lax.psum_scatter(negs_grad, 'dev', scatter_dimension=0, tiled=True)  153 us
    unnamed x50, local copies, waits for them, and re-layouts  55.6 us
    all_to_all x1, waiting for transfers between devices, local(): lax.all_to_all(rows_out, 'dev', split_axis=0, concat_axis=0, tiled=True)  37 us
    dot_general x1, matrix products, edge_terms(): lax.dot_general(query, neg_rows, (((1,), (1,)), ((), ())), precision=high...  30.7 us
    dot_general x1, matrix products, edge_terms(): lax.dot_general(neg_grad, query, (((0,), (0,)), ((), ())), precision=high...  27.9 us
    unnamed x12, starting transfers between devices  27.1 us
    scatter-add x1, other arithmetic, local(): jnp.zeros(relation_full.shape, jnp.float32).at[relations].add(rel_grad)  19.8 us
  transfers between devices with their start and end apart: 18, of which 4 were waited for; matrix products, arithmetic and copies ran while one was open for 70% of the time, Pallas kernels for 0%

commit v1 on v0

--- a/solution.py
+++ b/solution.py
@@ -1,7 +1,7 @@
 import jax
 import jax.numpy as jnp
 from jax import lax
-from jax.sharding import PartitionSpec as P
+from jax.sharding import Mesh, PartitionSpec as P
 
 highest = lax.Precision.HIGHEST
 rate = 0.1
@@ -58,6 +58,9 @@
     return (rows - rate * grads / (jnp.sqrt(new_state)[:, None] + 1e-10), new_state)
 
 
+AXES = ("x", "z", "y", "c")
+
+
 def local(
     entity_table,
     entity_state,
@@ -69,31 +72,44 @@
     pull_lists,
     negatives,
 ):
-    ent_rows = entity_table.shape[0]
-    width = entity_table.shape[1]
+    ent_rows, width = entity_table.shape
+    rel_rows = relation_table.shape[0]
+    neg_count = negatives.shape[0]
+    per = rel_rows + neg_count
     neg_local = entity_table[negatives]
-    relation_full, neg_rows = (
-        lax.all_gather(relation_table, "dev", axis=0, tiled=True),
-        lax.all_gather(neg_local, "dev", axis=0, tiled=True),
+    shared = lax.all_gather(
+        jnp.concatenate([relation_table, neg_local], axis=0), AXES, axis=0, tiled=False
     )
-    asked = lax.all_to_all(pull_lists, "dev", split_axis=0, concat_axis=0, tiled=True)
+    n_dev = shared.shape[0]
+    asked = lax.all_to_all(pull_lists, AXES, split_axis=0, concat_axis=0, tiled=True)
     rows_out = entity_table[asked]
-    fetched = lax.all_to_all(rows_out, "dev", split_axis=0, concat_axis=0, tiled=True)
+    fetched = lax.all_to_all(rows_out, AXES, split_axis=0, concat_axis=0, tiled=True)
     slots_total = fetched.shape[0] * fetched.shape[1]
     extended = jnp.concatenate([entity_table, fetched.reshape(slots_total, width)], axis=0)
+    neg_rows = shared[:, rel_rows:].reshape(n_dev * neg_count, width)
+    rel_here = shared[relations // rel_rows, relations % rel_rows]
     head_grad, rel_grad, tail_grad, negs_grad = edge_terms(
-        entity_table[heads], relation_full[relations], extended[tails], neg_rows
+        entity_table[heads], rel_here, extended[tails], neg_rows
     )
     extended_grad = jnp.zeros(extended.shape, jnp.float32).at[tails].add(tail_grad)
     local_grad = extended_grad[:ent_rows].at[heads].add(head_grad)
     outgoing = extended_grad[ent_rows:].reshape(fetched.shape)
-    returned = lax.all_to_all(outgoing, "dev", split_axis=0, concat_axis=0, tiled=True)
+    returned = lax.all_to_all(outgoing, AXES, split_axis=0, concat_axis=0, tiled=True)
     local_grad = local_grad.at[asked.reshape(slots_total)].add(returned.reshape(slots_total, width))
-    relation_grad = jnp.zeros(relation_full.shape, jnp.float32).at[relations].add(rel_grad)
-    neg_share, rel_share = (
-        lax.psum_scatter(negs_grad, "dev", scatter_dimension=0, tiled=True),
-        lax.psum_scatter(relation_grad, "dev", scatter_dimension=0, tiled=True),
+    owner = relations // rel_rows
+    chips = n_dev // 2
+    shared_grad = jnp.zeros((2, chips, per, width), jnp.float32)
+    shared_grad = shared_grad.at[:, :, rel_rows:].set(
+        negs_grad.reshape(chips, 2, neg_count, width).swapaxes(0, 1)
     )
+    shared_grad = shared_grad.at[owner % 2, owner // 2, relations % rel_rows].add(rel_grad)
+    core = lax.axis_index("c")
+    other = lax.ppermute(
+        lax.dynamic_index_in_dim(shared_grad, 1 - core, 0, keepdims=False), "c", [(0, 1), (1, 0)]
+    )
+    paired = lax.dynamic_index_in_dim(shared_grad, core, 0, keepdims=False) + other
+    share = jnp.sum(lax.all_to_all(paired, AXES[:3], split_axis=0, concat_axis=0, tiled=True), axis=0)
+    rel_share, neg_share = share[:rel_rows], share[rel_rows:]
     local_grad = local_grad.at[negatives].add(neg_share)
     new_entity_table, new_entity_state = adagrad(entity_table, entity_state, local_grad)
     new_relation_table, new_relation_state = adagrad(relation_table, relation_state, rel_share)
@@ -101,16 +117,8 @@
 
 
 def solution(mesh):
-    in_specs = (
-        P("dev", None),
-        P("dev"),
-        P("dev", None),
-        P("dev"),
-        P("dev"),
-        P("dev"),
-        P("dev"),
-        P("dev", None),
-        P("dev"),
-    )
-    out_specs = (P("dev", None), P("dev"), P("dev", None), P("dev"))
-    return jax.shard_map(local, mesh=mesh, in_specs=in_specs, out_specs=out_specs, check_vma=False)
+    grid = Mesh(mesh.devices.reshape(4, 4, 4, 2), AXES)
+    rows, flat = P(AXES, None), P(AXES)
+    in_specs = (rows, flat, rows, flat, flat, flat, flat, rows, flat)
+    out_specs = (rows, flat, rows, flat)
+    return jax.shard_map(local, mesh=grid, in_specs=in_specs, out_specs=out_specs, check_vma=False)

time: 970 us -> 641 us (0.66)
  the two profiles are of different devices: /device:TPU:0 before, /device:TPU:22 now
where the time goes in v1:
time: 641 us; the launch traced here: 630 us
  local copies, waits for them, and re-layouts  187 us (29%)
  waiting for transfers between devices  173 us (27%)
  other arithmetic  116 us (18%)
  matrix products  95.5 us (15%)
  starting transfers between devices  27.3 us (4%)
  blocking collectives  16.5 us (3%)
  between operations  14.9 us (2%)
    all_to_all x1, waiting for transfers between devices, local(): lax.all_to_all(paired, AXES[:3], split_axis=0, concat_axis=0, tiled=True)  102 us
    dot_general x1, matrix products, edge_terms(): lax.dot_general(query, neg_rows, (((1,), (1,)), ((), ())), precision=high...  53.1 us
    unnamed x55, local copies, waits for them, and re-layouts  45.2 us
    gather x1, local copies, waits for them, and re-layouts, local(): rel_here = shared[relations // rel_rows, relations % rel_rows]  35.3 us
    all_to_all x1, waiting for transfers between devices, local(): lax.all_to_all(rows_out, AXES, split_axis=0, concat_axis=0, tiled=True)  33.6 us
    dot_general x1, matrix products, edge_terms(): lax.dot_general(neg_grad, query, (((0,), (0,)), ((), ())), precision=high...  28.2 us
    unnamed x5, other arithmetic  26 us
    all_to_all x1, waiting for transfers between devices, local(): lax.all_to_all(outgoing, AXES, split_axis=0, concat_axis=0, tiled=True)  24.9 us
  transfers between devices with their start and end apart: 5, of which 4 were waited for; matrix products, arithmetic and copies ran while one was open for 22% of the time, Pallas kernels for 0%

profile of v1, /device:TPU:22, one launch (start us, length us, event | category | flops | bytes accessed | tf_op | source)
XLA Modules:
  0.0 630.5 jit_solution(118916768171491167)
XLA Ops:
  8.4 1.8 copy.82
  11.8 16.5 %all_to_all.27 = s32[128,1,16]{2,1,0:T(1,128)S(1)} all-to-all(s32[128,1,16]{2,1,0:T(1,128)S(1)} %bitcast.45), channel_id=1, replica_groups=mesh['x'=4,'z'=4,'y'=4,'c'=2] {'x','z','y','c'}, dimensions={0} | all-to-all | bytes 16384 | tf_op jit(solution)/shard_map/all_to_all | solution.py:84
  29.0 8.9 %gather_fusion.3 = f32[2048,400]{1,0:T(8,128)} fusion(f32[1024,400]{1,0:T(8,128)S(1)} %copy.82, s32[2048]{0:T(1024)S(1)} %broadcast_clamp_fusion.1), kind=kCustom, calls=%fused_computation.3 | custom fusion | bytes 6561792 | tf_op jit(solution)/shard_map/gather | solution.py:85
  37.9 8.8 %all-to-all-start.1 = ((f32[128,16,400]{2,1,0:T(8,128)}), f32[128,16,400]{2,1,0:T(8,128)}, u32[]{:S(2)}, u32[]{:S(2)}) async-start(f32[128,16,400]{2,1,0:T(8,128)} %bitcast.41), calls=%async_computation.1 | async-start | bytes 8388608 | tf_op jit(solution)/shard_map/all_to_all | solution.py:86
  47.3 8.8 %gather_fusion = f32[2048,400]{1,0:T(8,128)} fusion(f32[1024,400]{1,0:T(8,128)S(1)} %copy.82, s32[2048]{0:T(1024)S(1)} %get-tuple-element.49), kind=kCustom, calls=%fused_computation | custom fusion | bytes 6561792 | tf_op jit(solution)/shard_map/gather | solution.py:92
  56.1 5.2 fusion.13
  61.3 2.8 copy.85
  64.2 2.8 copy.87
  67.3 33.6 %all-to-all-done.1 = f32[128,16,400]{2,1,0:T(8,128)} async-done(((f32[128,16,400]{2,1,0:T(8,128)}), f32[128,16,400]{2,1,0:T(8,128)}, u32[]{:S(2)}, u32[]{:S(2)}) %all-to-all-start.1) | async-done | bytes 3276832 | tf_op jit(solution)/shard_map/all_to_all | solution.py:86
  100.9 5.5 pad_maximum_fusion
  106.4 13.3 %gather_fusion.4 = f32[2048,400]{1,0:T(8,128)} fusion(f32[3072,400]{1,0:T(8,128)} %pad_maximum_fusion, s32[2048]{0:T(1024)S(1)} %get-tuple-element.50), kind=kCustom, calls=%fused_computation.4 | custom fusion | bytes 6561792 | tf_op jit(solution)/shard_map/gather | solution.py:92
  119.7 5.4 copy.74
  125.1 12.3 %all-gather.4.cloned.1.call-done = f32[128,66,400]{2,1,0:T(8,128)} async-done(((f32[1,66,400]{2,1,0:T(8,128)}), f32[128,66,400]{2,1,0:T(8,128)}) %all-gather.4.cloned.1.call-update) | async-done | bytes 13516816 | tf_op jit(solution)/shard_map/all_gather | solution.py:80
  137.4 18.4 %copy.67 = f32[128,66,400]{2,0,1:T(8,128)} copy(f32[128,66,400]{2,1,0:T(8,128)} %all-gather.4.cloned.1.call-done) | data formatting | bytes 27033600 | tf_op jit(solution)/shard_map/all_gather | solution.py:80
  155.7 35.3 %gather_fusion.2 = f32[2048,400]{1,0:T(8,128)} fusion(f32[128,66,400]{2,0,1:T(8,128)} %copy.67, s32[2048]{0:T(1024)S(1)} %bitcast.40), kind=kCustom, calls=%fused_computation.2 | custom fusion | bytes 6569984 | tf_op jit(solution)/shard_map/gather | solution.py:90
  191.0 4.5 fusion.12
  195.5 2.8 copy.88
  198.3 1.7 copy.86
  200.0 3.7 multiply_subtract_fusion.2
  204.6 53.1 %divide_multiply_fusion = f32[2048,1024]{1,0:T(8,128)S(1)} fusion(f32[128,66,400]{2,1,0:T(8,128)} %all-gather.4.cloned.1.call-done, f32[2048,200]{0,1:T(8,128)S(1)} %get-tuple-element.37, f32[2048,200]{0,1:T(8,128)S(1)} %get-tuple-element.36), kind=kOutput, calls=%fused_computation.13 | convolution fusion | flops 10075537408 | bytes 13762560 | tf_op jit(solution)/shard_map/dot_general | solution.py:31
  257.7 28.2 %fusion.2 = f32[1024,400]{1,0:T(8,128)} fusion(f32[2048,1024]{1,0:T(8,128)S(1)} %divide_multiply_fusion, f32[2048,200]{0,1:T(8,128)S(1)} %get-tuple-element.37, f32[2048,200]{0,1:T(8,128)S(1)} %get-tuple-element.36), kind=kOutput, calls=%fused_computation.32 | convolution fusion | flops 10067148800 | bytes 13303808 | tf_op jit(solution)/shard_map/dot_general | solution.py:44
  286.0 14.2 %multiply_add_fusion = f32[2048,400]{0,1:T(8,128)S(1)} fusion(f32[2048,400]{0,1:T(8,128)S(1)} %copy-done.4, f32[2048,1024]{1,0:T(8,128)S(1)} %divide_multiply_fusion, f32[128,66,400]{2,1,0:T(8,128)} %all-gather.4.cloned.1.call-done, f32[2048]{0:T(1024)S(1)} %divide_add_fusion), kind=kOutput, calls=%fused_computation.18 | convolution fusion | flops 10067968000 | bytes 17047552 | tf_op jit(solution)/shard_map/dot_general | solution.py:40
  300.3 1.9 multiply_add_fusion.1
  302.2 3.5 pad_maximum_fusion.2
  305.7 5.0 copy.80
  310.7 10.6 %pad_bitcast_fusion = f32[2,66,64,400]{3,1,0,2:T(8,128)} fusion(f32[2,64,8,400]{3,2,0,1:T(8,128)} %bitcast.43), kind=kLoop, calls=%fused_computation.10 | loop fusion | bytes 15155200
  321.3 18.5 %copy.79 = f32[2,66,64,400]{3,2,1,0:T(8,128)} copy(f32[2,66,64,400]{3,1,0,2:T(8,128)} %pad_bitcast_fusion) | data formatting | bytes 27033600
  339.8 25.0 %scatter_fusion.2 = f32[8448,400]{1,0:T(8,128)} fusion(f32[8448,400]{1,0:T(8,128)} %bitcast.37, s32[2048]{0:T(1024)S(1)} %broadcast_select_fusion, f32[2048,400]{1,0:T(8,128)} %copy.80), kind=kCustom, calls=%fused_computation.9 | custom fusion | flops 819200 | bytes 9838592
  364.8 8.6 %dynamic-slice_bitcast_fusion = f32[64,66,400]{2,0,1:T(8,128)} fusion(f32[2,66,64,400]{3,2,1,0:T(8,128)} %bitcast.38, s32[]{:T(128)S(6)} %select_n.88), kind=kLoop, calls=%fused_computation.12 | loop fusion | bytes 13516804 | tf_op jit(solution)/shard_map/jit(dynamic_index_in_dim)/squeeze | solution.py:108
  373.7 2.1 broadcast_multiply_fusion
  375.7 5.0 copy.75
  380.7 16.2 %scatter_custom_fusion = f32[3072,400]{1,0:T(8,128)} fusion(s32[2048]{0:T(1024)S(1)} %get-tuple-element.51, f32[2048,400]{1,0:T(8,128)} %copy.75, f32[]{:T(128)} %constant.102.clone.1), kind=kCustom, calls=%fused_computation.20 | custom fusion | flops 819200 | bytes 4915712 | tf_op jit(solution)/shard_map/scatter-add | solution.py:94
  396.9 4.7 slice.94
  401.6 8.5 %all-to-all-start.2 = ((f32[128,16,400]{2,1,0:T(8,128)}), f32[128,16,400]{2,1,0:T(8,128)}, u32[]{:S(2)}, u32[]{:S(2)}) async-start(f32[128,16,400]{2,1,0:T(8,128)} %bitcast.42), calls=%async_computation.2 | async-start | bytes 8388608 | tf_op jit(solution)/shard_map/all_to_all | solution.py:97
  410.2 12.3 %bitcast_add_fusion = f32[64,66,400]{2,0,1:T(8,128)} fusion(f32[64,66,400]{2,0,1:T(8,128)} %collective-permute-done, f32[2,66,64,400]{3,2,1,0:T(8,128)} %bitcast.39, s32[]{:T(128)S(6)} %select_n.87), kind=kLoop, calls=%fused_computation.11 | loop fusion | flops 1689600 | bytes 20275204 | tf_op jit(solution)/shard_map/add | solution.py:110
  422.5 12.2 %copy.81 = f32[64,66,400]{2,1,0:T(8,128)} copy(f32[64,66,400]{2,0,1:T(8,128)} %bitcast_add_fusion) | data formatting | bytes 13516800 | tf_op jit(solution)/shard_map/add | solution.py:110
  434.7 24.9 %all-to-all-done.2 = f32[128,16,400]{2,1,0:T(8,128)} async-done(((f32[128,16,400]{2,1,0:T(8,128)}), f32[128,16,400]{2,1,0:T(8,128)}, u32[]{:S(2)}, u32[]{:S(2)}) %all-to-all-start.2) | async-done | bytes 3276832 | tf_op jit(solution)/shard_map/all_to_all | solution.py:97
  459.5 9.7 %all-to-all-start.3 = ((f32[64,66,400]{2,1,0:T(8,128)}), f32[64,66,400]{2,1,0:T(8,128)}, u32[]{:S(2)}, u32[]{:S(2)}) async-start(f32[64,66,400]{2,1,0:T(8,128)} %copy.81), calls=%async_computation.3 | async-start | bytes 18874368 | tf_op jit(solution)/shard_map/all_to_all | solution.py:111
  469.7 0.8 reduce.9
  470.7 5.2 copy.77
  475.9 14.0 %scatter_fusion = f32[1024,400]{1,0:T(8,128)S(1)} fusion(f32[1024,400]{1,0:T(8,128)S(1)} %slice-done, s32[2048]{0:T(1024)S(1)} %copy-done.13, f32[2048,400]{1,0:T(8,128)} %copy.77), kind=kCustom, calls=%fused_computation.6 | custom fusion | flops 819200 | bytes 9838592 | tf_op jit(solution)/shard_map/scatter-add | solution.py:95
  489.9 14.3 %scatter_fusion.1 = f32[1024,400]{1,0:T(8,128)S(1)} fusion(f32[1024,400]{1,0:T(8,128)S(1)} %scatter_fusion, s32[2048]{0:T(1024)S(1)} %bitcast.53, f32[2048,400]{1,0:T(8,128)} %bitcast.11), kind=kCustom, calls=%fused_computation.7 | custom fusion | flops 819200 | bytes 9838592 | tf_op jit(solution)/shard_map/scatter-add | solution.py:98
  504.2 102.3 %all-to-all-done.3 = f32[64,66,400]{2,1,0:T(8,128)} async-done(((f32[64,66,400]{2,1,0:T(8,128)}), f32[64,66,400]{2,1,0:T(8,128)}, u32[]{:S(2)}, u32[]{:S(2)}) %all-to-all-start.3) | async-done | bytes 6758432 | tf_op jit(solution)/shard_map/all_to_all | solution.py:111
  606.5 4.6 reduce_sum.37
  611.3 3.8 scatter_custom_fusion.3
  616.3 1.8 multiply_reduce_fusion.1
  618.7 1.8 divide_subtract_fusion
  620.5 2.7 copy.83
  (76 shorter events, 8.1 us)
Async XLA Ops:
  7.2 3.7 copy-start.11
  7.2 4.5 copy-start.14
  7.2 130.2 %all-gather.4.cloned.1.call-start = ((), (), s32[]{:S(2)}) async-start(), calls=%async_computation.4 | async-start | bytes 19021824 | tf_op jit(solution)/shard_map/all_gather | solution.py:80
  7.9 0.5 copy-start.20
  10.3 90.6 %copy-start = (f32[1024,400]{1,0:T(8,128)}, f32[1024,400]{1,0:T(8,128)S(1)}, u32[]{:S(2)}) copy-start(f32[1024,400]{1,0:T(8,128)S(1)} %copy.82) | copy-start | bytes 4915204
  28.3 0.6 copy-start.9
  37.9 8.8 %copy-start.15 = (s32[2048]{0:T(1024)S(1)}, s32[2048]{0:T(1024)}, u32[]{:S(2)}) copy-start(s32[2048]{0:T(1024)} %param.15) | copy-start | bytes 24580
  37.9 63.0 %all-to-all-start.1 = ((f32[128,16,400]{2,1,0:T(8,128)}), f32[128,16,400]{2,1,0:T(8,128)}, u32[]{:S(2)}, u32[]{:S(2)}) async-start(f32[128,16,400]{2,1,0:T(8,128)} %bitcast.41), calls=%async_computation.1 | async-start | bytes 8388608 | tf_op jit(solution)/shard_map/all_to_all | solution.py:86
  61.3 5.6 copy-start.16
  61.3 5.7 copy-start.19
  61.3 5.8 copy-start.21
  61.3 5.9 copy-start.17
  200.0 3.9 copy-start.4
  286.0 14.3 %copy-start.5 = (f32[2048,200]{0,1:T(8,128)S(1)}, f32[2048,200]{0,1:T(8,128)}, u32[]{:S(2)}) copy-start(f32[2048,200]{0,1:T(8,128)} %copy.85) | copy-start | bytes 4915204
  286.0 14.3 %copy-start.6 = (f32[2048,200]{0,1:T(8,128)S(1)}, f32[2048,200]{0,1:T(8,128)}, u32[]{:S(2)}) copy-start(f32[2048,200]{0,1:T(8,128)} %copy.87) | copy-start | bytes 4915204
  286.0 14.3 %copy-start.7 = (f32[2048,200]{0,1:T(8,128)S(1)}, f32[2048,200]{0,1:T(8,128)}, u32[]{:S(2)}) copy-start(f32[2048,200]{0,1:T(8,128)} %copy.88) | copy-start | bytes 4915204
  286.0 14.3 %copy-start.8 = (f32[2048,200]{0,1:T(8,128)S(1)}, f32[2048,200]{0,1:T(8,128)}, u32[]{:S(2)}) copy-start(f32[2048,200]{0,1:T(8,128)} %copy.86) | copy-start | bytes 4915204
  373.4 36.8 %collective-permute-start = (f32[64,66,400]{2,0,1:T(8,128)}, f32[64,66,400]{2,0,1:T(8,128)}, u32[]{:S(2)}, u32[]{:S(2)}) collective-permute-start(f32[64,66,400]{2,0,1:T(8,128)} %dynamic-slice_bitcast_fusion), channel_id=1, source_target_pairs={{0,1},{1,0},{2,3},{3,2},{4,5},{5,4},{6,7},{7,6},{8,9},{9,8},{10,11... | collective-permute-start | bytes 20275208 | tf_op jit(solution)/shard_map/ppermute | solution.py:107
  401.6 57.9 %all-to-all-start.2 = ((f32[128,16,400]{2,1,0:T(8,128)}), f32[128,16,400]{2,1,0:T(8,128)}, u32[]{:S(2)}, u32[]{:S(2)}) async-start(f32[128,16,400]{2,1,0:T(8,128)} %bitcast.42), calls=%async_computation.2 | async-start | bytes 8388608 | tf_op jit(solution)/shard_map/all_to_all | solution.py:97
  434.7 35.1 %copy-start.10 = (s32[128,1,16]{2,1,0:T(1,128)S(1)}, s32[128,1,16]{2,1,0:T(1,128)}, u32[]{:S(2)}) copy-start(s32[128,1,16]{2,1,0:T(1,128)} %copy-done.9) | copy-start | bytes 24580
  459.5 147.0 %all-to-all-start.3 = ((f32[64,66,400]{2,1,0:T(8,128)}), f32[64,66,400]{2,1,0:T(8,128)}, u32[]{:S(2)}, u32[]{:S(2)}) async-start(f32[64,66,400]{2,1,0:T(8,128)} %copy.81), calls=%async_computation.3 | async-start | bytes 18874368 | tf_op jit(solution)/shard_map/all_to_all | solution.py:111
  470.7 5.2 slice-start
  470.7 5.2 copy-start.13
  504.1 102.4 %copy-start.2 = (f32[1024,400]{1,0:T(8,128)}, f32[1024,400]{1,0:T(8,128)S(1)}, u32[]{:S(2)}) copy-start(f32[1024,400]{1,0:T(8,128)S(1)} %scatter_fusion.1) | copy-start | bytes 4915204
  504.1 110.9 %copy-start.22 = (f32[58]{0:T(128)S(1)}, f32[58]{0:T(128)}, u32[]{:S(2)}) copy-start(f32[58]{0:T(128)} %param.14) | copy-start | bytes 700
  504.1 111.4 %copy-start.12 = (f32[58,400]{1,0:T(8,128)S(1)}, f32[58,400]{1,0:T(8,128)}, u32[]{:S(2)}) copy-start(f32[58,400]{1,0:T(8,128)} %param.13) | copy-start | bytes 278404
  611.1 7.0 %copy-start.18 = (f32[1024]{0:T(1024)S(1)}, f32[1024]{0:T(1024)}, u32[]{:S(2)}) copy-start(f32[1024]{0:T(1024)} %param.12) | copy-start | bytes 12292
  611.1 7.6 %copy-start.1 = (f32[1024,400]{1,0:T(8,128)S(1)}, f32[1024,400]{1,0:T(8,128)}, u32[]{:S(2)}) copy-start(f32[1024,400]{1,0:T(8,128)} %copy-done) | copy-start | bytes 4915204
  615.0 3.7 copy-start.3
Sparse Core Ops, SparseCore 0:
  11.8 125.5 all-gather.3

commit v2 on v1

v2 whole, which is shorter than its diff:
```python
import jax
import jax.numpy as jnp
from jax import lax
from jax.experimental import pallas as pl
from jax.experimental.pallas import tpu as pltpu
from jax.sharding import Mesh, PartitionSpec as P

rate = 0.1
AXES = ("x", "z", "y", "c")
WIDTH = 400
HALF = 200
LANES = 128
CHUNKS = 4
SPANS = ((0, 128), (128, 72), (200, 128), (328, 72))
ENT_DEV = 1024
REL_DEV = 58
NEG_DEV = 8
E_DEV = 2048
N_DEV = 128
CAP = 16
NEG = N_DEV * NEG_DEV
SLOTS = N_DEV * CAP
CHIPS = N_DEV // 2
PER = CHUNKS * (REL_DEV + NEG_DEV)
REL4 = CHUNKS * REL_DEV
TILE = 256
UNROLL = 8

f32 = jnp.float32
bf16 = jnp.bfloat16
VMEM = pl.BlockSpec(memory_space=pltpu.VMEM)
SMEM = pl.BlockSpec(memory_space=pltpu.SMEM)
ANY = pl.BlockSpec(memory_space=pl.ANY)


def params(mib):
    return pltpu.CompilerParams(vmem_limit_bytes=mib * 1024 * 1024)


def cost(flops, moved):
    return pl.CostEstimate(flops=flops, bytes_accessed=moved, transcendentals=0)


def chunk_of(ref, c, n):
    return ref[pl.ds(c, n, stride=CHUNKS), :]


def row(i):
    return pl.ds(pl.multiple_of(i * CHUNKS, CHUNKS), CHUNKS)


def split(x):
    hi = x.astype(bf16)
    return hi, (x - hi.astype(f32)).astype(bf16)


def dot3(a, b, dims):
    (ah, al), (bh, bl) = a, b

    def one(p, q):
        return lax.dot_general(p, q, (dims, ((), ())), preferred_element_type=f32)

    return one(ah, bh) + (one(ah, bl) + one(al, bh))


def rows_loop(n, body):
    def step(s, carry):
        for u in range(UNROLL):
            body(s * UNROLL + u)
        return carry

    lax.fori_loop(0, n // UNROLL, step, 0)


def to_chunks(src, dst, n):
    for c, (start, size) in enumerate(SPANS):
        piece = src[start : start + size, :]
        if size < LANES:
            piece = jnp.concatenate([piece, jnp.zeros((LANES - size, n), f32)], axis=0)
        dst[pl.ds(c, n, stride=CHUNKS), :] = piece.T


def prep_kernel(negatives, table_t, rel_t, tab4, ag4, rel4):
    to_chunks(table_t, tab4, ENT_DEV)
    to_chunks(rel_t, rel4, LANES)
    ag4[0:REL4, :] = rel4[0:REL4, :]
    for i in range(NEG_DEV):
        ag4[REL4 + CHUNKS * i : REL4 + CHUNKS * (i + 1), :] = tab4[row(negatives[i]), :]


def prep(negatives, table_t, rel_t):
    return pl.pallas_call(
        prep_kernel,
        out_shape=(
            jax.ShapeDtypeStruct((ENT_DEV * CHUNKS, LANES), f32),
            jax.ShapeDtypeStruct((PER, LANES), f32),
        ),
        in_specs=[SMEM, VMEM, VMEM],
        out_specs=(VMEM, VMEM),
        scratch_shapes=[pltpu.VMEM((LANES * CHUNKS, LANES), f32)],
        compiler_params=params(24),
        cost_estimate=cost(0, 8 << 20),
        name="prep",
    )(negatives, table_t, rel_t)


def pull_kernel(asked, tab4, out):
    def body(i):
        out[row(i), :] = tab4[row(asked[i]), :]

    rows_loop(SLOTS, body)


def pull_rows(asked, tab4):
    return pl.pallas_call(
        pull_kernel,
        out_shape=jax.ShapeDtypeStruct((SLOTS * CHUNKS, LANES), f32),
        in_specs=[SMEM, VMEM],
        out_specs=VMEM,
        compiler_params=params(24),
        cost_estimate=cost(0, 8 << 20),
        name="pull_rows",
    )(asked, tab4)


def query_kernel(
    heads, rel_at, tails, tab4, fetched, shared,
    q_out, h_out, r_out, p_out, ext_grad_out,
    ext, rel, ext_grad, hb, rb, tb, sems,
):
    step = pl.program_id(0)
    local = ENT_DEV * CHUNKS

    @pl.when(step == 0)
    def _():
        loads = (
            pltpu.make_async_copy(tab4, ext.at[pl.ds(0, local)], sems.at[0]),
            pltpu.make_async_copy(fetched, ext.at[pl.ds(local, SLOTS * CHUNKS)], sems.at[1]),
            pltpu.make_async_copy(shared, rel, sems.at[2]),
        )
        for load in loads:
            load.start()
        ext_grad[...] = jnp.zeros_like(ext_grad)
        for load in loads:
            load.wait()

    base = step * TILE

    def gather(i):
        hb[row(i), :] = ext[row(heads[base + i]), :]
        rb[row(i), :] = rel[row(rel_at[base + i]), :]
        tb[row(i), :] = ext[row(tails[base + i]), :]

    rows_loop(TILE, gather)
    h = [chunk_of(hb, c, TILE) for c in range(CHUNKS)]
    r = [chunk_of(rb, c, TILE) for c in range(CHUNKS)]
    t = [chunk_of(tb, c, TILE) for c in range(CHUNKS)]
    q = [h[0] * r[0] - h[2] * r[2], h[1] * r[1] - h[3] * r[3], h[0] * r[2] + h[2] * r[0], h[1] * r[3] + h[3] * r[1]]
    score = (q[0] * t[0] + q[1] * t[1]) + (q[2] * t[2] + q[3] * t[3])
    pos_grad = jax.nn.sigmoid(jnp.sum(score, axis=1, keepdims=True)) - 1.0
    for c in range(CHUNKS):
        q_out[c] = q[c]
        h_out[c] = h[c]
        r_out[c] = r[c]
        p_out[c] = pos_grad * t[c]
        hb[pl.ds(c, TILE, stride=CHUNKS), :] = pos_grad * q[c]

    def scatter(i):
        at = row(tails[base + i])
        ext_grad[at, :] = ext_grad[at, :] + hb[row(i), :]

    rows_loop(TILE, scatter)

    @pl.when(step == E_DEV // TILE - 1)
    def _():
        store = pltpu.make_async_copy(ext_grad, ext_grad_out, sems.at[0])
        store.start()
        store.wait()


def queries(heads, rel_at, tails, tab4, fetched, shared):
    plane = jax.ShapeDtypeStruct((CHUNKS, E_DEV, LANES), f32)
    block = pl.BlockSpec((CHUNKS, TILE, LANES), lambda i: (0, i, 0))
    ext_rows = (ENT_DEV + SLOTS) * CHUNKS
    return pl.pallas_call(
        query_kernel,
        grid=(E_DEV // TILE,),
        out_shape=(plane, plane, plane, plane, jax.ShapeDtypeStruct((ext_rows, LANES), f32)),
        in_specs=[SMEM, SMEM, SMEM, ANY, ANY, ANY],
        out_specs=(block, block, block, block, ANY),
        scratch_shapes=[
            pltpu.VMEM((ext_rows, LANES), f32),
            pltpu.VMEM((N_DEV * PER, LANES), f32),
            pltpu.VMEM((ext_rows, LANES), f32),
            pltpu.VMEM((TILE * CHUNKS, LANES), f32),
            pltpu.VMEM((TILE * CHUNKS, LANES), f32),
            pltpu.VMEM((TILE * CHUNKS, LANES), f32),
            pltpu.SemaphoreType.DMA((3,)),
        ],
        compiler_params=params(44),
        cost_estimate=cost(0, 60 << 20),
        name="queries",
    )(heads, rel_at, tails, tab4, fetched, shared)


def grads_kernel(
    heads, grad_at, core, shared, local_grad, q_in, h_in, r_in, p_in,
    mine, other, head_grad,
    negs, n_hi, n_lo, t_hi, t_lo, neg_acc, rel_grad, hb, rb, sems,
):
    step = pl.program_id(0)

    @pl.when(step == 0)
    def _():
        load = pltpu.make_async_copy(shared.at[:, pl.ds(REL4, PER - REL4), :], negs, sems.at[0])
        load.start()
        start = pltpu.make_async_copy(local_grad.at[pl.ds(0, ENT_DEV * CHUNKS)], head_grad, sems.at[1])
        start.start()
        rel_grad[...] = jnp.zeros_like(rel_grad)
        neg_acc[...] = jnp.zeros_like(neg_acc)
        load.wait()
        flat = negs.reshape(NEG * CHUNKS, LANES)
        for c in range(CHUNKS):
            lanes = slice(c * LANES, (c + 1) * LANES)
            piece = chunk_of(flat, c, NEG)
            n_hi[:, lanes], n_lo[:, lanes] = split(piece)
            t_hi[lanes, :], t_lo[lanes, :] = split(piece.T)
        start.wait()

    base = step * TILE
    q = split(jnp.concatenate([q_in[c] for c in range(CHUNKS)], axis=1))
    negative = dot3(q, (t_hi[...], t_lo[...]), ((1,), (0,)))
    neg_grad = split(jax.nn.sigmoid(negative) * (1.0 / NEG))
    neg_acc[...] += dot3(neg_grad, q, ((0,), (0,)))
    back = dot3(neg_grad, (n_hi[...], n_lo[...]), ((1,), (0,)))
    g = [p_in[c] + back[:, c * LANES : (c + 1) * LANES] for c in range(CHUNKS)]
    for k in range(2):
        for buf, src in ((hb, r_in), (rb, h_in)):
            buf[pl.ds(k, TILE, stride=CHUNKS), :] = g[k] * src[k] + g[k + 2] * src[k + 2]
            buf[pl.ds(k + 2, TILE, stride=CHUNKS), :] = g[k + 2] * src[k] - g[k] * src[k + 2]

    def scatter(i):
        at = row(heads[base + i])
        rel = row(grad_at[base + i])
        head_grad[at, :] = head_grad[at, :] + hb[row(i), :]
        rel_grad[rel, :] = rel_grad[rel, :] + rb[row(i), :]

    rows_loop(TILE, scatter)

    @pl.when(step == E_DEV // TILE - 1)
    def _():
        def place(d, carry):
            spot = ((d % 2) * CHIPS + d // 2) * PER + REL4
            rows = pl.ds(pl.multiple_of(d * NEG_DEV, NEG_DEV), NEG_DEV)
            for c in range(CHUNKS):
                rel_grad[pl.ds(spot + c, NEG_DEV, stride=CHUNKS), :] = neg_acc[rows, c * LANES : (c + 1) * LANES]
            return carry

        lax.fori_loop(0, N_DEV, place, 0)
        side = core[0]
        half = CHIPS * PER
        stores = (
            pltpu.make_async_copy(rel_grad.at[pl.ds(pl.multiple_of((1 - side) * half, 8), half)], other, sems.at[0]),
            pltpu.make_async_copy(rel_grad.at[pl.ds(pl.multiple_of(side * half, 8), half)], mine, sems.at[1]),
        )
        for store in stores:
            store.start()
        for store in stores:
            store.wait()


def gradients(heads, grad_at, core, shared, ext_grad, q, h, r, p):
    block = pl.BlockSpec((CHUNKS, TILE, LANES), lambda i: (0, i, 0))
    half = jax.ShapeDtypeStruct((CHIPS * PER, LANES), f32)
    whole = pl.BlockSpec((ENT_DEV * CHUNKS, LANES), lambda i: (0, 0))
    return pl.pallas_call(
        grads_kernel,
        grid=(E_DEV // TILE,),
        out_shape=(half, half, jax.ShapeDtypeStruct((ENT_DEV * CHUNKS, LANES), f32)),
        in_specs=[SMEM, SMEM, SMEM, ANY, ANY, block, block, block, block],
        out_specs=(ANY, ANY, whole),
        scratch_shapes=[
            pltpu.VMEM((N_DEV, PER - REL4, LANES), f32),
            pltpu.VMEM((NEG, CHUNKS * LANES), bf16),
            pltpu.VMEM((NEG, CHUNKS * LANES), bf16),
            pltpu.VMEM((CHUNKS * LANES, NEG), bf16),
            pltpu.VMEM((CHUNKS * LANES, NEG), bf16),
            pltpu.VMEM((NEG, CHUNKS * LANES), f32),
            pltpu.VMEM((N_DEV * PER, LANES), f32),
            pltpu.VMEM((TILE * CHUNKS, LANES), f32),
            pltpu.VMEM((TILE * CHUNKS, LANES), f32),
            pltpu.SemaphoreType.DMA((2,)),
        ],
        compiler_params=params(52),
        cost_estimate=cost(36_000_000_000, 60 << 20),
        name="gradients",
    )(heads, grad_at, core, shared, ext_grad, q, h, r, p)


def returned_kernel(asked, returned, head_grad, out):
    out[...] = head_grad[...]

    def body(i):
        at = row(asked[i])
        out[at, :] = out[at, :] + returned[row(i), :]

    rows_loop(SLOTS, body)


def add_returned(asked, returned, head_grad):
    return pl.pallas_call(
        returned_kernel,
        out_shape=jax.ShapeDtypeStruct((ENT_DEV * CHUNKS, LANES), f32),
        in_specs=[SMEM, VMEM, VMEM],
        out_specs=VMEM,
        compiler_params=params(24),
        cost_estimate=cost(0, 10 << 20),
        name="add_returned",
    )(asked, returned, head_grad)


def adagrad(grad, n, table_t, state, new_table_t, new_state):
    g = [chunk_of(grad, c, n).T for c in range(CHUNKS)]
    squares = (g[0] * g[0] + g[1] * g[1]) + (g[2] * g[2] + g[3] * g[3])
    state_now = state[...] + jnp.sum(squares, axis=0, keepdims=True) * (1.0 / WIDTH)
    new_state[...] = state_now
    below = jnp.sqrt(state_now) + 1e-10
    for c, (start, size) in enumerate(SPANS):
        spot = slice(start, start + size)
        new_table_t[spot, :] = table_t[spot, :] - rate * g[c][:size] / below


def step_kernel(
    negatives, local_grad, parts, table_t, state, rel_t, rel_state,
    new_table_t, new_state, new_rel_t, new_rel_state,
    grad, share,
):
    grad[...] = local_grad[...]
    share[...] = jnp.zeros_like(share)
    share[0:PER, :] = jnp.sum(parts[...], axis=0)
    for i in range(NEG_DEV):
        at = row(negatives[i])
        grad[at, :] = grad[at, :] + share[REL4 + CHUNKS * i : REL4 + CHUNKS * (i + 1), :]
    adagrad(grad, ENT_DEV, table_t, state, new_table_t, new_state)
    adagrad(share, LANES, rel_t, rel_state, new_rel_t, new_rel_state)


def adagrad_step(negatives, local_grad, parts, table_t, state, rel_t, rel_state):
    def like(*shape):
        return jax.ShapeDtypeStruct(shape, f32)

    return pl.pallas_call(
        step_kernel,
        out_shape=(like(WIDTH, ENT_DEV), like(1, ENT_DEV), like(WIDTH, LANES), like(1, LANES)),
        in_specs=[SMEM] + [VMEM] * 6,
        out_specs=(VMEM,) * 4,
        scratch_shapes=[
            pltpu.VMEM((ENT_DEV * CHUNKS, LANES), f32),
            pltpu.VMEM((CHUNKS * LANES, LANES), f32),
        ],
        compiler_params=params(40),
        cost_estimate=cost(0, 16 << 20),
        name="adagrad_step",
    )(negatives, local_grad, parts, table_t, state, rel_t, rel_state)


def local(
    entity_table,
    entity_state,
    relation_table,
    relation_state,
    heads,
    relations,
    tails,
    pull_lists,
    negatives,
):
    table_t = entity_table.T
    rel_t = jnp.pad(relation_table, ((0, LANES - REL_DEV), (0, 0))).T
    owner, place = relations // REL_DEV, relations % REL_DEV
    rel_at = owner * (REL_DEV + NEG_DEV) + place
    grad_at = ((owner % 2) * CHIPS + owner // 2) * (REL_DEV + NEG_DEV) + place
    core = lax.axis_index("c")

    tab4, ag4 = prep(negatives, table_t, rel_t)
    shared = lax.all_gather(ag4, AXES, axis=0, tiled=True)
    asked = lax.all_to_all(pull_lists, AXES, split_axis=0, concat_axis=0, tiled=True).reshape(SLOTS)
    rows_out = pull_rows(asked, tab4)

    def exchange(rows):
        rows = rows.reshape(N_DEV, CAP * CHUNKS, LANES)
        return lax.all_to_all(rows, AXES, split_axis=0, concat_axis=0, tiled=True).reshape(SLOTS * CHUNKS, LANES)

    fetched = exchange(rows_out)
    q, h, r, p, ext_grad = queries(heads, rel_at, tails, tab4, fetched, shared)
    returned = exchange(ext_grad[ENT_DEV * CHUNKS :])
    mine, other, head_grad = gradients(
        heads, grad_at, core.reshape(1), shared.reshape(N_DEV, PER, LANES), ext_grad, q, h, r, p
    )
    paired = mine + lax.ppermute(other, "c", [(0, 1), (1, 0)])
    parts = lax.all_to_all(
        paired.reshape(CHIPS, PER, LANES), AXES[:3], split_axis=0, concat_axis=0, tiled=True
    )
    local_grad = add_returned(asked, returned, head_grad)
    new_table_t, new_state, new_rel_t, new_rel_state = adagrad_step(
        negatives,
        local_grad,
        parts,
        table_t,
        entity_state.reshape(1, ENT_DEV),
        rel_t,
        jnp.pad(relation_state, (0, LANES - REL_DEV)).reshape(1, LANES),
    )
    return (
        new_table_t.T,
        new_state.reshape(ENT_DEV),
        new_rel_t.T[:REL_DEV],
        new_rel_state.reshape(LANES)[:REL_DEV],
    )


def solution(mesh):
    grid = Mesh(mesh.devices.reshape(4, 4, 4, 2), AXES)
    rows, flat = P(AXES, None), P(AXES)
    in_specs = (rows, flat, rows, flat, flat, flat, flat, rows, flat)
    out_specs = (rows, flat, rows, flat)
    return jax.shard_map(local, mesh=grid, in_specs=in_specs, out_specs=out_specs, check_vma=False)
```

time: 641 us -> 422 us (0.66)
  the two profiles are of different devices: /device:TPU:22 before, /device:TPU:102 now
where the time goes in v2:
time: 422 us; the launch traced here: 421 us
  waiting for transfers between devices  241 us (57%)
  Pallas kernels  96.6 us (23%)
  starting transfers between devices  27.9 us (7%)
  blocking collectives  15.3 us (4%)
  local copies, waits for them, and re-layouts  15 us (4%)
  between operations  14.2 us (3%)
  other arithmetic  10.9 us (3%)
    all_to_all x1, waiting for transfers between devices, local(): lax.all_to_all(paired.reshape(CHIPS, PER, LANES), AXES[:3], split_axis=0,...  113 us
    all_to_all x2, waiting for transfers between devices, exchange(): lax.all_to_all(rows, AXES, split_axis=0, concat_axis=0, tiled=True)  92.5 us
    pallas_call x1, Pallas kernels, gradients(): pl.pallas_call(grads_kernel, grid=(E_DEV // TILE,), out_shape=(half, half...  45.8 us
    all_gather x1, waiting for transfers between devices, local(): shared = lax.all_gather(ag4, AXES, axis=0, tiled=True)  33.8 us
    pallas_call x1, Pallas kernels, queries(): pl.pallas_call(query_kernel, grid=(E_DEV // TILE,), out_shape=(plane, pla...  29.4 us
    all_to_all x2, starting transfers between devices, exchange(): lax.all_to_all(rows, AXES, split_axis=0, concat_axis=0, tiled=True)  18.7 us
    all_to_all x1, blocking collectives, local(): lax.all_to_all(pull_lists, AXES, split_axis=0, concat_axis=0, tiled=True)  15.3 us
    unnamed x29, local copies, waits for them, and re-layouts  11.7 us
  transfers between devices with their start and end apart: 5, of which 5 were waited for; matrix products, arithmetic and copies ran while one was open for 3% of the time, Pallas kernels for 3%

profile of v2, /device:TPU:102, one launch (start us, length us, event | category | flops | bytes accessed | tf_op | source)
XLA Modules:
  0.0 421.3 jit_solution(16525746407741261383)
XLA Ops:
  7.2 0.0 all-gather.2.cloned.1.call-start
  7.2 1.0 copy.19
  8.3 0.0 copy-start.1
  8.3 1.4 copy-done.1
  9.7 0.0 copy-start.7
  9.7 0.7 copy-done.7
  10.4 1.9 prep.1
  12.2 0.0 all-gather.2.cloned.1.call-update
  12.3 0.8 copy.18
  13.1 15.3 %all_to_all.24 = s32[128,1,16]{2,1,0:T(1,128)S(1)} all-to-all(s32[128,1,16]{2,1,0:T(1,128)S(1)} %bitcast.28), channel_id=1, replica_groups=mesh['x'=4,'z'=4,'y'=4,'c'=2] {'x','z','y','c'}, dimensions={0} | all-to-all | bytes 16384 | tf_op jit(solution)/shard_map/all_to_all | solution.py:387
  28.4 0.5 broadcast.24
  28.9 0.8 reduce.3
  29.7 0.1 reshape.46.asked
  29.8 4.2 pull_rows.1
  34.0 0.0 copy-start
  34.0 2.0 copy-done
  36.0 0.0 copy-start.11
  36.0 0.0 copy-start.4
  36.0 9.5 %all-to-all-start.1 = ((f32[128,64,128]{2,1,0:T(8,128)}), f32[128,64,128]{2,1,0:T(8,128)}, u32[]{:S(2)}, u32[]{:S(2)}) async-start(f32[128,64,128]{2,1,0:T(8,128)} %bitcast.20), calls=%async_computation.1 | async-start | bytes 8388608 | tf_op jit(solution)/shard_map/all_to_all | solution.py:392
  45.5 0.0 copy-done.11
  45.5 54.6 %all-to-all-done.1 = f32[128,64,128]{2,1,0:T(8,128)} async-done(((f32[128,64,128]{2,1,0:T(8,128)}), f32[128,64,128]{2,1,0:T(8,128)}, u32[]{:S(2)}, u32[]{:S(2)}) %all-to-all-start.1) | async-done | bytes 4194336 | tf_op jit(solution)/shard_map/all_to_all | solution.py:392
  100.1 33.8 %all-gather.2.cloned.1.call-done.shared = f32[33792,128]{1,0:T(8,128)} async-done(((f32[264,128]{1,0:T(8,128)}), f32[33792,128]{1,0:T(8,128)}) %all-gather.2.cloned.1.call-update) | async-done | bytes 17301520 | tf_op jit(solution)/shard_map/all_gather | solution.py:386
  133.9 0.0 copy-done.4
  133.9 0.0 copy-done.5
  133.9 29.4 %queries.1 = (f32[4,2048,128]{2,1,0:T(8,128)S(1)}, f32[4,2048,128]{2,1,0:T(8,128)}, f32[4,2048,128]{2,1,0:T(8,128)}, f32[4,2048,128]{2,1,0:T(8,128)}, f32[12288,128]{1,0:T(8,128)}) custom-call(s32[2048]{0:T(1024)S(1)} %copy-done.5, s32[2048]{0:T(1024)S(1)} %get-tuple-element.45.rel_at, s32[2048]{0:T(1024)S(1)} %copy-done.4, ...), custom_call_target="tpu_custom_call" | custom-call | bytes 62914560 | tf_op jit(solution)/shard_map/queries/pallas_call | solution.py:185
  163.3 0.0 copy-start.9
  163.3 2.0 copy-done.9
  165.3 0.0 copy-start.10
  165.3 45.8 %gradients.1 = (f32[16896,128]{1,0:T(8,128)}, f32[16896,128]{1,0:T(8,128)}, f32[4096,128]{1,0:T(8,128)}) custom-call(s32[2048]{0:T(1024)S(1)} %copy-done.5, s32[2048]{0:T(1024)S(1)} %get-tuple-element.44.grad_at, s32[1]{0:T(128)} %bitcast.7.core, f32[128,264,128]{2,1,0:T(8,128)} %bitcast.26, f32[12288,128]{1,0:T(8,128)} %get-tuple-element.20.local_grad, ...), custom_call_target="tpu_custom_call" | custom-call | flops 35999997952 | bytes 62914560 | tf_op jit(solution)/shard_map/gradients/pallas_call | solution.py:276
  211.1 0.4 collective-permute-start
  211.4 0.0 copy-done.10
  211.4 2.2 slice.12
  213.7 9.2 %all-to-all-start.2 = ((f32[128,64,128]{2,1,0:T(8,128)}), f32[128,64,128]{2,1,0:T(8,128)}, u32[]{:S(2)}, u32[]{:S(2)}) async-start(f32[128,64,128]{2,1,0:T(8,128)} %bitcast.27), calls=%async_computation.2 | async-start | bytes 8388608 | tf_op jit(solution)/shard_map/all_to_all | solution.py:392
  222.9 2.2 collective-permute-done
  225.0 10.0 %add.33 = f32[16896,128]{1,0:T(8,128)} add(f32[16896,128]{1,0:T(8,128)} %get-tuple-element.26, f32[16896,128]{1,0:T(8,128)} %collective-permute-done) | non-fusion elementwise | flops 2162688 | bytes 25952256 | tf_op jit(solution)/shard_map/add | solution.py:400
  235.1 37.9 %all-to-all-done.2 = f32[128,64,128]{2,1,0:T(8,128)} async-done(((f32[128,64,128]{2,1,0:T(8,128)}), f32[128,64,128]{2,1,0:T(8,128)}, u32[]{:S(2)}, u32[]{:S(2)}) %all-to-all-start.2) | async-done | bytes 4194336 | tf_op jit(solution)/shard_map/all_to_all | solution.py:392
  273.0 8.8 %all-to-all-start.3 = ((f32[64,264,128]{2,1,0:T(8,128)}), f32[64,264,128]{2,1,0:T(8,128)}, u32[]{:S(2)}, u32[]{:S(2)}) async-start(f32[64,264,128]{2,1,0:T(8,128)} %bitcast.25), calls=%async_computation.3 | async-start | bytes 17301504 | tf_op jit(solution)/shard_map/all_to_all | solution.py:401
  281.9 0.0 copy-done.12
  281.9 0.0 copy-start.3
  281.9 1.6 copy-done.3
  283.5 9.2 %add_returned.1.local_grad = f32[4096,128]{1,0:T(8,128)S(1)} custom-call(s32[2048]{0:T(1024)S(1)} %reshape.46.asked, f32[8192,128]{1,0:T(8,128)} %bitcast.6.returned, f32[4096,128]{1,0:T(8,128)S(1)} %copy-done.3), custom_call_target="tpu_custom_call" | custom-call | bytes 10485760 | tf_op jit(solution)/shard_map/add_returned/pallas_call | solution.py:311
  292.7 112.9 %all-to-all-done.3.parts = f32[64,264,128]{2,1,0:T(8,128)} async-done(((f32[64,264,128]{2,1,0:T(8,128)}), f32[64,264,128]{2,1,0:T(8,128)}, u32[]{:S(2)}, u32[]{:S(2)}) %all-to-all-start.3) | async-done | bytes 8650784 | tf_op jit(solution)/shard_map/all_to_all | solution.py:401
  405.6 0.0 copy-done.6
  405.6 0.0 copy-done.8
  405.6 1.4 copy-done.2
  407.0 6.1 %adagrad_step.1 = (f32[400,1024]{1,0:T(8,128)}, f32[1,1024]{1,0:T(1,128)}, f32[400,128]{1,0:T(8,128)S(1)}, f32[1,128]{1,0:T(1,128)S(1)}) custom-call(s32[8]{0:T(128)S(1)} %copy-done.8, f32[4096,128]{1,0:T(8,128)S(1)} %add_returned.1.local_grad, f32[64,264,128]{2,1,0:T(8,128)} %all-to-all-done.3.parts, f32[400,1024]{1,0:T(8,128)S(1)} %bitcast.22, ...), custom_call_target="tpu_custom_call" | custom-call | bytes 16777216 | tf_op jit(solution)/shard_map/adagrad_step/pallas_call | solution.py:352
  413.1 0.8 copy.20
  413.9 0.5 slice_bitcast_fusion
  (8 shorter events, 0.1 us)
Async XLA Ops:
  7.2 126.7 %all-gather.2.cloned.1.call-start = ((), (), s32[]{:S(2)}) async-start(), calls=%async_computation.4 | async-start | bytes 17436672 | tf_op jit(solution)/shard_map/all_gather | solution.py:386
  8.3 1.4 copy-start.1
  9.7 0.7 copy-start.7
  34.0 2.0 copy-start
  36.0 9.5 %copy-start.11 = (s32[2048]{0:T(1024)S(1)}, s32[2048]{0:T(1024)}, u32[]{:S(2)}) copy-start(s32[2048]{0:T(1024)} %param.14) | copy-start | bytes 24580
  36.0 97.9 %copy-start.4 = (s32[2048]{0:T(1024)S(1)}, s32[2048]{0:T(1024)}, u32[]{:S(2)}) copy-start(s32[2048]{0:T(1024)} %tails.1) | copy-start | bytes 24580
  36.0 97.9 %copy-start.5 = (s32[2048]{0:T(1024)S(1)}, s32[2048]{0:T(1024)}, u32[]{:S(2)}) copy-start(s32[2048]{0:T(1024)} %heads.3) | copy-start | bytes 24580
  36.0 64.1 %all-to-all-start.1 = ((f32[128,64,128]{2,1,0:T(8,128)}), f32[128,64,128]{2,1,0:T(8,128)}, u32[]{:S(2)}, u32[]{:S(2)}) async-start(f32[128,64,128]{2,1,0:T(8,128)} %bitcast.20), calls=%async_computation.1 | async-start | bytes 8388608 | tf_op jit(solution)/shard_map/all_to_all | solution.py:392
  163.3 2.0 copy-start.9
  165.3 46.2 %copy-start.10 = (f32[12288,128]{1,0:T(8,128)S(1)}, f32[12288,128]{1,0:T(8,128)}, u32[]{:S(2)}) copy-start(f32[12288,128]{1,0:T(8,128)} %get-tuple-element.20.local_grad) | copy-start | bytes 18874372
  211.1 14.0 %collective-permute-start = (f32[16896,128]{1,0:T(8,128)}, f32[16896,128]{1,0:T(8,128)}, u32[]{:S(2)}, u32[]{:S(2)}) collective-permute-start(f32[16896,128]{1,0:T(8,128)} %get-tuple-element.27), channel_id=1, source_target_pairs={{0,1},{1,0},{2,3},{3,2},{4,5},{5,4},{6,7},{7,6},{8,9},{9,8},{10,11... | collective-permute-start | bytes 25952264 | tf_op jit(solution)/shard_map/ppermute | solution.py:400
  213.7 59.4 %all-to-all-start.2 = ((f32[128,64,128]{2,1,0:T(8,128)}), f32[128,64,128]{2,1,0:T(8,128)}, u32[]{:S(2)}, u32[]{:S(2)}) async-start(f32[128,64,128]{2,1,0:T(8,128)} %bitcast.27), calls=%async_computation.2 | async-start | bytes 8388608 | tf_op jit(solution)/shard_map/all_to_all | solution.py:392
  273.0 8.8 %copy-start.12 = (f32[58]{0:T(128)S(1)}, f32[58]{0:T(128)}, u32[]{:S(2)}) copy-start(f32[58]{0:T(128)} %param.12) | copy-start | bytes 700
  273.0 132.5 %all-to-all-start.3 = ((f32[64,264,128]{2,1,0:T(8,128)}), f32[64,264,128]{2,1,0:T(8,128)}, u32[]{:S(2)}, u32[]{:S(2)}) async-start(f32[64,264,128]{2,1,0:T(8,128)} %bitcast.25), calls=%async_computation.3 | async-start | bytes 17301504 | tf_op jit(solution)/shard_map/all_to_all | solution.py:401
  281.9 1.6 copy-start.3
  283.5 122.1 %copy-start.6 = (f32[1024]{0:T(1024)S(1)}, f32[1024]{0:T(1024)}, u32[]{:S(2)}) copy-start(f32[1024]{0:T(1024)} %param.10) | copy-start | bytes 12292
  283.5 122.1 %copy-start.8 = (s32[8]{0:T(128)S(1)}, s32[8]{0:T(128)}, u32[]{:S(2)}) copy-start(s32[8]{0:T(128)} %negatives.3) | copy-start | bytes 100
  405.6 1.4 copy-start.2
Sparse Core Ops, SparseCore 0:
  12.4 121.4 all-gather.1

commit v3 on v2

--- a/solution.py
+++ b/solution.py
@@ -123,11 +123,7 @@
     )(asked, tab4)
 
 
-def query_kernel(
-    heads, rel_at, tails, tab4, fetched, shared,
-    q_out, h_out, r_out, p_out, ext_grad_out,
-    ext, rel, ext_grad, hb, rb, tb, sems,
-):
+def ends_kernel(heads, tails, tab4, fetched, h_out, t_out, ext, hb, tb, sems):
     step = pl.program_id(0)
     local = ENT_DEV * CHUNKS
 
@@ -136,11 +132,9 @@
         loads = (
             pltpu.make_async_copy(tab4, ext.at[pl.ds(0, local)], sems.at[0]),
             pltpu.make_async_copy(fetched, ext.at[pl.ds(local, SLOTS * CHUNKS)], sems.at[1]),
-            pltpu.make_async_copy(shared, rel, sems.at[2]),
         )
         for load in loads:
             load.start()
-        ext_grad[...] = jnp.zeros_like(ext_grad)
         for load in loads:
             load.wait()
 
@@ -148,19 +142,63 @@
 
     def gather(i):
         hb[row(i), :] = ext[row(heads[base + i]), :]
+        tb[row(i), :] = ext[row(tails[base + i]), :]
+
+    rows_loop(TILE, gather)
+    for c in range(CHUNKS):
+        h_out[c] = chunk_of(hb, c, TILE)
+        t_out[c] = chunk_of(tb, c, TILE)
+
+
+def ends(heads, tails, tab4, fetched):
+    plane = jax.ShapeDtypeStruct((CHUNKS, E_DEV, LANES), f32)
+    block = pl.BlockSpec((CHUNKS, TILE, LANES), lambda i: (0, i, 0))
+    return pl.pallas_call(
+        ends_kernel,
+        grid=(E_DEV // TILE,),
+        out_shape=(plane, plane),
+        in_specs=[SMEM, SMEM, ANY, ANY],
+        out_specs=(block, block),
+        scratch_shapes=[
+            pltpu.VMEM(((ENT_DEV + SLOTS) * CHUNKS, LANES), f32),
+            pltpu.VMEM((TILE * CHUNKS, LANES), f32),
+            pltpu.VMEM((TILE * CHUNKS, LANES), f32),
+            pltpu.SemaphoreType.DMA((2,)),
+        ],
+        compiler_params=params(24),
+        cost_estimate=cost(0, 30 << 20),
+        name="ends",
+    )(heads, tails, tab4, fetched)
+
+
+def query_kernel(
+    rel_at, tails, shared, h_in, t_in,
+    q_out, r_out, p_out, tail_local, outgoing,
+    rel, ext_grad, hb, rb, sems,
+):
+    step = pl.program_id(0)
+
+    @pl.when(step == 0)
+    def _():
+        load = pltpu.make_async_copy(shared, rel, sems.at[0])
+        load.start()
+        ext_grad[...] = jnp.zeros_like(ext_grad)
+        load.wait()
+
+    base = step * TILE
+
+    def gather(i):
         rb[row(i), :] = rel[row(rel_at[base + i]), :]
-        tb[row(i), :] = ext[row(tails[base + i]), :]
 
     rows_loop(TILE, gather)
-    h = [chunk_of(hb, c, TILE) for c in range(CHUNKS)]
+    h = [h_in[c] for c in range(CHUNKS)]
     r = [chunk_of(rb, c, TILE) for c in range(CHUNKS)]
-    t = [chunk_of(tb, c, TILE) for c in range(CHUNKS)]
+    t = [t_in[c] for c in range(CHUNKS)]
     q = [h[0] * r[0] - h[2] * r[2], h[1] * r[1] - h[3] * r[3], h[0] * r[2] + h[2] * r[0], h[1] * r[3] + h[3] * r[1]]
     score = (q[0] * t[0] + q[1] * t[1]) + (q[2] * t[2] + q[3] * t[3])
     pos_grad = jax.nn.sigmoid(jnp.sum(score, axis=1, keepdims=True)) - 1.0
     for c in range(CHUNKS):
         q_out[c] = q[c]
-        h_out[c] = h[c]
         r_out[c] = r[c]
         p_out[c] = pos_grad * t[c]
         hb[pl.ds(c, TILE, stride=CHUNKS), :] = pos_grad * q[c]
@@ -173,34 +211,43 @@
 
     @pl.when(step == E_DEV // TILE - 1)
     def _():
-        store = pltpu.make_async_copy(ext_grad, ext_grad_out, sems.at[0])
-        store.start()
-        store.wait()
-
-
-def queries(heads, rel_at, tails, tab4, fetched, shared):
+        local = ENT_DEV * CHUNKS
+        stores = (
+            pltpu.make_async_copy(ext_grad.at[pl.ds(0, local)], tail_local, sems.at[0]),
+            pltpu.make_async_copy(ext_grad.at[pl.ds(local, SLOTS * CHUNKS)], outgoing, sems.at[1]),
+        )
+        for store in stores:
+            store.start()
+        for store in stores:
+            store.wait()
+
+
+def queries(rel_at, tails, shared, h, t):
     plane = jax.ShapeDtypeStruct((CHUNKS, E_DEV, LANES), f32)
     block = pl.BlockSpec((CHUNKS, TILE, LANES), lambda i: (0, i, 0))
-    ext_rows = (ENT_DEV + SLOTS) * CHUNKS
     return pl.pallas_call(
         query_kernel,
         grid=(E_DEV // TILE,),
-        out_shape=(plane, plane, plane, plane, jax.ShapeDtypeStruct((ext_rows, LANES), f32)),
-        in_specs=[SMEM, SMEM, SMEM, ANY, ANY, ANY],
-        out_specs=(block, block, block, block, ANY),
+        out_shape=(
+            plane,
+            plane,
+            plane,
+            jax.ShapeDtypeStruct((ENT_DEV * CHUNKS, LANES), f32),
+            jax.ShapeDtypeStruct((SLOTS * CHUNKS, LANES), f32),
+        ),
+        in_specs=[SMEM, SMEM, ANY, block, block],
+        out_specs=(block, block, block, ANY, ANY),
         scratch_shapes=[
-            pltpu.VMEM((ext_rows, LANES), f32),
             pltpu.VMEM((N_DEV * PER, LANES), f32),
-            pltpu.VMEM((ext_rows, LANES), f32),
-            pltpu.VMEM((TILE * CHUNKS, LANES), f32),
-            pltpu.VMEM((TILE * CHUNKS, LANES), f32),
-            pltpu.VMEM((TILE * CHUNKS, LANES), f32),
-            pltpu.SemaphoreType.DMA((3,)),
+            pltpu.VMEM(((ENT_DEV + SLOTS) * CHUNKS, LANES), f32),
+            pltpu.VMEM((TILE * CHUNKS, LANES), f32),
+            pltpu.VMEM((TILE * CHUNKS, LANES), f32),
+            pltpu.SemaphoreType.DMA((2,)),
         ],
-        compiler_params=params(44),
+        compiler_params=params(40),
         cost_estimate=cost(0, 60 << 20),
         name="queries",
-    )(heads, rel_at, tails, tab4, fetched, shared)
+    )(rel_at, tails, shared, h, t)
 
 
 def grads_kernel(
@@ -214,7 +261,7 @@
     def _():
         load = pltpu.make_async_copy(shared.at[:, pl.ds(REL4, PER - REL4), :], negs, sems.at[0])
         load.start()
-        start = pltpu.make_async_copy(local_grad.at[pl.ds(0, ENT_DEV * CHUNKS)], head_grad, sems.at[1])
+        start = pltpu.make_async_copy(local_grad, head_grad, sems.at[1])
         start.start()
         rel_grad[...] = jnp.zeros_like(rel_grad)
         neg_acc[...] = jnp.zeros_like(neg_acc)
@@ -269,7 +316,7 @@
             store.wait()
 
 
-def gradients(heads, grad_at, core, shared, ext_grad, q, h, r, p):
+def gradients(heads, grad_at, core, shared, tail_local, q, h, r, p):
     block = pl.BlockSpec((CHUNKS, TILE, LANES), lambda i: (0, i, 0))
     half = jax.ShapeDtypeStruct((CHIPS * PER, LANES), f32)
     whole = pl.BlockSpec((ENT_DEV * CHUNKS, LANES), lambda i: (0, 0))
@@ -294,7 +341,7 @@
         compiler_params=params(52),
         cost_estimate=cost(36_000_000_000, 60 << 20),
         name="gradients",
-    )(heads, grad_at, core, shared, ext_grad, q, h, r, p)
+    )(heads, grad_at, core, shared, tail_local, q, h, r, p)
 
 
 def returned_kernel(asked, returned, head_grad, out):
@@ -392,11 +439,13 @@
         return lax.all_to_all(rows, AXES, split_axis=0, concat_axis=0, tiled=True).reshape(SLOTS * CHUNKS, LANES)
 
     fetched = exchange(rows_out)
-    q, h, r, p, ext_grad = queries(heads, rel_at, tails, tab4, fetched, shared)
-    returned = exchange(ext_grad[ENT_DEV * CHUNKS :])
+    h, t = ends(heads, tails, tab4, fetched)
+    q, r, p, tail_local, outgoing = queries(rel_at, tails, shared, h, t)
+    returned = exchange(outgoing)
     mine, other, head_grad = gradients(
-        heads, grad_at, core.reshape(1), shared.reshape(N_DEV, PER, LANES), ext_grad, q, h, r, p
+        heads, grad_at, core.reshape(1), shared.reshape(N_DEV, PER, LANES), tail_local, q, h, r, p
     )
+    other, returned = lax.optimization_barrier((other, returned))
     paired = mine + lax.ppermute(other, "c", [(0, 1), (1, 0)])
     parts = lax.all_to_all(
         paired.reshape(CHIPS, PER, LANES), AXES[:3], split_axis=0, concat_axis=0, tiled=True

time: 422 us -> 400 us (0.948); the launches traced: 421 us -> 395 us
  waiting for transfers between devices: 241 us -> 208 us
  local copies, waits for them, and re-layouts: 15 us -> 20.2 us
    all_to_all x2, waiting for transfers between devices: 92.5 us -> 59 us  [exchange(): lax.all_to_all(rows, AXES, split_axis=0, concat_axis=0, tiled=True)]
    all_gather x1, waiting for transfers between devices: 33.8 us -> 20 us  [local(): shared = lax.all_gather(ag4, AXES, axis=0, tiled=True)]
    ppermute x1, waiting for transfers between devices: 2.16 us -> 13.7 us  [local(): paired = mine + lax.ppermute(other, 'c', [(0, 1), (1, 0)])]
    pallas_call x0 -> x1, Pallas kernels: none -> 9.82 us  [ends(): pl.pallas_call(ends_kernel, grid=(E_DEV // TILE,), out_shape=(plane, plan...]
    unnamed x29 -> x35, local copies, waits for them, and re-layouts: 11.7 us -> 19.1 us
    pallas_call x1, Pallas kernels: 29.4 us -> 23 us  [queries(): pl.pallas_call(query_kernel, grid=(E_DEV // TILE,), out_shape=(plane, pla...]
  transfers between devices with their start and end apart: 5 -> 5, of which waited for: 5 -> 5; matrix products, arithmetic and copies ran while one was open for 3% -> 1% of each run, Pallas kernels for 3% -> 17%
where the time goes in v3:
time: 400 us; the launch traced here: 395 us
  waiting for transfers between devices  208 us (52%)
  Pallas kernels  99.9 us (25%)
  starting transfers between devices  27.6 us (7%)
  local copies, waits for them, and re-layouts  20.2 us (5%)
  blocking collectives  15.3 us (4%)
  between operations  14.2 us (4%)
  other arithmetic  9.28 us (2%)
    all_to_all x1, waiting for transfers between devices, local(): lax.all_to_all(paired.reshape(CHIPS, PER, LANES), AXES[:3], split_axis=0,...  115 us
    all_to_all x2, waiting for transfers between devices, exchange(): lax.all_to_all(rows, AXES, split_axis=0, concat_axis=0, tiled=True)  59 us
    pallas_call x1, Pallas kernels, gradients(): pl.pallas_call(grads_kernel, grid=(E_DEV // TILE,), out_shape=(half, half...  45.7 us
    pallas_call x1, Pallas kernels, queries(): pl.pallas_call(query_kernel, grid=(E_DEV // TILE,), out_shape=(plane, pla...  23 us
    all_gather x1, waiting for transfers between devices, local(): shared = lax.all_gather(ag4, AXES, axis=0, tiled=True)  20 us
    unnamed x35, local copies, waits for them, and re-layouts  19.1 us
    all_to_all x2, starting transfers between devices, exchange(): lax.all_to_all(rows, AXES, split_axis=0, concat_axis=0, tiled=True)  18.7 us
    all_to_all x1, blocking collectives, local(): lax.all_to_all(pull_lists, AXES, split_axis=0, concat_axis=0, tiled=True)  15.3 us
  transfers between devices with their start and end apart: 5, of which 5 were waited for; matrix products, arithmetic and copies ran while one was open for 1% of the time, Pallas kernels for 17%

profile of v3, /device:TPU:102, one launch (start us, length us, event | category | flops | bytes accessed | tf_op | source)
XLA Modules:
  0.0 394.6 jit_solution(7072305061293375472)
XLA Ops:
  7.2 0.0 all-gather.2.cloned.1.call-start
  7.2 1.0 copy.19
  8.3 0.0 copy-start.1
  8.3 1.4 copy-done.1
  9.7 0.7 copy-done.9
  10.4 1.9 prep.1
  12.2 0.0 all-gather.2.cloned.1.call-update
  12.3 0.8 copy.18
  13.1 15.3 %all_to_all.24 = s32[128,1,16]{2,1,0:T(1,128)S(1)} all-to-all(s32[128,1,16]{2,1,0:T(1,128)S(1)} %bitcast.28), channel_id=1, replica_groups=mesh['x'=4,'z'=4,'y'=4,'c'=2] {'x','z','y','c'}, dimensions={0} | all-to-all | bytes 16384 | tf_op jit(solution)/shard_map/all_to_all | solution.py:434
  28.4 0.5 broadcast.24
  28.9 0.8 reduce.3
  29.7 0.1 reshape.46.asked
  29.8 4.2 %pull_rows.1 = f32[8192,128]{1,0:T(8,128)S(1)} custom-call(s32[2048]{0:T(1024)S(1)} %reshape.46.asked, f32[4096,128]{1,0:T(8,128)S(1)} %get-tuple-element.23.tab4), custom_call_target="tpu_custom_call" | custom-call | bytes 8388608 | tf_op jit(solution)/shard_map/pull_rows/pallas_call | solution.py:115
  34.0 0.0 copy-start
  34.0 2.0 copy-done
  36.0 9.5 %all-to-all-start.1 = ((f32[128,64,128]{2,1,0:T(8,128)}), f32[128,64,128]{2,1,0:T(8,128)}, u32[]{:S(2)}, u32[]{:S(2)}) async-start(f32[128,64,128]{2,1,0:T(8,128)} %bitcast.20), calls=%async_computation.1 | async-start | bytes 8388608 | tf_op jit(solution)/shard_map/all_to_all | solution.py:439
  45.5 0.0 copy-done.14
  45.5 54.5 %all-to-all-done.1 = f32[128,64,128]{2,1,0:T(8,128)} async-done(((f32[128,64,128]{2,1,0:T(8,128)}), f32[128,64,128]{2,1,0:T(8,128)}, u32[]{:S(2)}, u32[]{:S(2)}) %all-to-all-start.1) | async-done | bytes 4194336 | tf_op jit(solution)/shard_map/all_to_all | solution.py:439
  100.1 0.0 copy-done.6
  100.1 0.0 copy-done.7
  100.1 9.8 %ends.1 = (f32[4,2048,128]{2,1,0:T(8,128)S(1)}, f32[4,2048,128]{2,1,0:T(8,128)S(1)}) custom-call(s32[2048]{0:T(1024)S(1)} %copy-done.7, s32[2048]{0:T(1024)S(1)} %copy-done.6, f32[4096,128]{1,0:T(8,128)S(1)} %get-tuple-element.23.tab4, f32[8192,128]{1,0:T(8,128)} %bitcast.6.fetched), custom_call_target="tpu_custom_call" | custom-call | bytes 31457280 | tf_op jit(solution)/shard_map/ends/pallas_call | solution.py:156
  109.9 0.0 copy-start.3
  109.9 2.1 copy-done.3
  112.0 2.0 copy-done.4
  114.0 20.0 %all-gather.2.cloned.1.call-done.shared = f32[33792,128]{1,0:T(8,128)} async-done(((f32[264,128]{1,0:T(8,128)}), f32[33792,128]{1,0:T(8,128)}) %all-gather.2.cloned.1.call-update) | async-done | bytes 17301520 | tf_op jit(solution)/shard_map/all_gather | solution.py:433
  134.0 23.0 %queries.1 = (f32[4,2048,128]{2,1,0:T(8,128)S(1)}, f32[4,2048,128]{2,1,0:T(8,128)S(1)}, f32[4,2048,128]{2,1,0:T(8,128)}, f32[4096,128]{1,0:T(8,128)S(1)}, f32[8192,128]{1,0:T(8,128)}) custom-call(s32[2048]{0:T(1024)S(1)} %get-tuple-element.52.rel_at, s32[2048]{0:T(1024)S(1)} %copy-done.6, f32[33792,128]{1,0:T(8,128)} %all-gather.2.cloned.1.call-done.shared, ...), custom_call_target="tpu_custom_call" | custom-call | bytes 62914560 | tf_op jit(solution)/shard_map/queries/pallas_call | solution.py:228
  157.0 0.0 copy-start.11
  157.0 2.0 copy-done.11
  159.0 2.0 copy-done.12
  161.0 1.4 copy-done.13
  162.3 9.2 %all-to-all-start.2 = ((f32[128,64,128]{2,1,0:T(8,128)}), f32[128,64,128]{2,1,0:T(8,128)}, u32[]{:S(2)}, u32[]{:S(2)}) async-start(f32[128,64,128]{2,1,0:T(8,128)} %bitcast.27), calls=%async_computation.2 | async-start | bytes 8388608 | tf_op jit(solution)/shard_map/all_to_all | solution.py:439
  171.5 45.7 %gradients.1 = (f32[16896,128]{1,0:T(8,128)}, f32[16896,128]{1,0:T(8,128)}, f32[4096,128]{1,0:T(8,128)}) custom-call(s32[2048]{0:T(1024)S(1)} %copy-done.7, s32[2048]{0:T(1024)S(1)} %get-tuple-element.53.grad_at, s32[1]{0:T(128)} %bitcast.1.core, f32[128,264,128]{2,1,0:T(8,128)} %bitcast.26, f32[4096,128]{1,0:T(8,128)} %copy-done.13, ...), custom_call_target="tpu_custom_call" | custom-call | flops 35999997952 | bytes 62914560 | tf_op jit(solution)/shard_map/gradients/pallas_call | solution.py:323
  217.2 4.5 %all-to-all-done.2 = f32[128,64,128]{2,1,0:T(8,128)} async-done(((f32[128,64,128]{2,1,0:T(8,128)}), f32[128,64,128]{2,1,0:T(8,128)}, u32[]{:S(2)}, u32[]{:S(2)}) %all-to-all-start.2) | async-done | bytes 4194336 | tf_op jit(solution)/shard_map/all_to_all | solution.py:439
  221.7 0.0 collective-permute-start
  221.7 13.7 %collective-permute-done = f32[16896,128]{1,0:T(8,128)S(1)} collective-permute-done((f32[16896,128]{1,0:T(8,128)}, f32[16896,128]{1,0:T(8,128)S(1)}, u32[]{:S(2)}, u32[]{:S(2)}) %collective-permute-start) | collective-permute-done | bytes 8650784 | tf_op jit(solution)/shard_map/ppermute | solution.py:449
  235.4 8.4 %add.33 = f32[16896,128]{1,0:T(8,128)} add(f32[16896,128]{1,0:T(8,128)} %get-tuple-element.34, f32[16896,128]{1,0:T(8,128)S(1)} %collective-permute-done) | non-fusion elementwise | flops 2162688 | bytes 25952256 | tf_op jit(solution)/shard_map/add | solution.py:449
  243.9 8.8 %all-to-all-start.3 = ((f32[64,264,128]{2,1,0:T(8,128)}), f32[64,264,128]{2,1,0:T(8,128)}, u32[]{:S(2)}, u32[]{:S(2)}) async-start(f32[64,264,128]{2,1,0:T(8,128)} %bitcast.25), calls=%async_computation.3 | async-start | bytes 17301504 | tf_op jit(solution)/shard_map/all_to_all | solution.py:450
  252.7 0.0 copy-done.15
  252.7 0.0 copy-start.5
  252.7 1.6 copy-done.5
  254.3 9.2 %add_returned.1.local_grad = f32[4096,128]{1,0:T(8,128)S(1)} custom-call(s32[2048]{0:T(1024)S(1)} %reshape.46.asked, f32[8192,128]{1,0:T(8,128)} %bitcast.8.returned, f32[4096,128]{1,0:T(8,128)S(1)} %copy-done.5), custom_call_target="tpu_custom_call" | custom-call | bytes 10485760 | tf_op jit(solution)/shard_map/add_returned/pallas_call | solution.py:358
  263.6 115.3 %all-to-all-done.3.parts = f32[64,264,128]{2,1,0:T(8,128)} async-done(((f32[64,264,128]{2,1,0:T(8,128)}), f32[64,264,128]{2,1,0:T(8,128)}, u32[]{:S(2)}, u32[]{:S(2)}) %all-to-all-start.3) | async-done | bytes 8650784 | tf_op jit(solution)/shard_map/all_to_all | solution.py:450
  378.9 0.0 copy-done.8
  378.9 0.0 copy-done.10
  378.9 1.4 copy-done.2
  380.3 6.1 %adagrad_step.1 = (f32[400,1024]{1,0:T(8,128)}, f32[1,1024]{1,0:T(1,128)}, f32[400,128]{1,0:T(8,128)S(1)}, f32[1,128]{1,0:T(1,128)S(1)}) custom-call(s32[8]{0:T(128)S(1)} %copy-done.10, f32[4096,128]{1,0:T(8,128)S(1)} %add_returned.1.local_grad, f32[64,264,128]{2,1,0:T(8,128)} %all-to-all-done.3.parts, f32[400,1024]{1,0:T(8,128)S(1)} %bitcast.22, ...), custom_call_target="tpu_custom_call" | custom-call | bytes 16777216 | tf_op jit(solution)/shard_map/adagrad_step/pallas_call | solution.py:399
  386.5 0.8 copy.20
  387.3 0.5 slice_bitcast_fusion
  (14 shorter events, 0.1 us)
Async XLA Ops:
  7.2 126.8 %all-gather.2.cloned.1.call-start = ((), (), s32[]{:S(2)}) async-start(), calls=%async_computation.4 | async-start | bytes 17436672 | tf_op jit(solution)/shard_map/all_gather | solution.py:433
  8.3 1.4 copy-start.1
  9.7 0.7 copy-start.9
  34.0 2.0 copy-start
  36.0 9.5 %copy-start.14 = (s32[2048]{0:T(1024)S(1)}, s32[2048]{0:T(1024)}, u32[]{:S(2)}) copy-start(s32[2048]{0:T(1024)} %param.14) | copy-start | bytes 24580
  36.0 64.1 %copy-start.6 = (s32[2048]{0:T(1024)S(1)}, s32[2048]{0:T(1024)}, u32[]{:S(2)}) copy-start(s32[2048]{0:T(1024)} %tails.3) | copy-start | bytes 24580
  36.0 64.1 %copy-start.7 = (s32[2048]{0:T(1024)S(1)}, s32[2048]{0:T(1024)}, u32[]{:S(2)}) copy-start(s32[2048]{0:T(1024)} %heads.3) | copy-start | bytes 24580
  36.0 64.1 %all-to-all-start.1 = ((f32[128,64,128]{2,1,0:T(8,128)}), f32[128,64,128]{2,1,0:T(8,128)}, u32[]{:S(2)}, u32[]{:S(2)}) async-start(f32[128,64,128]{2,1,0:T(8,128)} %bitcast.20), calls=%async_computation.1 | async-start | bytes 8388608 | tf_op jit(solution)/shard_map/all_to_all | solution.py:439
  109.9 2.1 copy-start.3
  112.0 2.0 copy-start.4
  157.0 2.0 copy-start.11
  159.0 2.0 copy-start.12
  161.0 1.4 copy-start.13
  162.3 59.3 %all-to-all-start.2 = ((f32[128,64,128]{2,1,0:T(8,128)}), f32[128,64,128]{2,1,0:T(8,128)}, u32[]{:S(2)}, u32[]{:S(2)}) async-start(f32[128,64,128]{2,1,0:T(8,128)} %bitcast.27), calls=%async_computation.2 | async-start | bytes 8388608 | tf_op jit(solution)/shard_map/all_to_all | solution.py:439
  221.7 13.7 %collective-permute-start = (f32[16896,128]{1,0:T(8,128)}, f32[16896,128]{1,0:T(8,128)S(1)}, u32[]{:S(2)}, u32[]{:S(2)}) collective-permute-start(f32[16896,128]{1,0:T(8,128)} %get-tuple-element.35), channel_id=1, source_target_pairs={{0,1},{1,0},{2,3},{3,2},{4,5},{5,4},{6,7},{7,6},{8,9},{9,8},{10,11... | collective-permute-start | bytes 25952264 | tf_op jit(solution)/shard_map/ppermute | solution.py:449
  243.9 8.8 %copy-start.15 = (f32[58]{0:T(128)S(1)}, f32[58]{0:T(128)}, u32[]{:S(2)}) copy-start(f32[58]{0:T(128)} %param.12) | copy-start | bytes 700
  243.9 135.0 %all-to-all-start.3 = ((f32[64,264,128]{2,1,0:T(8,128)}), f32[64,264,128]{2,1,0:T(8,128)}, u32[]{:S(2)}, u32[]{:S(2)}) async-start(f32[64,264,128]{2,1,0:T(8,128)} %bitcast.25), calls=%async_computation.3 | async-start | bytes 17301504 | tf_op jit(solution)/shard_map/all_to_all | solution.py:450
  252.7 1.6 copy-start.5
  254.3 124.6 %copy-start.8 = (f32[1024]{0:T(1024)S(1)}, f32[1024]{0:T(1024)}, u32[]{:S(2)}) copy-start(f32[1024]{0:T(1024)} %param.10) | copy-start | bytes 12292
  254.3 124.6 %copy-start.10 = (s32[8]{0:T(128)S(1)}, s32[8]{0:T(128)}, u32[]{:S(2)}) copy-start(s32[8]{0:T(128)} %negatives.3) | copy-start | bytes 100
  378.9 1.4 copy-start.2
Sparse Core Ops, SparseCore 0:
  12.4 121.5 all-gather.1

commit v4 on v3

--- a/solution.py
+++ b/solution.py
@@ -24,6 +24,8 @@
 PER = CHUNKS * (REL_DEV + NEG_DEV)
 REL4 = CHUNKS * REL_DEV
 TILE = 256
+PACK16 = 56
+PACK66 = 208
 UNROLL = 8
 
 f32 = jnp.float32
@@ -31,6 +33,7 @@
 VMEM = pl.BlockSpec(memory_space=pltpu.VMEM)
 SMEM = pl.BlockSpec(memory_space=pltpu.SMEM)
 ANY = pl.BlockSpec(memory_space=pl.ANY)
+HBM = pl.BlockSpec(memory_space=pltpu.HBM)
 
 
 def params(mib):
@@ -70,6 +73,95 @@
         return carry
 
     lax.fori_loop(0, n // UNROLL, step, 0)
+
+
+def lane(n):
+    return lax.broadcasted_iota(jnp.int32, (n, LANES), 1)
+
+
+def join(c1, c3):
+    return jnp.where(lane(c1.shape[0]) < 72, c1, pltpu.roll(c3, 72, 1))
+
+
+def rest(c3, k):
+    return pltpu.roll(c3, (72 + 16 * k) % LANES, 1)
+
+
+def part(joined, rem, k):
+    at = lane(joined.shape[0])
+    c1 = jnp.where(at < 72, joined, 0.0)
+    tail = jnp.where(at < 72, pltpu.roll(rem, (56 - 16 * k) % LANES, 1), 0.0)
+    return c1, jnp.where(at < 56, pltpu.roll(joined, 56, 1), tail)
+
+
+def four(ref, base, n):
+    return [ref[pl.ds(base + c, n, stride=CHUNKS), :] for c in range(CHUNKS)]
+
+
+def pack16(src, src_base, dst, dst_base):
+    rem = None
+    for k in range(2):
+        c0, c1, c2, c3 = four(src, src_base + 32 * k, 8)
+        dst[pl.ds(dst_base + 8 * k, 8), :] = c0
+        dst[pl.ds(dst_base + 16 + 8 * k, 8), :] = c2
+        dst[pl.ds(dst_base + 32 + 8 * k, 8), :] = join(c1, c3)
+        rem = rest(c3, 0) if k == 0 else jnp.where(lane(8) < 16, rem, rest(c3, 1))
+    dst[pl.ds(dst_base + 48, 8), :] = rem
+
+
+def unpack16(src, src_base, dst, dst_base):
+    rem = src[pl.ds(src_base + 48, 8), :]
+    for k in range(2):
+        c1, c3 = part(src[pl.ds(src_base + 32 + 8 * k, 8), :], rem, k)
+        c0 = src[pl.ds(src_base + 8 * k, 8), :]
+        c2 = src[pl.ds(src_base + 16 + 8 * k, 8), :]
+        for c, piece in enumerate((c0, c1, c2, c3)):
+            dst[pl.ds(dst_base + 32 * k + c, 8, stride=CHUNKS), :] = piece
+
+
+def blocks_loop(n, unroll, body):
+    def step(s, carry):
+        for u in range(unroll):
+            body(s * unroll + u)
+        return carry
+
+    lax.fori_loop(0, n // unroll, step, 0)
+
+
+def pack_slots(src, src_base, dst):
+    blocks_loop(N_DEV, 4, lambda d: pack16(src, src_base + d * CAP * CHUNKS, dst, d * PACK16))
+
+
+def unpack_slots(src, dst, dst_base):
+    blocks_loop(N_DEV, 4, lambda d: unpack16(src, d * PACK16, dst, dst_base + d * CAP * CHUNKS))
+
+
+def pack66(src, src_base, dst, dst_base):
+    rows = REL_DEV + NEG_DEV
+    rem = None
+    for k in range(9):
+        n = 8 if k < 8 else 2
+        c0, c1, c2, c3 = four(src, src_base + 32 * k, n)
+        dst[pl.ds(dst_base + 8 * k, n), :] = c0
+        dst[pl.ds(dst_base + rows + 8 * k, n), :] = c2
+        dst[pl.ds(dst_base + 2 * rows + 8 * k, n), :] = join(c1, c3)
+        if k == 8:
+            dst[pl.ds(dst_base + 3 * rows + 8, 2), :] = rest(c3, 0)
+        else:
+            rem = rest(c3, k) if k == 0 else jnp.where(lane(8) < 16 * k, rem, rest(c3, k))
+    dst[pl.ds(dst_base + 3 * rows, 8), :] = rem
+
+
+def unpack66(src, dst):
+    rows = REL_DEV + NEG_DEV
+    for k in range(9):
+        n = 8 if k < 8 else 2
+        rem = src[pl.ds(3 * rows, 8), :] if k < 8 else src[pl.ds(3 * rows + 8, 2), :]
+        c1, c3 = part(src[pl.ds(2 * rows + 8 * k, n), :], rem, k % 8)
+        c0 = src[pl.ds(8 * k, n), :]
+        c2 = src[pl.ds(rows + 8 * k, n), :]
+        for c, piece in enumerate((c0, c1, c2, c3)):
+            dst[pl.ds(32 * k + c, n, stride=CHUNKS), :] = piece
 
 
 def to_chunks(src, dst, n):
@@ -98,32 +190,41 @@
         in_specs=[SMEM, VMEM, VMEM],
         out_specs=(VMEM, VMEM),
         scratch_shapes=[pltpu.VMEM((LANES * CHUNKS, LANES), f32)],
-        compiler_params=params(24),
+        compiler_params=params(58),
         cost_estimate=cost(0, 8 << 20),
         name="prep",
     )(negatives, table_t, rel_t)
 
 
-def pull_kernel(asked, tab4, out):
+def pull_kernel(asked, tab4, out, picked, packed, sem):
     def body(i):
-        out[row(i), :] = tab4[row(asked[i]), :]
+        picked[row(i), :] = tab4[row(asked[i]), :]
 
     rows_loop(SLOTS, body)
+    pack_slots(picked, 0, packed)
+    store = pltpu.make_async_copy(packed, out, sem)
+    store.start()
+    store.wait()
 
 
 def pull_rows(asked, tab4):
     return pl.pallas_call(
         pull_kernel,
-        out_shape=jax.ShapeDtypeStruct((SLOTS * CHUNKS, LANES), f32),
+        out_shape=jax.ShapeDtypeStruct((N_DEV * PACK16, LANES), f32),
         in_specs=[SMEM, VMEM],
-        out_specs=VMEM,
-        compiler_params=params(24),
+        out_specs=HBM,
+        scratch_shapes=[
+            pltpu.VMEM((SLOTS * CHUNKS, LANES), f32),
+            pltpu.VMEM((N_DEV * PACK16, LANES), f32),
+            pltpu.SemaphoreType.DMA,
+        ],
+        compiler_params=params(58),
         cost_estimate=cost(0, 8 << 20),
         name="pull_rows",
     )(asked, tab4)
 
 
-def ends_kernel(heads, tails, tab4, fetched, h_out, t_out, ext, hb, tb, sems):
+def ends_kernel(heads, tails, tab4, fetched, h_out, t_out, ext, packed, hb, tb, sems):
     step = pl.program_id(0)
     local = ENT_DEV * CHUNKS
 
@@ -131,12 +232,13 @@
     def _():
         loads = (
             pltpu.make_async_copy(tab4, ext.at[pl.ds(0, local)], sems.at[0]),
-            pltpu.make_async_copy(fetched, ext.at[pl.ds(local, SLOTS * CHUNKS)], sems.at[1]),
+            pltpu.make_async_copy(fetched, packed, sems.at[1]),
         )
         for load in loads:
             load.start()
         for load in loads:
             load.wait()
+        unpack_slots(packed, ext, local)
 
     base = step * TILE
 
@@ -161,11 +263,12 @@
         out_specs=(block, block),
         scratch_shapes=[
             pltpu.VMEM(((ENT_DEV + SLOTS) * CHUNKS, LANES), f32),
+            pltpu.VMEM((N_DEV * PACK16, LANES), f32),
             pltpu.VMEM((TILE * CHUNKS, LANES), f32),
             pltpu.VMEM((TILE * CHUNKS, LANES), f32),
             pltpu.SemaphoreType.DMA((2,)),
         ],
-        compiler_params=params(24),
+        compiler_params=params(58),
         cost_estimate=cost(0, 30 << 20),
         name="ends",
     )(heads, tails, tab4, fetched)
@@ -174,7 +277,7 @@
 def query_kernel(
     rel_at, tails, shared, h_in, t_in,
     q_out, r_out, p_out, tail_local, outgoing,
-    rel, ext_grad, hb, rb, sems,
+    rel, ext_grad, packed, hb, rb, sems,
 ):
     step = pl.program_id(0)
 
@@ -214,10 +317,11 @@
         local = ENT_DEV * CHUNKS
         stores = (
             pltpu.make_async_copy(ext_grad.at[pl.ds(0, local)], tail_local, sems.at[0]),
-            pltpu.make_async_copy(ext_grad.at[pl.ds(local, SLOTS * CHUNKS)], outgoing, sems.at[1]),
+            pltpu.make_async_copy(packed, outgoing, sems.at[1]),
         )
-        for store in stores:
-            store.start()
+        stores[0].start()
+        pack_slots(ext_grad, local, packed)
+        stores[1].start()
         for store in stores:
             store.wait()
 
@@ -233,18 +337,19 @@
             plane,
             plane,
             jax.ShapeDtypeStruct((ENT_DEV * CHUNKS, LANES), f32),
-            jax.ShapeDtypeStruct((SLOTS * CHUNKS, LANES), f32),
+            jax.ShapeDtypeStruct((N_DEV * PACK16, LANES), f32),
         ),
         in_specs=[SMEM, SMEM, ANY, block, block],
-        out_specs=(block, block, block, ANY, ANY),
+        out_specs=(block, block, block, HBM, HBM),
         scratch_shapes=[
             pltpu.VMEM((N_DEV * PER, LANES), f32),
             pltpu.VMEM(((ENT_DEV + SLOTS) * CHUNKS, LANES), f32),
+            pltpu.VMEM((N_DEV * PACK16, LANES), f32),
             pltpu.VMEM((TILE * CHUNKS, LANES), f32),
             pltpu.VMEM((TILE * CHUNKS, LANES), f32),
             pltpu.SemaphoreType.DMA((2,)),
         ],
-        compiler_params=params(40),
+        compiler_params=params(58),
         cost_estimate=cost(0, 60 << 20),
         name="queries",
     )(rel_at, tails, shared, h, t)
@@ -253,7 +358,7 @@
 def grads_kernel(
     heads, grad_at, core, shared, local_grad, q_in, h_in, r_in, p_in,
     mine, other, head_grad,
-    negs, n_hi, n_lo, t_hi, t_lo, neg_acc, rel_grad, hb, rb, sems,
+    negs, n_hi, n_lo, t_hi, t_lo, neg_acc, rel_grad, packed, hb, rb, sems,
 ):
     step = pl.program_id(0)
 
@@ -305,27 +410,32 @@
 
         lax.fori_loop(0, N_DEV, place, 0)
         side = core[0]
-        half = CHIPS * PER
+        half = CHIPS * PACK66
         stores = (
-            pltpu.make_async_copy(rel_grad.at[pl.ds(pl.multiple_of((1 - side) * half, 8), half)], other, sems.at[0]),
-            pltpu.make_async_copy(rel_grad.at[pl.ds(pl.multiple_of(side * half, 8), half)], mine, sems.at[1]),
+            pltpu.make_async_copy(packed.at[pl.ds(0, half)], other, sems.at[0]),
+            pltpu.make_async_copy(packed.at[pl.ds(half, half)], mine, sems.at[1]),
         )
-        for store in stores:
-            store.start()
+        for i, owner in enumerate((1 - side, side)):
+
+            def pack(d, i=i, owner=owner):
+                pack66(rel_grad, (owner * CHIPS + d) * PER, packed, (i * CHIPS + d) * PACK66)
+
+            blocks_loop(CHIPS, 2, pack)
+            stores[i].start()
         for store in stores:
             store.wait()
 
 
 def gradients(heads, grad_at, core, shared, tail_local, q, h, r, p):
     block = pl.BlockSpec((CHUNKS, TILE, LANES), lambda i: (0, i, 0))
-    half = jax.ShapeDtypeStruct((CHIPS * PER, LANES), f32)
+    half = jax.ShapeDtypeStruct((CHIPS * PACK66, LANES), f32)
     whole = pl.BlockSpec((ENT_DEV * CHUNKS, LANES), lambda i: (0, 0))
     return pl.pallas_call(
         grads_kernel,
         grid=(E_DEV // TILE,),
         out_shape=(half, half, jax.ShapeDtypeStruct((ENT_DEV * CHUNKS, LANES), f32)),
         in_specs=[SMEM, SMEM, SMEM, ANY, ANY, block, block, block, block],
-        out_specs=(ANY, ANY, whole),
+        out_specs=(HBM, HBM, whole),
         scratch_shapes=[
             pltpu.VMEM((N_DEV, PER - REL4, LANES), f32),
             pltpu.VMEM((NEG, CHUNKS * LANES), bf16),
@@ -334,18 +444,20 @@
             pltpu.VMEM((CHUNKS * LANES, NEG), bf16),
             pltpu.VMEM((NEG, CHUNKS * LANES), f32),
             pltpu.VMEM((N_DEV * PER, LANES), f32),
+            pltpu.VMEM((N_DEV * PACK66, LANES), f32),
             pltpu.VMEM((TILE * CHUNKS, LANES), f32),
             pltpu.VMEM((TILE * CHUNKS, LANES), f32),
             pltpu.SemaphoreType.DMA((2,)),
         ],
-        compiler_params=params(52),
+        compiler_params=params(58),
         cost_estimate=cost(36_000_000_000, 60 << 20),
         name="gradients",
     )(heads, grad_at, core, shared, tail_local, q, h, r, p)
 
 
-def returned_kernel(asked, returned, head_grad, out):
+def returned_kernel(asked, packed, head_grad, out, returned):
     out[...] = head_grad[...]
+    unpack_slots(packed, returned, 0)
 
     def body(i):
         at = row(asked[i])
@@ -360,6 +472,7 @@
         out_shape=jax.ShapeDtypeStruct((ENT_DEV * CHUNKS, LANES), f32),
         in_specs=[SMEM, VMEM, VMEM],
         out_specs=VMEM,
+        scratch_shapes=[pltpu.VMEM((SLOTS * CHUNKS, LANES), f32)],
         compiler_params=params(24),
         cost_estimate=cost(0, 10 << 20),
         name="add_returned",
@@ -380,11 +493,12 @@
 def step_kernel(
     negatives, local_grad, parts, table_t, state, rel_t, rel_state,
     new_table_t, new_state, new_rel_t, new_rel_state,
-    grad, share,
+    grad, share, packed,
 ):
     grad[...] = local_grad[...]
     share[...] = jnp.zeros_like(share)
-    share[0:PER, :] = jnp.sum(parts[...], axis=0)
+    packed[...] = jnp.sum(parts[...], axis=0)
+    unpack66(packed, share)
     for i in range(NEG_DEV):
         at = row(negatives[i])
         grad[at, :] = grad[at, :] + share[REL4 + CHUNKS * i : REL4 + CHUNKS * (i + 1), :]
@@ -404,6 +518,7 @@
         scratch_shapes=[
             pltpu.VMEM((ENT_DEV * CHUNKS, LANES), f32),
             pltpu.VMEM((CHUNKS * LANES, LANES), f32),
+            pltpu.VMEM((PACK66, LANES), f32),
         ],
         compiler_params=params(40),
         cost_estimate=cost(0, 16 << 20),
@@ -435,8 +550,8 @@
     rows_out = pull_rows(asked, tab4)
 
     def exchange(rows):
-        rows = rows.reshape(N_DEV, CAP * CHUNKS, LANES)
-        return lax.all_to_all(rows, AXES, split_axis=0, concat_axis=0, tiled=True).reshape(SLOTS * CHUNKS, LANES)
+        rows = rows.reshape(N_DEV, PACK16, LANES)
+        return lax.all_to_all(rows, AXES, split_axis=0, concat_axis=0, tiled=True).reshape(N_DEV * PACK16, LANES)
 
     fetched = exchange(rows_out)
     h, t = ends(heads, tails, tab4, fetched)
@@ -448,7 +563,7 @@
     other, returned = lax.optimization_barrier((other, returned))
     paired = mine + lax.ppermute(other, "c", [(0, 1), (1, 0)])
     parts = lax.all_to_all(
-        paired.reshape(CHIPS, PER, LANES), AXES[:3], split_axis=0, concat_axis=0, tiled=True
+        paired.reshape(CHIPS, PACK66, LANES), AXES[:3], split_axis=0, concat_axis=0, tiled=True
     )
     local_grad = add_returned(asked, returned, head_grad)
     new_table_t, new_state, new_rel_t, new_rel_state = adagrad_step(

time: 400 us -> 359 us (0.90)
  waiting for transfers between devices: 208 us -> 164 us
  Pallas kernels: 99.9 us -> 120 us
  local copies, waits for them, and re-layouts: 20.2 us -> 8.06 us
    all_to_all x1, waiting for transfers between devices: 115 us -> 87.1 us  [local(): lax.all_to_all(paired.reshape(CHIPS, PACK66, LANES), AXES[:3], split_axis...]
    unnamed x35 -> x19, local copies, waits for them, and re-layouts: 19.1 us -> 5.65 us
    all_to_all x2, waiting for transfers between devices: 59 us -> 46.1 us  [exchange(): lax.all_to_all(rows, AXES, split_axis=0, concat_axis=0, tiled=True)]
    pallas_call x1, Pallas kernels: 4.17 us -> 9.67 us  [pull_rows(): pl.pallas_call(pull_kernel, out_shape=jax.ShapeDtypeStruct((N_DEV * PACK1...]
    pallas_call x1, Pallas kernels: 9.82 us -> 14.3 us  [ends(): pl.pallas_call(ends_kernel, grid=(E_DEV // TILE,), out_shape=(plane, plan...]
  transfers between devices with their start and end apart: 5 -> 5, of which waited for: 5 -> 4; matrix products, arithmetic and copies ran while one was open for 1% -> 1% of each run, Pallas kernels for 17% -> 24%
where the time goes in v4:
time: 359 us; the launch traced here: 357 us
  waiting for transfers between devices  164 us (46%)
  Pallas kernels  120 us (33%)
  starting transfers between devices  29.4 us (8%)
  blocking collectives  15.3 us (4%)
  between operations  14.2 us (4%)
  local copies, waits for them, and re-layouts  8.06 us (2%)
  other arithmetic  6.59 us (2%)
    all_to_all x1, waiting for transfers between devices, local(): lax.all_to_all(paired.reshape(CHIPS, PACK66, LANES), AXES[:3], split_axis...  87.1 us
    pallas_call x1, Pallas kernels, gradients(): pl.pallas_call(grads_kernel, grid=(E_DEV // TILE,), out_shape=(half, half...  49.2 us
    all_to_all x2, waiting for transfers between devices, exchange(): lax.all_to_all(rows, AXES, split_axis=0, concat_axis=0, tiled=True)  46.1 us
    pallas_call x1, Pallas kernels, queries(): pl.pallas_call(query_kernel, grid=(E_DEV // TILE,), out_shape=(plane, pla...  25.9 us
    all_gather x1, waiting for transfers between devices, local(): shared = lax.all_gather(ag4, AXES, axis=0, tiled=True)  19.8 us
    all_to_all x2, starting transfers between devices, exchange(): lax.all_to_all(rows, AXES, split_axis=0, concat_axis=0, tiled=True)  18.5 us
    all_to_all x1, blocking collectives, local(): lax.all_to_all(pull_lists, AXES, split_axis=0, concat_axis=0, tiled=True)  15.3 us
    pallas_call x1, Pallas kernels, ends(): pl.pallas_call(ends_kernel, grid=(E_DEV // TILE,), out_shape=(plane, plan...  14.3 us
  transfers between devices with their start and end apart: 5, of which 4 were waited for; matrix products, arithmetic and copies ran while one was open for 1% of the time, Pallas kernels for 24%

profile of v4, /device:TPU:102, one launch (start us, length us, event | category | flops | bytes accessed | tf_op | source)
XLA Modules:
  0.0 357.4 jit_solution(8674579741997369974)
XLA Ops:
  7.2 0.0 all-gather.2.cloned.1.call-start
  7.2 1.0 copy.19
  8.2 0.7 pad_bitcast_fusion.rel_t
  8.9 3.5 prep.1
  12.4 0.0 all-gather.2.cloned.1.call-update
  12.5 0.8 copy.18
  13.3 15.3 %all_to_all.24 = s32[128,1,16]{2,1,0:T(1,128)S(1)} all-to-all(s32[128,1,16]{2,1,0:T(1,128)S(1)} %bitcast.28), channel_id=1, replica_groups=mesh['x'=4,'z'=4,'y'=4,'c'=2] {'x','z','y','c'}, dimensions={0} | all-to-all | bytes 16384 | tf_op jit(solution)/shard_map/all_to_all | solution.py:549
  28.6 0.5 broadcast.24
  29.1 0.8 reduce.3
  29.9 0.7 reshape.46.asked
  30.6 9.7 %pull_rows.1 = f32[7168,128]{1,0:T(8,128)} custom-call(s32[2048]{0:T(1024)} %reshape.46.asked, f32[4096,128]{1,0:T(8,128)} %get-tuple-element.23.tab4), custom_call_target="tpu_custom_call" | custom-call | bytes 8388608 | tf_op jit(solution)/shard_map/pull_rows/pallas_call | solution.py:211
  40.3 0.0 copy-start.6
  40.3 9.3 %all-to-all-start.1 = ((f32[128,56,128]{2,1,0:T(8,128)}), f32[128,56,128]{2,1,0:T(8,128)}, u32[]{:S(2)}, u32[]{:S(2)}) async-start(f32[128,56,128]{2,1,0:T(8,128)} %bitcast.26), calls=%async_computation.1 | async-start | bytes 7340032 | tf_op jit(solution)/shard_map/all_to_all | solution.py:554
  49.6 0.0 copy-done.6
  49.6 0.6 multiply_add_fusion
  50.3 46.1 %all-to-all-done.1 = f32[128,56,128]{2,1,0:T(8,128)} async-done(((f32[128,56,128]{2,1,0:T(8,128)}), f32[128,56,128]{2,1,0:T(8,128)}, u32[]{:S(2)}, u32[]{:S(2)}) %all-to-all-start.1) | async-done | bytes 3670048 | tf_op jit(solution)/shard_map/all_to_all | solution.py:554
  96.4 14.3 %ends.1 = (f32[4,2048,128]{2,1,0:T(8,128)}, f32[4,2048,128]{2,1,0:T(8,128)}) custom-call(s32[2048]{0:T(1024)} %heads.3, s32[2048]{0:T(1024)} %tails.3, f32[4096,128]{1,0:T(8,128)} %get-tuple-element.23.tab4, f32[7168,128]{1,0:T(8,128)} %bitcast.6.fetched), custom_call_target="tpu_custom_call" | custom-call | bytes 31457280 | tf_op jit(solution)/shard_map/ends/pallas_call | solution.py:258
  110.7 19.8 %all-gather.2.cloned.1.call-done.shared = f32[33792,128]{1,0:T(8,128)} async-done(((f32[264,128]{1,0:T(8,128)}), f32[33792,128]{1,0:T(8,128)}) %all-gather.2.cloned.1.call-update) | async-done | bytes 17301520 | tf_op jit(solution)/shard_map/all_gather | solution.py:548
  130.5 25.9 %queries.1 = (f32[4,2048,128]{2,1,0:T(8,128)}, f32[4,2048,128]{2,1,0:T(8,128)}, f32[4,2048,128]{2,1,0:T(8,128)}, f32[4096,128]{1,0:T(8,128)}, f32[7168,128]{1,0:T(8,128)}) custom-call(s32[2048]{0:T(1024)} %get-tuple-element.52.rel_at, s32[2048]{0:T(1024)} %tails.3, f32[33792,128]{1,0:T(8,128)} %all-gather.2.cloned.1.call-done.shared, ...), custom_call_target="tpu_custom_call" | custom-call | bytes 62914560 | tf_op jit(solution)/shard_map/queries/pallas_call | solution.py:332
  156.4 9.1 %all-to-all-start.2 = ((f32[128,56,128]{2,1,0:T(8,128)}), f32[128,56,128]{2,1,0:T(8,128)}, u32[]{:S(2)}, u32[]{:S(2)}) async-start(f32[128,56,128]{2,1,0:T(8,128)} %bitcast.27), calls=%async_computation.2 | async-start | bytes 7340032 | tf_op jit(solution)/shard_map/all_to_all | solution.py:554
  165.5 49.2 %gradients.1 = (f32[13312,128]{1,0:T(8,128)}, f32[13312,128]{1,0:T(8,128)}, f32[4096,128]{1,0:T(8,128)}) custom-call(s32[2048]{0:T(1024)} %heads.3, s32[2048]{0:T(1024)} %get-tuple-element.53.grad_at, s32[1]{0:T(128)} %bitcast.1.core, f32[128,264,128]{2,1,0:T(8,128)} %bitcast.25, f32[4096,128]{1,0:T(8,128)} %get-tuple-element.26.local_grad, ...), custom_call_target="tpu_custom_call" | custom-call | flops 35999997952 | bytes 62914560 | tf_op jit(solution)/shard_map/gradients/pallas_call | solution.py:433
  214.7 0.0 all-to-all-done.2
  214.7 0.3 collective-permute-start
  215.0 10.9 %collective-permute-done = f32[13312,128]{1,0:T(8,128)S(1)} collective-permute-done((f32[13312,128]{1,0:T(8,128)}, f32[13312,128]{1,0:T(8,128)S(1)}, u32[]{:S(2)}, u32[]{:S(2)}) %collective-permute-start) | collective-permute-done | bytes 6815776 | tf_op jit(solution)/shard_map/ppermute | solution.py:564
  225.9 5.2 %add.33 = f32[13312,128]{1,0:T(8,128)} add(f32[13312,128]{1,0:T(8,128)} %get-tuple-element.34, f32[13312,128]{1,0:T(8,128)S(1)} %collective-permute-done) | non-fusion elementwise | flops 1703936 | bytes 20447232 | tf_op jit(solution)/shard_map/add | solution.py:564
  231.1 0.0 copy-start.7
  231.1 0.0 copy-start.3
  231.1 0.0 copy-start.2
  231.1 0.0 copy-start.4
  231.1 10.7 %all-to-all-start.3 = ((f32[64,208,128]{2,1,0:T(8,128)}), f32[64,208,128]{2,1,0:T(8,128)}, u32[]{:S(2)}, u32[]{:S(2)}) async-start(f32[64,208,128]{2,1,0:T(8,128)} %bitcast.24), calls=%async_computation.3 | async-start | bytes 13631488 | tf_op jit(solution)/shard_map/all_to_all | solution.py:565
  241.7 0.0 copy-done.7
  241.7 0.0 copy-start.5
  241.8 0.0 copy-done.3
  241.8 0.0 copy-start.1
  241.8 1.6 copy-done.1
  243.4 11.8 %add_returned.1.local_grad = f32[4096,128]{1,0:T(8,128)S(1)} custom-call(s32[2048]{0:T(1024)S(1)} %copy-done.3, f32[7168,128]{1,0:T(8,128)} %bitcast.8.packed, f32[4096,128]{1,0:T(8,128)S(1)} %copy-done.1), custom_call_target="tpu_custom_call" | custom-call | bytes 10485760 | tf_op jit(solution)/shard_map/add_returned/pallas_call | solution.py:470
  255.2 87.1 %all-to-all-done.3.parts = f32[64,208,128]{2,1,0:T(8,128)} async-done(((f32[64,208,128]{2,1,0:T(8,128)}), f32[64,208,128]{2,1,0:T(8,128)}, u32[]{:S(2)}, u32[]{:S(2)}) %all-to-all-start.3) | async-done | bytes 6815776 | tf_op jit(solution)/shard_map/all_to_all | solution.py:565
  342.3 0.0 copy-done.2
  342.3 0.0 copy-done.4
  342.3 0.0 copy-done.5
  342.3 0.0 copy-start
  342.3 1.4 copy-done
  343.7 5.6 %adagrad_step.1 = (f32[400,1024]{1,0:T(8,128)}, f32[1,1024]{1,0:T(1,128)}, f32[400,128]{1,0:T(8,128)S(1)}, f32[1,128]{1,0:T(1,128)S(1)}) custom-call(s32[8]{0:T(128)S(1)} %copy-done.5, f32[4096,128]{1,0:T(8,128)S(1)} %add_returned.1.local_grad, f32[64,208,128]{2,1,0:T(8,128)} %all-to-all-done.3.parts, f32[400,1024]{1,0:T(8,128)S(1)} %bitcast.21, ...), custom_call_target="tpu_custom_call" | custom-call | bytes 16777216 | tf_op jit(solution)/shard_map/adagrad_step/pallas_call | solution.py:513
  349.3 0.8 copy.20
  350.1 0.5 slice_bitcast_fusion
  (1 shorter events, 0.0 us)
Async XLA Ops:
  7.2 123.3 %all-gather.2.cloned.1.call-start = ((), (), s32[]{:S(2)}) async-start(), calls=%async_computation.4 | async-start | bytes 17436672 | tf_op jit(solution)/shard_map/all_gather | solution.py:548
  40.3 9.4 %copy-start.6 = (s32[2048]{0:T(1024)S(1)}, s32[2048]{0:T(1024)}, u32[]{:S(2)}) copy-start(s32[2048]{0:T(1024)} %param.14) | copy-start | bytes 24580
  40.3 56.1 %all-to-all-start.1 = ((f32[128,56,128]{2,1,0:T(8,128)}), f32[128,56,128]{2,1,0:T(8,128)}, u32[]{:S(2)}, u32[]{:S(2)}) async-start(f32[128,56,128]{2,1,0:T(8,128)} %bitcast.26), calls=%async_computation.1 | async-start | bytes 7340032 | tf_op jit(solution)/shard_map/all_to_all | solution.py:554
  156.4 58.3 %all-to-all-start.2 = ((f32[128,56,128]{2,1,0:T(8,128)}), f32[128,56,128]{2,1,0:T(8,128)}, u32[]{:S(2)}, u32[]{:S(2)}) async-start(f32[128,56,128]{2,1,0:T(8,128)} %bitcast.27), calls=%async_computation.2 | async-start | bytes 7340032 | tf_op jit(solution)/shard_map/all_to_all | solution.py:554
  214.7 11.2 %collective-permute-start = (f32[13312,128]{1,0:T(8,128)}, f32[13312,128]{1,0:T(8,128)S(1)}, u32[]{:S(2)}, u32[]{:S(2)}) collective-permute-start(f32[13312,128]{1,0:T(8,128)} %get-tuple-element.35), channel_id=1, source_target_pairs={{0,1},{1,0},{2,3},{3,2},{4,5},{5,4},{6,7},{7,6},{8,9},{9,8},{10,11... | collective-permute-start | bytes 20447240 | tf_op jit(solution)/shard_map/ppermute | solution.py:564
  231.1 10.7 %copy-start.7 = (f32[58]{0:T(128)S(1)}, f32[58]{0:T(128)}, u32[]{:S(2)}) copy-start(f32[58]{0:T(128)} %param.12) | copy-start | bytes 700
  231.1 10.7 %copy-start.3 = (s32[2048]{0:T(1024)S(1)}, s32[2048]{0:T(1024)}, u32[]{:S(2)}) copy-start(s32[2048]{0:T(1024)} %reshape.46.asked) | copy-start | bytes 24580
  231.1 111.2 %copy-start.2 = (f32[400,128]{1,0:T(8,128)S(1)}, f32[400,128]{1,0:T(8,128)}, u32[]{:S(2)}) copy-start(f32[400,128]{1,0:T(8,128)} %pad_bitcast_fusion.rel_t) | copy-start | bytes 614404
  231.1 111.2 %copy-start.4 = (f32[1024]{0:T(1024)S(1)}, f32[1024]{0:T(1024)}, u32[]{:S(2)}) copy-start(f32[1024]{0:T(1024)} %param.10) | copy-start | bytes 12292
  231.1 111.2 %all-to-all-start.3 = ((f32[64,208,128]{2,1,0:T(8,128)}), f32[64,208,128]{2,1,0:T(8,128)}, u32[]{:S(2)}, u32[]{:S(2)}) async-start(f32[64,208,128]{2,1,0:T(8,128)} %bitcast.24), calls=%async_computation.3 | async-start | bytes 13631488 | tf_op jit(solution)/shard_map/all_to_all | solution.py:565
  241.7 100.5 %copy-start.5 = (s32[8]{0:T(128)S(1)}, s32[8]{0:T(128)}, u32[]{:S(2)}) copy-start(s32[8]{0:T(128)} %negatives.3) | copy-start | bytes 100
  241.8 1.6 copy-start.1
  342.3 1.4 copy-start
Sparse Core Ops, SparseCore 0:
  12.6 117.8 all-gather.1

commit v5 on v4

--- a/solution.py
+++ b/solution.py
@@ -224,18 +224,109 @@
     )(asked, tab4)
 
 
-def ends_kernel(heads, tails, tab4, fetched, h_out, t_out, ext, packed, hb, tb, sems):
+def query_kernel(
+    heads, rel_at, tab4, shared,
+    q_out, h_out, r_out, back_out, neg_acc,
+    tab, rel, n_hi, n_lo, t_hi, t_lo, hb, rb, sems,
+):
     step = pl.program_id(0)
-    local = ENT_DEV * CHUNKS
 
     @pl.when(step == 0)
     def _():
         loads = (
-            pltpu.make_async_copy(tab4, ext.at[pl.ds(0, local)], sems.at[0]),
-            pltpu.make_async_copy(fetched, packed, sems.at[1]),
+            pltpu.make_async_copy(tab4, tab, sems.at[0]),
+            pltpu.make_async_copy(shared, rel, sems.at[1]),
         )
         for load in loads:
             load.start()
+        neg_acc[...] = jnp.zeros_like(neg_acc)
+        for load in loads:
+            load.wait()
+
+        for c in range(CHUNKS):
+            lanes = slice(c * LANES, (c + 1) * LANES)
+
+            def place(d, carry, c=c):
+                rows = pl.ds(pl.multiple_of(d * NEG_DEV, NEG_DEV), NEG_DEV)
+                hb[rows, :] = rel[pl.ds(d * PER + REL4 + c, NEG_DEV, stride=CHUNKS), :]
+                return carry
+
+            lax.fori_loop(0, N_DEV, place, 0)
+            piece = hb[...]
+            n_hi[:, lanes], n_lo[:, lanes] = split(piece)
+            t_hi[lanes, :], t_lo[lanes, :] = split(piece.T)
+
+    base = step * TILE
+
+    def gather(i):
+        hb[row(i), :] = tab[row(heads[base + i]), :]
+        rb[row(i), :] = rel[row(rel_at[base + i]), :]
+
+    rows_loop(TILE, gather)
+    h = [chunk_of(hb, c, TILE) for c in range(CHUNKS)]
+    r = [chunk_of(rb, c, TILE) for c in range(CHUNKS)]
+    q = [h[0] * r[0] - h[2] * r[2], h[1] * r[1] - h[3] * r[3], h[0] * r[2] + h[2] * r[0], h[1] * r[3] + h[3] * r[1]]
+    for c in range(CHUNKS):
+        q_out[c] = q[c]
+        h_out[c] = h[c]
+        r_out[c] = r[c]
+    q = split(jnp.concatenate(q, axis=1))
+    negative = dot3(q, (t_hi[...], t_lo[...]), ((1,), (0,)))
+    neg_grad = split(jax.nn.sigmoid(negative) * (1.0 / NEG))
+    neg_acc[...] += dot3(neg_grad, q, ((0,), (0,)))
+    back = dot3(neg_grad, (n_hi[...], n_lo[...]), ((1,), (0,)))
+    for c in range(CHUNKS):
+        back_out[c] = back[:, c * LANES : (c + 1) * LANES]
+
+
+PLANE = jax.ShapeDtypeStruct((CHUNKS, E_DEV, LANES), f32)
+BLOCK = pl.BlockSpec((CHUNKS, TILE, LANES), lambda i: (0, i, 0))
+
+
+def queries(heads, rel_at, tab4, shared):
+    rows = pltpu.VMEM((TILE * CHUNKS, LANES), f32)
+    wide = pltpu.VMEM((NEG, CHUNKS * LANES), bf16)
+    tall = pltpu.VMEM((CHUNKS * LANES, NEG), bf16)
+    return pl.pallas_call(
+        query_kernel,
+        grid=(E_DEV // TILE,),
+        out_shape=(PLANE, PLANE, PLANE, PLANE, jax.ShapeDtypeStruct((NEG, CHUNKS * LANES), f32)),
+        in_specs=[SMEM, SMEM, ANY, ANY],
+        out_specs=(BLOCK, BLOCK, BLOCK, BLOCK, pl.BlockSpec((NEG, CHUNKS * LANES), lambda i: (0, 0))),
+        scratch_shapes=[
+            pltpu.VMEM((ENT_DEV * CHUNKS, LANES), f32),
+            pltpu.VMEM((N_DEV * PER, LANES), f32),
+            wide,
+            wide,
+            tall,
+            tall,
+            rows,
+            rows,
+            pltpu.SemaphoreType.DMA((2,)),
+        ],
+        compiler_params=params(58),
+        cost_estimate=cost(36_000_000_000, 60 << 20),
+        name="queries",
+    )(heads, rel_at, tab4, shared)
+
+
+def tail_kernel(
+    tails, tab4, fetched, q_in,
+    p_out, tail_local, outgoing,
+    ext, ext_grad, packed, tb, sems,
+):
+    step = pl.program_id(0)
+    local = ENT_DEV * CHUNKS
+
+    @pl.when(step == 0)
+    def _():
+        loads = (
+            pltpu.make_async_copy(fetched, packed, sems.at[1]),
+            pltpu.make_async_copy(tab4, ext.at[pl.ds(0, local)], sems.at[0]),
+        )
+        for load in loads:
+            load.start()
+        ext_grad[...] = jnp.zeros_like(ext_grad)
         for load in loads:
             load.wait()
         unpack_slots(packed, ext, local)
@@ -243,78 +334,25 @@
     base = step * TILE
 
     def gather(i):
-        hb[row(i), :] = ext[row(heads[base + i]), :]
         tb[row(i), :] = ext[row(tails[base + i]), :]
 
     rows_loop(TILE, gather)
-    for c in range(CHUNKS):
-        h_out[c] = chunk_of(hb, c, TILE)
-        t_out[c] = chunk_of(tb, c, TILE)
-
-
-def ends(heads, tails, tab4, fetched):
-    plane = jax.ShapeDtypeStruct((CHUNKS, E_DEV, LANES), f32)
-    block = pl.BlockSpec((CHUNKS, TILE, LANES), lambda i: (0, i, 0))
-    return pl.pallas_call(
-        ends_kernel,
-        grid=(E_DEV // TILE,),
-        out_shape=(plane, plane),
-        in_specs=[SMEM, SMEM, ANY, ANY],
-        out_specs=(block, block),
-        scratch_shapes=[
-            pltpu.VMEM(((ENT_DEV + SLOTS) * CHUNKS, LANES), f32),
-            pltpu.VMEM((N_DEV * PACK16, LANES), f32),
-            pltpu.VMEM((TILE * CHUNKS, LANES), f32),
-            pltpu.VMEM((TILE * CHUNKS, LANES), f32),
-            pltpu.SemaphoreType.DMA((2,)),
-        ],
-        compiler_params=params(58),
-        cost_estimate=cost(0, 30 << 20),
-        name="ends",
-    )(heads, tails, tab4, fetched)
-
-
-def query_kernel(
-    rel_at, tails, shared, h_in, t_in,
-    q_out, r_out, p_out, tail_local, outgoing,
-    rel, ext_grad, packed, hb, rb, sems,
-):
-    step = pl.program_id(0)
-
-    @pl.when(step == 0)
-    def _():
-        load = pltpu.make_async_copy(shared, rel, sems.at[0])
-        load.start()
-        ext_grad[...] = jnp.zeros_like(ext_grad)
-        load.wait()
-
-    base = step * TILE
-
-    def gather(i):
-        rb[row(i), :] = rel[row(rel_at[base + i]), :]
-
-    rows_loop(TILE, gather)
-    h = [h_in[c] for c in range(CHUNKS)]
-    r = [chunk_of(rb, c, TILE) for c in range(CHUNKS)]
-    t = [t_in[c] for c in range(CHUNKS)]
-    q = [h[0] * r[0] - h[2] * r[2], h[1] * r[1] - h[3] * r[3], h[0] * r[2] + h[2] * r[0], h[1] * r[3] + h[3] * r[1]]
+    t = [chunk_of(tb, c, TILE) for c in range(CHUNKS)]
+    q = [q_in[c] for c in range(CHUNKS)]
     score = (q[0] * t[0] + q[1] * t[1]) + (q[2] * t[2] + q[3] * t[3])
     pos_grad = jax.nn.sigmoid(jnp.sum(score, axis=1, keepdims=True)) - 1.0
     for c in range(CHUNKS):
-        q_out[c] = q[c]
-        r_out[c] = r[c]
         p_out[c] = pos_grad * t[c]
-        hb[pl.ds(c, TILE, stride=CHUNKS), :] = pos_grad * q[c]
+        tb[pl.ds(c, TILE, stride=CHUNKS), :] = pos_grad * q[c]
 
     def scatter(i):
         at = row(tails[base + i])
-        ext_grad[at, :] = ext_grad[at, :] + hb[row(i), :]
+        ext_grad[at, :] = ext_grad[at, :] + tb[row(i), :]
 
     rows_loop(TILE, scatter)
 
     @pl.when(step == E_DEV // TILE - 1)
     def _():
-        local = ENT_DEV * CHUNKS
         stores = (
             pltpu.make_async_copy(ext_grad.at[pl.ds(0, local)], tail_local, sems.at[0]),
             pltpu.make_async_copy(packed, outgoing, sems.at[1]),
@@ -326,66 +364,46 @@
             store.wait()
 
 
-def queries(rel_at, tails, shared, h, t):
-    plane = jax.ShapeDtypeStruct((CHUNKS, E_DEV, LANES), f32)
-    block = pl.BlockSpec((CHUNKS, TILE, LANES), lambda i: (0, i, 0))
+def tail_terms(tails, tab4, fetched, q):
     return pl.pallas_call(
-        query_kernel,
+        tail_kernel,
         grid=(E_DEV // TILE,),
         out_shape=(
-            plane,
-            plane,
-            plane,
+            PLANE,
             jax.ShapeDtypeStruct((ENT_DEV * CHUNKS, LANES), f32),
             jax.ShapeDtypeStruct((N_DEV * PACK16, LANES), f32),
         ),
-        in_specs=[SMEM, SMEM, ANY, block, block],
-        out_specs=(block, block, block, HBM, HBM),
+        in_specs=[SMEM, ANY, ANY, BLOCK],
+        out_specs=(BLOCK, HBM, HBM),
         scratch_shapes=[
-            pltpu.VMEM((N_DEV * PER, LANES), f32),
+            pltpu.VMEM(((ENT_DEV + SLOTS) * CHUNKS, LANES), f32),
             pltpu.VMEM(((ENT_DEV + SLOTS) * CHUNKS, LANES), f32),
             pltpu.VMEM((N_DEV * PACK16, LANES), f32),
-            pltpu.VMEM((TILE * CHUNKS, LANES), f32),
             pltpu.VMEM((TILE * CHUNKS, LANES), f32),
             pltpu.SemaphoreType.DMA((2,)),
         ],
         compiler_params=params(58),
-        cost_estimate=cost(0, 60 << 20),
-        name="queries",
-    )(rel_at, tails, shared, h, t)
-
-
-def grads_kernel(
-    heads, grad_at, core, shared, local_grad, q_in, h_in, r_in, p_in,
+        cost_estimate=cost(0, 30 << 20),
+        name="tail_terms",
+    )(tails, tab4, fetched, q)
+
+
+def edge_kernel(
+    heads, grad_at, core, tail_local, neg_acc, h_in, r_in, p_in, back_in,
     mine, other, head_grad,
-    negs, n_hi, n_lo, t_hi, t_lo, neg_acc, rel_grad, packed, hb, rb, sems,
+    rel_grad, packed, hb, rb, sems,
 ):
     step = pl.program_id(0)
 
     @pl.when(step == 0)
     def _():
-        load = pltpu.make_async_copy(shared.at[:, pl.ds(REL4, PER - REL4), :], negs, sems.at[0])
-        load.start()
-        start = pltpu.make_async_copy(local_grad, head_grad, sems.at[1])
+        start = pltpu.make_async_copy(tail_local, head_grad, sems.at[0])
         start.start()
         rel_grad[...] = jnp.zeros_like(rel_grad)
-        neg_acc[...] = jnp.zeros_like(neg_acc)
-        load.wait()
-        flat = negs.reshape(NEG * CHUNKS, LANES)
-        for c in range(CHUNKS):
-            lanes = slice(c * LANES, (c + 1) * LANES)
-            piece = chunk_of(flat, c, NEG)
-            n_hi[:, lanes], n_lo[:, lanes] = split(piece)
-            t_hi[lanes, :], t_lo[lanes, :] = split(piece.T)
         start.wait()
 
     base = step * TILE
-    q = split(jnp.concatenate([q_in[c] for c in range(CHUNKS)], axis=1))
-    negative = dot3(q, (t_hi[...], t_lo[...]), ((1,), (0,)))
-    neg_grad = split(jax.nn.sigmoid(negative) * (1.0 / NEG))
-    neg_acc[...] += dot3(neg_grad, q, ((0,), (0,)))
-    back = dot3(neg_grad, (n_hi[...], n_lo[...]), ((1,), (0,)))
-    g = [p_in[c] + back[:, c * LANES : (c + 1) * LANES] for c in range(CHUNKS)]
+    g = [p_in[c] + back_in[c] for c in range(CHUNKS)]
     for k in range(2):
         for buf, src in ((hb, r_in), (rb, h_in)):
             buf[pl.ds(k, TILE, stride=CHUNKS), :] = g[k] * src[k] + g[k + 2] * src[k + 2]
@@ -426,23 +444,16 @@
             store.wait()
 
 
-def gradients(heads, grad_at, core, shared, tail_local, q, h, r, p):
-    block = pl.BlockSpec((CHUNKS, TILE, LANES), lambda i: (0, i, 0))
+def gradients(heads, grad_at, core, tail_local, neg_acc, h, r, p, back):
     half = jax.ShapeDtypeStruct((CHIPS * PACK66, LANES), f32)
     whole = pl.BlockSpec((ENT_DEV * CHUNKS, LANES), lambda i: (0, 0))
     return pl.pallas_call(
-        grads_kernel,
+        edge_kernel,
         grid=(E_DEV // TILE,),
         out_shape=(half, half, jax.ShapeDtypeStruct((ENT_DEV * CHUNKS, LANES), f32)),
-        in_specs=[SMEM, SMEM, SMEM, ANY, ANY, block, block, block, block],
+        in_specs=[SMEM, SMEM, SMEM, ANY, pl.BlockSpec((NEG, CHUNKS * LANES), lambda i: (0, 0)), BLOCK, BLOCK, BLOCK, BLOCK],
         out_specs=(HBM, HBM, whole),
         scratch_shapes=[
-            pltpu.VMEM((N_DEV, PER - REL4, LANES), f32),
-            pltpu.VMEM((NEG, CHUNKS * LANES), bf16),
-            pltpu.VMEM((NEG, CHUNKS * LANES), bf16),
-            pltpu.VMEM((CHUNKS * LANES, NEG), bf16),
-            pltpu.VMEM((CHUNKS * LANES, NEG), bf16),
-            pltpu.VMEM((NEG, CHUNKS * LANES), f32),
             pltpu.VMEM((N_DEV * PER, LANES), f32),
             pltpu.VMEM((N_DEV * PACK66, LANES), f32),
             pltpu.VMEM((TILE * CHUNKS, LANES), f32),
@@ -450,9 +461,9 @@
             pltpu.SemaphoreType.DMA((2,)),
         ],
         compiler_params=params(58),
-        cost_estimate=cost(36_000_000_000, 60 << 20),
+        cost_estimate=cost(0, 1 << 20),
         name="gradients",
-    )(heads, grad_at, core, shared, tail_local, q, h, r, p)
+    )(heads, grad_at, core, tail_local, neg_acc, h, r, p, back)
 
 
 def returned_kernel(asked, packed, head_grad, out, returned):
@@ -547,18 +558,18 @@
     tab4, ag4 = prep(negatives, table_t, rel_t)
     shared = lax.all_gather(ag4, AXES, axis=0, tiled=True)
     asked = lax.all_to_all(pull_lists, AXES, split_axis=0, concat_axis=0, tiled=True).reshape(SLOTS)
-    rows_out = pull_rows(asked, tab4)
+    rows_out, shared = lax.optimization_barrier((pull_rows(asked, tab4), shared))
 
     def exchange(rows):
         rows = rows.reshape(N_DEV, PACK16, LANES)
         return lax.all_to_all(rows, AXES, split_axis=0, concat_axis=0, tiled=True).reshape(N_DEV * PACK16, LANES)
 
     fetched = exchange(rows_out)
-    h, t = ends(heads, tails, tab4, fetched)
-    q, r, p, tail_local, outgoing = queries(rel_at, tails, shared, h, t)
+    q, h, r, back, neg_acc = queries(heads, rel_at, tab4, shared)
+    p, tail_local, outgoing = tail_terms(tails, tab4, fetched, q)
     returned = exchange(outgoing)
     mine, other, head_grad = gradients(
-        heads, grad_at, core.reshape(1), shared.reshape(N_DEV, PER, LANES), tail_local, q, h, r, p
+        heads, grad_at, core.reshape(1), tail_local, neg_acc, h, r, p, back
     )
     other, returned = lax.optimization_barrier((other, returned))
     paired = mine + lax.ppermute(other, "c", [(0, 1), (1, 0)])

time: 359 us -> 366 us (1.019)
  Pallas kernels: 120 us -> 126 us
    all_gather x1, waiting for transfers between devices: 19.8 us -> 54 us  [local(): shared = lax.all_gather(ag4, AXES, axis=0, tiled=True)]
    all_to_all x2, waiting for transfers between devices: 46.1 us -> 15.7 us  [exchange(): lax.all_to_all(rows, AXES, split_axis=0, concat_axis=0, tiled=True)]
    pallas_call x3, Pallas kernels: 89.3 us -> 95.6 us  [the longest x1 41.5 us: queries(): pl.pallas_call(query_kernel, grid=(E_DEV // TILE,), out_shape=(PLANE, PLA...]
  transfers between devices with their start and end apart: 5 -> 5, of which waited for: 4 -> 5; matrix products, arithmetic and copies ran while one was open for 1% -> 1% of each run, Pallas kernels for 24% -> 25%
where the time goes in v5:
time: 366 us; the launch traced here: 363 us
  waiting for transfers between devices  164 us (45%)
  Pallas kernels  126 us (34%)
  starting transfers between devices  28.4 us (8%)
  blocking collectives  15.3 us (4%)
  between operations  14.2 us (4%)
  local copies, waits for them, and re-layouts  8.06 us (2%)
  other arithmetic  6.64 us (2%)
    all_to_all x1, waiting for transfers between devices, local(): lax.all_to_all(paired.reshape(CHIPS, PACK66, LANES), AXES[:3], split_axis...  83.5 us
    all_gather x1, waiting for transfers between devices, local(): shared = lax.all_gather(ag4, AXES, axis=0, tiled=True)  54 us
    pallas_call x1, Pallas kernels, queries(): pl.pallas_call(query_kernel, grid=(E_DEV // TILE,), out_shape=(PLANE, PLA...  41.5 us
    pallas_call x1, Pallas kernels, gradients(): pl.pallas_call(edge_kernel, grid=(E_DEV // TILE,), out_shape=(half, half,...  28.8 us
    pallas_call x1, Pallas kernels, tail_terms(): pl.pallas_call(tail_kernel, grid=(E_DEV // TILE,), out_shape=(PLANE, jax....  25.3 us
    all_to_all x2, starting transfers between devices, exchange(): lax.all_to_all(rows, AXES, split_axis=0, concat_axis=0, tiled=True)  18.6 us
    all_to_all x2, waiting for transfers between devices, exchange(): lax.all_to_all(rows, AXES, split_axis=0, concat_axis=0, tiled=True)  15.7 us
    all_to_all x1, blocking collectives, local(): lax.all_to_all(pull_lists, AXES, split_axis=0, concat_axis=0, tiled=True)  15.3 us
  transfers between devices with their start and end apart: 5, of which 5 were waited for; matrix products, arithmetic and copies ran while one was open for 1% of the time, Pallas kernels for 25%

profile of v5, /device:TPU:102, one launch (start us, length us, event | category | flops | bytes accessed | tf_op | source)
XLA Modules:
  0.0 362.9 jit_solution(18045414063187179247)
XLA Ops:
  7.2 0.0 all-gather.2.cloned.1.call-start
  7.2 1.0 copy.19
  8.2 0.7 pad_bitcast_fusion.rel_t
  8.9 3.4 prep.1
  12.4 0.0 all-gather.2.cloned.1.call-update
  12.4 0.8 copy.18
  13.2 15.3 %all_to_all.24 = s32[128,1,16]{2,1,0:T(1,128)S(1)} all-to-all(s32[128,1,16]{2,1,0:T(1,128)S(1)} %bitcast.26), channel_id=1, replica_groups=mesh['x'=4,'z'=4,'y'=4,'c'=2] {'x','z','y','c'}, dimensions={0} | all-to-all | bytes 16384 | tf_op jit(solution)/shard_map/all_to_all | solution.py:560
  28.5 0.5 broadcast.24
  29.1 0.8 reduce.3
  29.9 0.7 reshape.43.asked
  30.6 9.7 %pull_rows.1 = f32[7168,128]{1,0:T(8,128)} custom-call(s32[2048]{0:T(1024)} %reshape.43.asked, f32[4096,128]{1,0:T(8,128)} %get-tuple-element.25.tab4), custom_call_target="tpu_custom_call" | custom-call | bytes 8388608 | tf_op jit(solution)/shard_map/pull_rows/pallas_call | solution.py:211
  40.2 0.0 copy-start.6
  40.2 54.0 %all-gather.2.cloned.1.call-done.shared = f32[33792,128]{1,0:T(8,128)} async-done(((f32[264,128]{1,0:T(8,128)}), f32[33792,128]{1,0:T(8,128)}) %all-gather.2.cloned.1.call-update) | async-done | bytes 17301520 | tf_op jit(solution)/shard_map/all_gather | solution.py:559
  94.2 9.1 %all-to-all-start.1 = ((f32[128,56,128]{2,1,0:T(8,128)}), f32[128,56,128]{2,1,0:T(8,128)}, u32[]{:S(2)}, u32[]{:S(2)}) async-start(f32[128,56,128]{2,1,0:T(8,128)} %bitcast.24), calls=%async_computation.1 | async-start | bytes 7340032 | tf_op jit(solution)/shard_map/all_to_all | solution.py:565
  103.3 0.0 copy-done.6
  103.3 0.6 multiply_add_fusion
  104.0 41.5 %queries.1 = (f32[4,2048,128]{2,1,0:T(8,128)}, f32[4,2048,128]{2,1,0:T(8,128)}, f32[4,2048,128]{2,1,0:T(8,128)}, f32[4,2048,128]{2,1,0:T(8,128)}, f32[1024,512]{1,0:T(8,128)}) custom-call(s32[2048]{0:T(1024)} %heads.3, s32[2048]{0:T(1024)} %get-tuple-element.58.rel_at, f32[4096,128]{1,0:T(8,128)} %get-tuple-element.25.tab4, ...), custom_call_target="tpu_custom_call" | custom-call | flops 35999997952 | bytes 62914560 | tf_op jit(solution)/shard_map/queries/pallas_call | solution.py:290
  145.5 1.2 all-to-all-done.1
  146.6 25.3 %tail_terms.1 = (f32[4,2048,128]{2,1,0:T(8,128)}, f32[4096,128]{1,0:T(8,128)}, f32[7168,128]{1,0:T(8,128)}) custom-call(s32[2048]{0:T(1024)} %tails.1, f32[4096,128]{1,0:T(8,128)} %get-tuple-element.25.tab4, f32[7168,128]{1,0:T(8,128)} %bitcast.5.fetched, f32[4,2048,128]{2,1,0:T(8,128)} %get-tuple-element.29.q_in), custom_call_target="tpu_custom_call" | custom-call | bytes 31457280 | tf_op jit(solution)/shard_map/tail_terms/pallas_call | solution.py:368
  171.9 9.5 %all-to-all-start.2 = ((f32[128,56,128]{2,1,0:T(8,128)}), f32[128,56,128]{2,1,0:T(8,128)}, u32[]{:S(2)}, u32[]{:S(2)}) async-start(f32[128,56,128]{2,1,0:T(8,128)} %bitcast.25), calls=%async_computation.2 | async-start | bytes 7340032 | tf_op jit(solution)/shard_map/all_to_all | solution.py:565
  181.4 28.8 %gradients.1 = (f32[13312,128]{1,0:T(8,128)}, f32[13312,128]{1,0:T(8,128)}, f32[4096,128]{1,0:T(8,128)}) custom-call(s32[2048]{0:T(1024)} %heads.3, s32[2048]{0:T(1024)} %get-tuple-element.59.grad_at, s32[1]{0:T(128)} %bitcast.1.core, f32[4096,128]{1,0:T(8,128)} %get-tuple-element.30.tail_local, f32[1024,512]{1,0:T(8,128)} %get-tuple-element.31.neg_acc, ...), custom_call_target="tpu_custom_call" | custom-call | bytes 1048576 | tf_op jit(solution)/shard_map/gradients/pallas_call | solution.py:450
  210.3 14.5 %all-to-all-done.2 = f32[128,56,128]{2,1,0:T(8,128)} async-done(((f32[128,56,128]{2,1,0:T(8,128)}), f32[128,56,128]{2,1,0:T(8,128)}, u32[]{:S(2)}, u32[]{:S(2)}) %all-to-all-start.2) | async-done | bytes 3670048 | tf_op jit(solution)/shard_map/all_to_all | solution.py:565
  224.7 0.0 collective-permute-start
  224.7 11.1 %collective-permute-done = f32[13312,128]{1,0:T(8,128)S(1)} collective-permute-done((f32[13312,128]{1,0:T(8,128)}, f32[13312,128]{1,0:T(8,128)S(1)}, u32[]{:S(2)}, u32[]{:S(2)}) %collective-permute-start) | collective-permute-done | bytes 6815776 | tf_op jit(solution)/shard_map/ppermute | solution.py:575
  235.9 5.2 %add.33 = f32[13312,128]{1,0:T(8,128)} add(f32[13312,128]{1,0:T(8,128)} %get-tuple-element.40, f32[13312,128]{1,0:T(8,128)S(1)} %collective-permute-done) | non-fusion elementwise | flops 1703936 | bytes 20447232 | tf_op jit(solution)/shard_map/add | solution.py:575
  241.1 0.0 copy-start.7
  241.1 0.0 copy-start.3
  241.1 0.0 copy-start.2
  241.1 0.0 copy-start.4
  241.1 9.7 %all-to-all-start.3 = ((f32[64,208,128]{2,1,0:T(8,128)}), f32[64,208,128]{2,1,0:T(8,128)}, u32[]{:S(2)}, u32[]{:S(2)}) async-start(f32[64,208,128]{2,1,0:T(8,128)} %bitcast.23), calls=%async_computation.3 | async-start | bytes 13631488 | tf_op jit(solution)/shard_map/all_to_all | solution.py:576
  250.8 0.0 copy-done.7
  250.8 0.0 copy-start.5
  250.9 0.0 copy-done.3
  250.9 0.0 copy-start.1
  250.9 1.6 copy-done.1
  252.5 11.8 %add_returned.1.local_grad = f32[4096,128]{1,0:T(8,128)S(1)} custom-call(s32[2048]{0:T(1024)S(1)} %copy-done.3, f32[7168,128]{1,0:T(8,128)} %bitcast.7.packed, f32[4096,128]{1,0:T(8,128)S(1)} %copy-done.1), custom_call_target="tpu_custom_call" | custom-call | bytes 10485760 | tf_op jit(solution)/shard_map/add_returned/pallas_call | solution.py:481
  264.2 83.5 %all-to-all-done.3.parts = f32[64,208,128]{2,1,0:T(8,128)} async-done(((f32[64,208,128]{2,1,0:T(8,128)}), f32[64,208,128]{2,1,0:T(8,128)}, u32[]{:S(2)}, u32[]{:S(2)}) %all-to-all-start.3) | async-done | bytes 6815776 | tf_op jit(solution)/shard_map/all_to_all | solution.py:576
  347.7 0.0 copy-done.2
  347.7 0.0 copy-done.4
  347.7 0.0 copy-done.5
  347.7 0.0 copy-start
  347.8 1.4 copy-done
  349.2 5.6 %adagrad_step.1 = (f32[400,1024]{1,0:T(8,128)}, f32[1,1024]{1,0:T(1,128)}, f32[400,128]{1,0:T(8,128)S(1)}, f32[1,128]{1,0:T(1,128)S(1)}) custom-call(s32[8]{0:T(128)S(1)} %copy-done.5, f32[4096,128]{1,0:T(8,128)S(1)} %add_returned.1.local_grad, f32[64,208,128]{2,1,0:T(8,128)} %all-to-all-done.3.parts, f32[400,1024]{1,0:T(8,128)S(1)} %bitcast.20, ...), custom_call_target="tpu_custom_call" | custom-call | bytes 16777216 | tf_op jit(solution)/shard_map/adagrad_step/pallas_call | solution.py:524
  354.8 0.8 copy.20
  355.5 0.5 slice_bitcast_fusion
  (1 shorter events, 0.0 us)
Async XLA Ops:
  7.2 87.0 %all-gather.2.cloned.1.call-start = ((), (), s32[]{:S(2)}) async-start(), calls=%async_computation.4 | async-start | bytes 17436672 | tf_op jit(solution)/shard_map/all_gather | solution.py:559
  40.2 63.1 %copy-start.6 = (s32[2048]{0:T(1024)S(1)}, s32[2048]{0:T(1024)}, u32[]{:S(2)}) copy-start(s32[2048]{0:T(1024)} %param.14) | copy-start | bytes 24580
  94.2 52.4 %all-to-all-start.1 = ((f32[128,56,128]{2,1,0:T(8,128)}), f32[128,56,128]{2,1,0:T(8,128)}, u32[]{:S(2)}, u32[]{:S(2)}) async-start(f32[128,56,128]{2,1,0:T(8,128)} %bitcast.24), calls=%async_computation.1 | async-start | bytes 7340032 | tf_op jit(solution)/shard_map/all_to_all | solution.py:565
  171.9 52.8 %all-to-all-start.2 = ((f32[128,56,128]{2,1,0:T(8,128)}), f32[128,56,128]{2,1,0:T(8,128)}, u32[]{:S(2)}, u32[]{:S(2)}) async-start(f32[128,56,128]{2,1,0:T(8,128)} %bitcast.25), calls=%async_computation.2 | async-start | bytes 7340032 | tf_op jit(solution)/shard_map/all_to_all | solution.py:565
  224.7 11.1 %collective-permute-start = (f32[13312,128]{1,0:T(8,128)}, f32[13312,128]{1,0:T(8,128)S(1)}, u32[]{:S(2)}, u32[]{:S(2)}) collective-permute-start(f32[13312,128]{1,0:T(8,128)} %get-tuple-element.41), channel_id=1, source_target_pairs={{0,1},{1,0},{2,3},{3,2},{4,5},{5,4},{6,7},{7,6},{8,9},{9,8},{10,11... | collective-permute-start | bytes 20447240 | tf_op jit(solution)/shard_map/ppermute | solution.py:575
  241.1 9.8 %copy-start.7 = (f32[58]{0:T(128)S(1)}, f32[58]{0:T(128)}, u32[]{:S(2)}) copy-start(f32[58]{0:T(128)} %param.12) | copy-start | bytes 700
  241.1 9.8 %copy-start.3 = (s32[2048]{0:T(1024)S(1)}, s32[2048]{0:T(1024)}, u32[]{:S(2)}) copy-start(s32[2048]{0:T(1024)} %reshape.43.asked) | copy-start | bytes 24580
  241.1 106.7 %copy-start.2 = (f32[400,128]{1,0:T(8,128)S(1)}, f32[400,128]{1,0:T(8,128)}, u32[]{:S(2)}) copy-start(f32[400,128]{1,0:T(8,128)} %pad_bitcast_fusion.rel_t) | copy-start | bytes 614404
  241.1 106.7 %copy-start.4 = (f32[1024]{0:T(1024)S(1)}, f32[1024]{0:T(1024)}, u32[]{:S(2)}) copy-start(f32[1024]{0:T(1024)} %param.10) | copy-start | bytes 12292
  241.1 106.6 %all-to-all-start.3 = ((f32[64,208,128]{2,1,0:T(8,128)}), f32[64,208,128]{2,1,0:T(8,128)}, u32[]{:S(2)}, u32[]{:S(2)}) async-start(f32[64,208,128]{2,1,0:T(8,128)} %bitcast.23), calls=%async_computation.3 | async-start | bytes 13631488 | tf_op jit(solution)/shard_map/all_to_all | solution.py:576
  250.8 96.9 %copy-start.5 = (s32[8]{0:T(128)S(1)}, s32[8]{0:T(128)}, u32[]{:S(2)}) copy-start(s32[8]{0:T(128)} %negatives.3) | copy-start | bytes 100
  250.9 1.6 copy-start.1
  347.7 1.4 copy-start
Sparse Core Ops, SparseCore 0:
  12.5 81.6 all-gather.1

commit v6 on v5

--- a/solution.py
+++ b/solution.py
@@ -26,6 +26,7 @@
 TILE = 256
 PACK16 = 56
 PACK66 = 208
+PIECES = 4
 UNROLL = 8
 
 f32 = jnp.float32
@@ -152,16 +153,16 @@
     dst[pl.ds(dst_base + 3 * rows, 8), :] = rem
 
 
-def unpack66(src, dst):
+def unpack66(src, src_base, dst, dst_base):
     rows = REL_DEV + NEG_DEV
     for k in range(9):
         n = 8 if k < 8 else 2
-        rem = src[pl.ds(3 * rows, 8), :] if k < 8 else src[pl.ds(3 * rows + 8, 2), :]
-        c1, c3 = part(src[pl.ds(2 * rows + 8 * k, n), :], rem, k % 8)
-        c0 = src[pl.ds(8 * k, n), :]
-        c2 = src[pl.ds(rows + 8 * k, n), :]
+        rem = src[pl.ds(src_base + 3 * rows + (0 if k < 8 else 8), n), :]
+        c1, c3 = part(src[pl.ds(src_base + 2 * rows + 8 * k, n), :], rem, k % 8)
+        c0 = src[pl.ds(src_base + 8 * k, n), :]
+        c2 = src[pl.ds(src_base + rows + 8 * k, n), :]
         for c, piece in enumerate((c0, c1, c2, c3)):
-            dst[pl.ds(32 * k + c, n, stride=CHUNKS), :] = piece
+            dst[pl.ds(dst_base + 32 * k + c, n, stride=CHUNKS), :] = piece
 
 
 def to_chunks(src, dst, n):
@@ -172,12 +173,12 @@
         dst[pl.ds(c, n, stride=CHUNKS), :] = piece.T
 
 
-def prep_kernel(negatives, table_t, rel_t, tab4, ag4, rel4):
+def prep_kernel(negatives, table_t, rel_t, tab4, send, rel4):
     to_chunks(table_t, tab4, ENT_DEV)
     to_chunks(rel_t, rel4, LANES)
-    ag4[0:REL4, :] = rel4[0:REL4, :]
     for i in range(NEG_DEV):
-        ag4[REL4 + CHUNKS * i : REL4 + CHUNKS * (i + 1), :] = tab4[row(negatives[i]), :]
+        rel4[REL4 + CHUNKS * i : REL4 + CHUNKS * (i + 1), :] = tab4[row(negatives[i]), :]
+    pack66(rel4, 0, send, 0)
 
 
 def prep(negatives, table_t, rel_t):
@@ -185,7 +186,7 @@
         prep_kernel,
         out_shape=(
             jax.ShapeDtypeStruct((ENT_DEV * CHUNKS, LANES), f32),
-            jax.ShapeDtypeStruct((PER, LANES), f32),
+            jax.ShapeDtypeStruct((PACK66, LANES), f32),
         ),
         in_specs=[SMEM, VMEM, VMEM],
         out_specs=(VMEM, VMEM),
@@ -227,21 +228,26 @@
 def query_kernel(
     heads, rel_at, tab4, shared,
     q_out, h_out, r_out, back_out, neg_acc,
-    tab, rel, n_hi, n_lo, t_hi, t_lo, hb, rb, sems,
+    tab, rel, packed, n_hi, n_lo, t_hi, t_lo, hb, rb, sems,
 ):
     step = pl.program_id(0)
 
     @pl.when(step == 0)
     def _():
-        loads = (
-            pltpu.make_async_copy(tab4, tab, sems.at[0]),
-            pltpu.make_async_copy(shared, rel, sems.at[1]),
-        )
+        size = N_DEV * PACK66 // PIECES
+        loads = [
+            pltpu.make_async_copy(shared.at[pl.ds(i * size, size)], packed.at[pl.ds(i * size, size)], sems.at[i])
+            for i in range(PIECES)
+        ]
+        loads.append(pltpu.make_async_copy(tab4, tab, sems.at[PIECES]))
         for load in loads:
             load.start()
         neg_acc[...] = jnp.zeros_like(neg_acc)
-        for load in loads:
-            load.wait()
+        each = N_DEV // PIECES
+        for i in range(PIECES):
+            loads[i].wait()
+            blocks_loop(each, 2, lambda d, i=i: unpack66(packed, (i * each + d) * PACK66, rel, (i * each + d) * PER))
+        loads[PIECES].wait()
 
         for c in range(CHUNKS):
             lanes = slice(c * LANES, (c + 1) * LANES)
@@ -296,13 +302,14 @@
         scratch_shapes=[
             pltpu.VMEM((ENT_DEV * CHUNKS, LANES), f32),
             pltpu.VMEM((N_DEV * PER, LANES), f32),
+            pltpu.VMEM((N_DEV * PACK66, LANES), f32),
             wide,
             wide,
             tall,
             tall,
             rows,
             rows,
-            pltpu.SemaphoreType.DMA((2,)),
+            pltpu.SemaphoreType.DMA((PIECES + 1,)),
         ],
         compiler_params=params(58),
         cost_estimate=cost(36_000_000_000, 60 << 20),
@@ -390,7 +397,7 @@
 
 def edge_kernel(
     heads, grad_at, core, tail_local, neg_acc, h_in, r_in, p_in, back_in,
-    mine, other, head_grad,
+    mine, other0, other1, other2, other3, head_grad,
     rel_grad, packed, hb, rb, sems,
 ):
     step = pl.program_id(0)
@@ -428,42 +435,78 @@
 
         lax.fori_loop(0, N_DEV, place, 0)
         side = core[0]
-        half = CHIPS * PACK66
-        stores = (
-            pltpu.make_async_copy(packed.at[pl.ds(0, half)], other, sems.at[0]),
-            pltpu.make_async_copy(packed.at[pl.ds(half, half)], mine, sems.at[1]),
-        )
-        for i, owner in enumerate((1 - side, side)):
-
-            def pack(d, i=i, owner=owner):
-                pack66(rel_grad, (owner * CHIPS + d) * PER, packed, (i * CHIPS + d) * PACK66)
-
-            blocks_loop(CHIPS, 2, pack)
+        size = CHIPS * PACK66 // PIECES
+        stores = [
+            pltpu.make_async_copy(packed.at[pl.ds(i * size, size)], other, sems.at[i])
+            for i, other in enumerate((other0, other1, other2, other3))
+        ]
+        stores.append(pltpu.make_async_copy(packed.at[pl.ds(PIECES * size, PIECES * size)], mine, sems.at[PIECES]))
+
+        def pack(d, owner, first):
+            pack66(rel_grad, (owner * CHIPS + d) * PER, packed, (first + d) * PACK66)
+
+        chips = CHIPS // PIECES
+        for i in range(PIECES):
+            blocks_loop(chips, 2, lambda d, i=i: pack(i * chips + d, 1 - side, 0))
             stores[i].start()
+        blocks_loop(CHIPS, 2, lambda d: pack(d, side, CHIPS))
+        stores[PIECES].start()
         for store in stores:
             store.wait()
 
 
 def gradients(heads, grad_at, core, tail_local, neg_acc, h, r, p, back):
     half = jax.ShapeDtypeStruct((CHIPS * PACK66, LANES), f32)
+    piece = jax.ShapeDtypeStruct((CHIPS * PACK66 // PIECES, LANES), f32)
     whole = pl.BlockSpec((ENT_DEV * CHUNKS, LANES), lambda i: (0, 0))
     return pl.pallas_call(
         edge_kernel,
         grid=(E_DEV // TILE,),
-        out_shape=(half, half, jax.ShapeDtypeStruct((ENT_DEV * CHUNKS, LANES), f32)),
+        out_shape=(half, piece, piece, piece, piece, jax.ShapeDtypeStruct((ENT_DEV * CHUNKS, LANES), f32)),
         in_specs=[SMEM, SMEM, SMEM, ANY, pl.BlockSpec((NEG, CHUNKS * LANES), lambda i: (0, 0)), BLOCK, BLOCK, BLOCK, BLOCK],
-        out_specs=(HBM, HBM, whole),
+        out_specs=(HBM,) * 5 + (whole,),
         scratch_shapes=[
             pltpu.VMEM((N_DEV * PER, LANES), f32),
             pltpu.VMEM((N_DEV * PACK66, LANES), f32),
             pltpu.VMEM((TILE * CHUNKS, LANES), f32),
             pltpu.VMEM((TILE * CHUNKS, LANES), f32),
-            pltpu.SemaphoreType.DMA((2,)),
+            pltpu.SemaphoreType.DMA((PIECES + 1,)),
         ],
         compiler_params=params(58),
         cost_estimate=cost(0, 1 << 20),
         name="gradients",
     )(heads, grad_at, core, tail_local, neg_acc, h, r, p, back)
+
+
+def merge_kernel(mine, got0, got1, got2, got3, out):
+    part = pl.program_id(0) // (MERGE_STEPS // PIECES)
+    for i, got in enumerate((got0, got1, got2, got3)):
+
+        @pl.when(part == i)
+        def _(got=got):
+            out[...] = mine[...] + got[...]
+
+
+MERGE_STEPS = 16
+
+
+def merge(mine, got):
+    size = CHIPS * PACK66 // MERGE_STEPS
+    each = MERGE_STEPS // PIECES
+    block = pl.BlockSpec((size, LANES), lambda s: (s, 0))
+    pieces = [
+        pl.BlockSpec((size, LANES), lambda s, i=i: (jnp.clip(s - i * each, 0, each - 1), 0)) for i in range(PIECES)
+    ]
+    return pl.pallas_call(
+        merge_kernel,
+        grid=(MERGE_STEPS,),
+        out_shape=jax.ShapeDtypeStruct((CHIPS * PACK66, LANES), f32),
+        in_specs=[block] + pieces,
+        out_specs=block,
+        compiler_params=params(58),
+        cost_estimate=cost(0, 1 << 16),
+        name="merge",
+    )(mine, *got)
 
 
 def returned_kernel(asked, packed, head_grad, out, returned):
@@ -509,7 +552,7 @@
     grad[...] = local_grad[...]
     share[...] = jnp.zeros_like(share)
     packed[...] = jnp.sum(parts[...], axis=0)
-    unpack66(packed, share)
+    unpack66(packed, 0, share, 0)
     for i in range(NEG_DEV):
         at = row(negatives[i])
         grad[at, :] = grad[at, :] + share[REL4 + CHUNKS * i : REL4 + CHUNKS * (i + 1), :]
@@ -555,8 +598,8 @@
     grad_at = ((owner % 2) * CHIPS + owner // 2) * (REL_DEV + NEG_DEV) + place
     core = lax.axis_index("c")
 
-    tab4, ag4 = prep(negatives, table_t, rel_t)
-    shared = lax.all_gather(ag4, AXES, axis=0, tiled=True)
+    tab4, send = prep(negatives, table_t, rel_t)
+    shared = lax.all_gather(send, AXES, axis=0, tiled=True)
     asked = lax.all_to_all(pull_lists, AXES, split_axis=0, concat_axis=0, tiled=True).reshape(SLOTS)
     rows_out, shared = lax.optimization_barrier((pull_rows(asked, tab4), shared))
 
@@ -568,11 +611,11 @@
     q, h, r, back, neg_acc = queries(heads, rel_at, tab4, shared)
     p, tail_local, outgoing = tail_terms(tails, tab4, fetched, q)
     returned = exchange(outgoing)
-    mine, other, head_grad = gradients(
+    mine, *others, head_grad = gradients(
         heads, grad_at, core.reshape(1), tail_local, neg_acc, h, r, p, back
     )
-    other, returned = lax.optimization_barrier((other, returned))
-    paired = mine + lax.ppermute(other, "c", [(0, 1), (1, 0)])
+    paired = merge(mine, [lax.ppermute(other, "c", [(0, 1), (1, 0)]) for other in others])
+    paired, returned = lax.optimization_barrier((paired, returned))
     parts = lax.all_to_all(
         paired.reshape(CHIPS, PACK66, LANES), AXES[:3], split_axis=0, concat_axis=0, tiled=True
     )

time: 366 us -> 360 us (0.984)
  waiting for transfers between devices: 164 us -> 146 us
  Pallas kernels: 126 us -> 142 us
  other arithmetic: 6.64 us -> 1.43 us
    all_to_all x2, waiting for transfers between devices: 15.7 us -> 0.01 us  [exchange(): lax.all_to_all(rows, AXES, split_axis=0, concat_axis=0, tiled=True)]
    pallas_call x1 -> x2, Pallas kernels: 28.8 us -> 41.8 us  [the longest x1 28.9 us: gradients(): pl.pallas_call(edge_kernel, grid=(E_DEV // TILE,), out_shape=(half, piece...]
    all_gather x1, waiting for transfers between devices: 54 us -> 48.4 us  [local(): shared = lax.all_gather(send, AXES, axis=0, tiled=True)]
    add x1 -> x0, other arithmetic: 5.21 us -> none  [local(): paired = mine + lax.ppermute(other, 'c', [(0, 1), (1, 0)])]
    ppermute x1 -> x4, waiting for transfers between devices: 11.1 us -> 10.1 us  [local(): lax.ppermute(other, 'c', [(0, 1), (1, 0)])]
  transfers between devices with their start and end apart: 5 -> 8, of which waited for: 5 -> 5; matrix products, arithmetic and copies ran while one was open for 1% -> 1% of each run, Pallas kernels for 25% -> 30%
where the time goes in v6:
time: 360 us; the launch traced here: 358 us
  waiting for transfers between devices  146 us (41%)
  Pallas kernels  142 us (39%)
  starting transfers between devices  31.5 us (9%)
  blocking collectives  15.3 us (4%)
  between operations  14.2 us (4%)
  local copies, waits for them, and re-layouts  8.55 us (2%)
    all_to_all x1, waiting for transfers between devices, local(): lax.all_to_all(paired.reshape(CHIPS, PACK66, LANES), AXES[:3], split_axis...  87.1 us
    all_gather x1, waiting for transfers between devices, local(): shared = lax.all_gather(send, AXES, axis=0, tiled=True)  48.4 us
    pallas_call x1, Pallas kernels, queries(): pl.pallas_call(query_kernel, grid=(E_DEV // TILE,), out_shape=(PLANE, PLA...  43.9 us
    pallas_call x1, Pallas kernels, gradients(): pl.pallas_call(edge_kernel, grid=(E_DEV // TILE,), out_shape=(half, piece...  28.9 us
    pallas_call x1, Pallas kernels, tail_terms(): pl.pallas_call(tail_kernel, grid=(E_DEV // TILE,), out_shape=(PLANE, jax....  25.3 us
    all_to_all x2, starting transfers between devices, exchange(): lax.all_to_all(rows, AXES, split_axis=0, concat_axis=0, tiled=True)  19.8 us
    all_to_all x1, blocking collectives, local(): lax.all_to_all(pull_lists, AXES, split_axis=0, concat_axis=0, tiled=True)  15.3 us
    pallas_call x1, Pallas kernels, merge(): pl.pallas_call(merge_kernel, grid=(MERGE_STEPS,), out_shape=jax.ShapeDtyp...  12.9 us
  transfers between devices with their start and end apart: 8, of which 5 were waited for; matrix products, arithmetic and copies ran while one was open for 1% of the time, Pallas kernels for 30%

profile of v6, /device:TPU:102, one launch (start us, length us, event | category | flops | bytes accessed | tf_op | source)
XLA Modules:
  0.0 358.3 jit_solution(13649290876961498315)
XLA Ops:
  7.2 0.0 copy-start.9
  7.2 0.0 all-gather.2.cloned.1.call-start
  7.2 1.0 copy.19
  8.3 0.7 pad_bitcast_fusion.rel_t
  9.0 3.5 prep.1
  12.4 0.0 all-gather.2.cloned.1.call-update
  12.4 0.0 copy-done.9
  12.5 0.1 copy.18
  12.6 15.3 %all_to_all.24 = s32[128,1,16]{2,1,0:T(1,128)S(1)} all-to-all(s32[128,1,16]{2,1,0:T(1,128)S(1)} %bitcast.26), channel_id=1, replica_groups=mesh['x'=4,'z'=4,'y'=4,'c'=2] {'x','z','y','c'}, dimensions={0} | all-to-all | bytes 16384 | tf_op jit(solution)/shard_map/all_to_all | solution.py:603
  27.9 0.5 broadcast.24
  28.4 0.8 reduce.3
  29.2 0.7 reshape.43.asked
  29.9 9.7 %pull_rows.1 = f32[7168,128]{1,0:T(8,128)} custom-call(s32[2048]{0:T(1024)} %reshape.43.asked, f32[4096,128]{1,0:T(8,128)} %get-tuple-element.28.tab4), custom_call_target="tpu_custom_call" | custom-call | bytes 8388608 | tf_op jit(solution)/shard_map/pull_rows/pallas_call | solution.py:212
  39.6 48.4 %all-gather.2.cloned.1.call-done.shared = f32[26624,128]{1,0:T(8,128)} async-done(((f32[208,128]{1,0:T(8,128)}), f32[26624,128]{1,0:T(8,128)}) %all-gather.2.cloned.1.call-update) | async-done | bytes 13631504 | tf_op jit(solution)/shard_map/all_gather | solution.py:602
  88.0 9.5 %all-to-all-start.1 = ((f32[128,56,128]{2,1,0:T(8,128)}), f32[128,56,128]{2,1,0:T(8,128)}, u32[]{:S(2)}, u32[]{:S(2)}) async-start(f32[128,56,128]{2,1,0:T(8,128)} %bitcast.24), calls=%async_computation.1 | async-start | bytes 7340032 | tf_op jit(solution)/shard_map/all_to_all | solution.py:608
  97.6 0.0 copy-done.10
  97.6 0.6 multiply_add_fusion
  98.2 43.9 %queries.1 = (f32[4,2048,128]{2,1,0:T(8,128)}, f32[4,2048,128]{2,1,0:T(8,128)}, f32[4,2048,128]{2,1,0:T(8,128)}, f32[4,2048,128]{2,1,0:T(8,128)}, f32[1024,512]{1,0:T(8,128)}) custom-call(s32[2048]{0:T(1024)} %heads.3, s32[2048]{0:T(1024)} %get-tuple-element.64.rel_at, f32[4096,128]{1,0:T(8,128)} %get-tuple-element.28.tab4, ...), custom_call_target="tpu_custom_call" | custom-call | flops 35999997952 | bytes 62914560 | tf_op jit(solution)/shard_map/queries/pallas_call | solution.py:296
  142.1 0.0 all-to-all-done.1
  142.1 25.3 %tail_terms.1 = (f32[4,2048,128]{2,1,0:T(8,128)}, f32[4096,128]{1,0:T(8,128)}, f32[7168,128]{1,0:T(8,128)}) custom-call(s32[2048]{0:T(1024)} %tails.1, f32[4096,128]{1,0:T(8,128)} %get-tuple-element.28.tab4, f32[7168,128]{1,0:T(8,128)} %bitcast.5.fetched, f32[4,2048,128]{2,1,0:T(8,128)} %get-tuple-element.32.q_in), custom_call_target="tpu_custom_call" | custom-call | bytes 31457280 | tf_op jit(solution)/shard_map/tail_terms/pallas_call | solution.py:375
  167.5 10.2 %all-to-all-start.2 = ((f32[128,56,128]{2,1,0:T(8,128)}), f32[128,56,128]{2,1,0:T(8,128)}, u32[]{:S(2)}, u32[]{:S(2)}) async-start(f32[128,56,128]{2,1,0:T(8,128)} %bitcast.25), calls=%async_computation.2 | async-start | bytes 7340032 | tf_op jit(solution)/shard_map/all_to_all | solution.py:608
  177.7 28.9 %gradients.1 = (f32[13312,128]{1,0:T(8,128)}, f32[3328,128]{1,0:T(8,128)}, f32[3328,128]{1,0:T(8,128)}, f32[3328,128]{1,0:T(8,128)}, f32[3328,128]{1,0:T(8,128)}, /*index=5*/f32[4096,128]{1,0:T(8,128)}) custom-call(s32[2048]{0:T(1024)} %heads.3, s32[2048]{0:T(1024)} %get-tuple-element.65.grad_at, s32[1]{0:T(128)} %bitcast.1.core, ...), custom_call_target="tpu_custom_call" | custom-call | bytes 1048576 | tf_op jit(solution)/shard_map/gradients/pallas_call | solution.py:462
  206.7 0.2 collective-permute-start
  206.9 0.4 collective-permute-start.1
  207.2 0.1 collective-permute-start.2
  207.4 0.4 collective-permute-start.3
  207.8 2.8 collective-permute-done.got0
  210.5 4.9 %collective-permute-done.1.got1 = f32[3328,128]{1,0:T(8,128)S(1)} collective-permute-done((f32[3328,128]{1,0:T(8,128)}, f32[3328,128]{1,0:T(8,128)S(1)}, u32[]{:S(2)}, u32[]{:S(2)}) %collective-permute-start.1) | collective-permute-done | bytes 1703968 | tf_op jit(solution)/shard_map/ppermute | solution.py:617
  215.4 2.4 collective-permute-done.2.got2
  217.9 0.0 collective-permute-done.3.got3
  217.9 0.0 copy-done.6
  217.9 0.0 copy-done.7
  217.9 1.2 copy-done.8
  219.1 12.9 %merge.1 = f32[13312,128]{1,0:T(8,128)} custom-call(f32[13312,128]{1,0:T(8,128)} %get-tuple-element.39.mine, f32[3328,128]{1,0:T(8,128)} %copy-done.6, f32[3328,128]{1,0:T(8,128)} %copy-done.7, f32[3328,128]{1,0:T(8,128)} %copy-done.8, f32[3328,128]{1,0:T(8,128)} %collective-permute-done.3.got3), custom_call_target="tpu_custom_call" | custom-call | bytes 65536 | tf_op jit(solution)/shard_map/merge/pallas_call | solution.py:500
  232.0 0.0 all-to-all-done.2
  232.0 0.0 copy-start.3
  232.0 10.6 %all-to-all-start.3 = ((f32[64,208,128]{2,1,0:T(8,128)}), f32[64,208,128]{2,1,0:T(8,128)}, u32[]{:S(2)}, u32[]{:S(2)}) async-start(f32[64,208,128]{2,1,0:T(8,128)} %bitcast.23), calls=%async_computation.3 | async-start | bytes 13631488 | tf_op jit(solution)/shard_map/all_to_all | solution.py:619
  242.6 0.0 copy-done.11
  242.6 0.0 copy-done.3
  242.7 0.0 copy-start.1
  242.7 1.6 copy-done.1
  244.3 11.8 %add_returned.1.local_grad = f32[4096,128]{1,0:T(8,128)S(1)} custom-call(s32[2048]{0:T(1024)S(1)} %copy-done.3, f32[7168,128]{1,0:T(8,128)} %bitcast.7.packed, f32[4096,128]{1,0:T(8,128)S(1)} %copy-done.1), custom_call_target="tpu_custom_call" | custom-call | bytes 10485760 | tf_op jit(solution)/shard_map/add_returned/pallas_call | solution.py:524
  256.1 87.1 %all-to-all-done.3.parts = f32[64,208,128]{2,1,0:T(8,128)} async-done(((f32[64,208,128]{2,1,0:T(8,128)}), f32[64,208,128]{2,1,0:T(8,128)}, u32[]{:S(2)}, u32[]{:S(2)}) %all-to-all-start.3) | async-done | bytes 6815776 | tf_op jit(solution)/shard_map/all_to_all | solution.py:619
  343.2 0.0 copy-start
  343.2 1.4 copy-done
  344.6 5.6 %adagrad_step.1 = (f32[400,1024]{1,0:T(8,128)}, f32[1,1024]{1,0:T(1,128)}, f32[400,128]{1,0:T(8,128)S(1)}, f32[1,128]{1,0:T(1,128)S(1)}) custom-call(s32[8]{0:T(128)S(1)} %copy-done.5, f32[4096,128]{1,0:T(8,128)S(1)} %add_returned.1.local_grad, f32[64,208,128]{2,1,0:T(8,128)} %all-to-all-done.3.parts, f32[400,1024]{1,0:T(8,128)S(1)} %bitcast.20, ...), custom_call_target="tpu_custom_call" | custom-call | bytes 16777216 | tf_op jit(solution)/shard_map/adagrad_step/pallas_call | solution.py:567
  350.2 0.8 copy.20
  351.0 0.5 slice_bitcast_fusion
  (12 shorter events, 0.0 us)
Async XLA Ops:
  7.2 5.3 %copy-start.9 = (s32[128,16]{0,1:T(8,128)S(1)}, s32[128,16]{0,1:T(8,128)}, u32[]{:S(2)}) copy-start(s32[128,16]{0,1:T(8,128)} %param.16) | copy-start | bytes 24580
  7.2 80.8 %all-gather.2.cloned.1.call-start = ((), (), s32[]{:S(2)}) async-start(), calls=%async_computation.4 | async-start | bytes 13737984 | tf_op jit(solution)/shard_map/all_gather | solution.py:602
  88.0 9.5 %copy-start.10 = (s32[2048]{0:T(1024)S(1)}, s32[2048]{0:T(1024)}, u32[]{:S(2)}) copy-start(s32[2048]{0:T(1024)} %param.14) | copy-start | bytes 24580
  88.0 54.1 %all-to-all-start.1 = ((f32[128,56,128]{2,1,0:T(8,128)}), f32[128,56,128]{2,1,0:T(8,128)}, u32[]{:S(2)}, u32[]{:S(2)}) async-start(f32[128,56,128]{2,1,0:T(8,128)} %bitcast.24), calls=%async_computation.1 | async-start | bytes 7340032 | tf_op jit(solution)/shard_map/all_to_all | solution.py:608
  167.5 64.5 %all-to-all-start.2 = ((f32[128,56,128]{2,1,0:T(8,128)}), f32[128,56,128]{2,1,0:T(8,128)}, u32[]{:S(2)}, u32[]{:S(2)}) async-start(f32[128,56,128]{2,1,0:T(8,128)} %bitcast.25), calls=%async_computation.2 | async-start | bytes 7340032 | tf_op jit(solution)/shard_map/all_to_all | solution.py:608
  206.7 3.9 %collective-permute-start = (f32[3328,128]{1,0:T(8,128)}, f32[3328,128]{1,0:T(8,128)S(1)}, u32[]{:S(2)}, u32[]{:S(2)}) collective-permute-start(f32[3328,128]{1,0:T(8,128)} %get-tuple-element.40), channel_id=1, source_target_pairs={{0,1},{1,0},{2,3},{3,2},{4,5},{5,4},{6,7},{7,6},{8,9},{9,8},{10,11... | collective-permute-start | bytes 5111816 | tf_op jit(solution)/shard_map/ppermute | solution.py:617
  206.9 8.5 %collective-permute-start.1 = (f32[3328,128]{1,0:T(8,128)}, f32[3328,128]{1,0:T(8,128)S(1)}, u32[]{:S(2)}, u32[]{:S(2)}) collective-permute-start(f32[3328,128]{1,0:T(8,128)} %get-tuple-element.41), channel_id=1, source_target_pairs={{0,1},{1,0},{2,3},{3,2},{4,5},{5,4},{6,7},{7,6},{8,9},{9,8},{10,11... | collective-permute-start | bytes 5111816 | tf_op jit(solution)/shard_map/ppermute | solution.py:617
  207.2 10.6 %collective-permute-start.2 = (f32[3328,128]{1,0:T(8,128)}, f32[3328,128]{1,0:T(8,128)S(1)}, u32[]{:S(2)}, u32[]{:S(2)}) collective-permute-start(f32[3328,128]{1,0:T(8,128)} %get-tuple-element.42), channel_id=1, source_target_pairs={{0,1},{1,0},{2,3},{3,2},{4,5},{5,4},{6,7},{7,6},{8,9},{9,8},{10,11... | collective-permute-start | bytes 5111816 | tf_op jit(solution)/shard_map/ppermute | solution.py:617
  207.4 10.5 %collective-permute-start.3 = (f32[3328,128]{1,0:T(8,128)}, f32[3328,128]{1,0:T(8,128)}, u32[]{:S(2)}, u32[]{:S(2)}) collective-permute-start(f32[3328,128]{1,0:T(8,128)} %get-tuple-element.43), channel_id=1, source_target_pairs={{0,1},{1,0},{2,3},{3,2},{4,5},{5,4},{6,7},{7,6},{8,9},{9,8},{10,11... | collective-permute-start | bytes 5111816 | tf_op jit(solution)/shard_map/ppermute | solution.py:617
  210.5 7.3 %copy-start.6 = (f32[3328,128]{1,0:T(8,128)}, f32[3328,128]{1,0:T(8,128)S(1)}, u32[]{:S(2)}) copy-start(f32[3328,128]{1,0:T(8,128)S(1)} %collective-permute-done.got0) | copy-start | bytes 5111812
  215.4 2.5 copy-start.7
  217.9 1.2 copy-start.8
  232.0 10.6 %copy-start.11 = (f32[58]{0:T(128)S(1)}, f32[58]{0:T(128)}, u32[]{:S(2)}) copy-start(f32[58]{0:T(128)} %param.12) | copy-start | bytes 700
  232.0 10.7 %copy-start.3 = (s32[2048]{0:T(1024)S(1)}, s32[2048]{0:T(1024)}, u32[]{:S(2)}) copy-start(s32[2048]{0:T(1024)} %reshape.43.asked) | copy-start | bytes 24580
  232.0 111.2 %all-to-all-start.3 = ((f32[64,208,128]{2,1,0:T(8,128)}), f32[64,208,128]{2,1,0:T(8,128)}, u32[]{:S(2)}, u32[]{:S(2)}) async-start(f32[64,208,128]{2,1,0:T(8,128)} %bitcast.23), calls=%async_computation.3 | async-start | bytes 13631488 | tf_op jit(solution)/shard_map/all_to_all | solution.py:619
  242.7 1.6 copy-start.1
  244.2 98.9 %copy-start.2 = (f32[400,128]{1,0:T(8,128)S(1)}, f32[400,128]{1,0:T(8,128)}, u32[]{:S(2)}) copy-start(f32[400,128]{1,0:T(8,128)} %pad_bitcast_fusion.rel_t) | copy-start | bytes 614404
  244.2 98.9 %copy-start.4 = (f32[1024]{0:T(1024)S(1)}, f32[1024]{0:T(1024)}, u32[]{:S(2)}) copy-start(f32[1024]{0:T(1024)} %param.10) | copy-start | bytes 12292
  244.3 98.9 %copy-start.5 = (s32[8]{0:T(128)S(1)}, s32[8]{0:T(128)}, u32[]{:S(2)}) copy-start(s32[8]{0:T(128)} %negatives.3) | copy-start | bytes 100
  343.2 1.4 copy-start
Sparse Core Ops, SparseCore 0:
  12.6 75.4 all-gather.1

commit v7 on v6

--- a/solution.py
+++ b/solution.py
@@ -27,6 +27,8 @@
 PACK16 = 56
 PACK66 = 208
 PIECES = 4
+KEPT = PACK66 // 2
+GROUPS = (0, 11, 22, 33, 44, 54, 64)
 UNROLL = 8
 
 f32 = jnp.float32
@@ -478,35 +480,122 @@
     )(heads, grad_at, core, tail_local, neg_acc, h, r, p, back)
 
 
-def merge_kernel(mine, got0, got1, got2, got3, out):
-    part = pl.program_id(0) // (MERGE_STEPS // PIECES)
+def merge_kernel(
+    color, mine, got0, got1, got2, got3,
+    keep, send0, send1, send2, send3, send4, send5,
+    total, came, sems, came_sems,
+):
+    each = CHIPS // PIECES
+    loads, arrivals = [], []
     for i, got in enumerate((got0, got1, got2, got3)):
-
-        @pl.when(part == i)
-        def _(got=got):
-            out[...] = mine[...] + got[...]
-
-
-MERGE_STEPS = 16
-
-
-def merge(mine, got):
-    size = CHIPS * PACK66 // MERGE_STEPS
-    each = MERGE_STEPS // PIECES
-    block = pl.BlockSpec((size, LANES), lambda s: (s, 0))
-    pieces = [
-        pl.BlockSpec((size, LANES), lambda s, i=i: (jnp.clip(s - i * each, 0, each - 1), 0)) for i in range(PIECES)
+        here = pl.ds(i * each, each)
+        loads.append(pltpu.make_async_copy(mine.at[here], total.at[here], sems.at[i]))
+        arrivals.append(pltpu.make_async_copy(got, came.at[here], came_sems.at[i]))
+        loads[i].start()
+        arrivals[i].start()
+    own = pl.ds(pl.multiple_of(color[0] * KEPT, 8), KEPT)
+    theirs = pl.ds(pl.multiple_of((1 - color[0]) * KEPT, 8), KEPT)
+    stores = [
+        pltpu.make_async_copy(total.at[pl.ds(first, last - first), theirs], send, sems.at[PIECES + i])
+        for i, (first, last, send) in enumerate(
+            zip(GROUPS[:-1], GROUPS[1:], (send0, send1, send2, send3, send4, send5), strict=True)
+        )
     ]
+    stores.append(pltpu.make_async_copy(total.at[:, own], keep, sems.at[PIECES + 6]))
+    started = 0
+    for i in range(PIECES):
+        loads[i].wait()
+        arrivals[i].wait()
+
+        def add(d, carry, i=i):
+            total[i * each + d] = total[i * each + d] + came[i * each + d]
+            return carry
+
+        lax.fori_loop(0, each, add, 0)
+        while started < 6 and GROUPS[started + 1] <= (i + 1) * each:
+            stores[started].start()
+            started += 1
+    stores[6].start()
+    for store in stores:
+        store.wait()
+
+
+def merge(color, mine, got):
+    def blocks(n, rows):
+        return jax.ShapeDtypeStruct((n, rows, LANES), f32)
+
     return pl.pallas_call(
         merge_kernel,
-        grid=(MERGE_STEPS,),
-        out_shape=jax.ShapeDtypeStruct((CHIPS * PACK66, LANES), f32),
-        in_specs=[block] + pieces,
-        out_specs=block,
+        out_shape=(blocks(CHIPS, KEPT),) + tuple(blocks(b - a, KEPT) for a, b in zip(GROUPS[:-1], GROUPS[1:], strict=True)),
+        in_specs=[SMEM, ANY] + [ANY] * PIECES,
+        out_specs=(HBM,) * 7,
+        scratch_shapes=[
+            pltpu.VMEM((CHIPS, PACK66, LANES), f32),
+            pltpu.VMEM((CHIPS, PACK66, LANES), f32),
+            pltpu.SemaphoreType.DMA((PIECES + 7,)),
+            pltpu.SemaphoreType.DMA((PIECES,)),
+        ],
         compiler_params=params(58),
         cost_estimate=cost(0, 1 << 16),
         name="merge",
-    )(mine, *got)
+    )(color, mine.reshape(CHIPS, PACK66, LANES), *[x.reshape(CHIPS // PIECES, PACK66, LANES) for x in got])
+
+
+def meet_kernel(keep, got0, got1, got2, got3, got4, got5, out, total, came, sems, came_sems):
+    spans = list(zip(GROUPS[:-1], GROUPS[1:], (got0, got1, got2, got3, got4, got5), strict=True))
+    loads, arrivals, stores = [], [], []
+    for i, (first, last, got) in enumerate(spans):
+        here = pl.ds(first, last - first)
+        loads.append(pltpu.make_async_copy(keep.at[here], total.at[here], sems.at[i]))
+        stores.append(pltpu.make_async_copy(total.at[here], out.at[here], sems.at[6 + i]))
+        arrivals.append(pltpu.make_async_copy(got, came.at[here], came_sems.at[i]))
+        loads[i].start()
+        arrivals[i].start()
+    for i, (first, last, _) in enumerate(spans):
+        loads[i].wait()
+        arrivals[i].wait()
+
+        def add(d, carry, first=first):
+            total[first + d] = total[first + d] + came[first + d]
+            return carry
+
+        lax.fori_loop(0, last - first, add, 0)
+        stores[i].start()
+    for store in stores:
+        store.wait()
+
+
+def meet(keep, got):
+    return pl.pallas_call(
+        meet_kernel,
+        out_shape=jax.ShapeDtypeStruct((CHIPS, KEPT, LANES), f32),
+        in_specs=[ANY] * 7,
+        out_specs=HBM,
+        scratch_shapes=[
+            pltpu.VMEM((CHIPS, KEPT, LANES), f32),
+            pltpu.VMEM((CHIPS, KEPT, LANES), f32),
+            pltpu.SemaphoreType.DMA((12,)),
+            pltpu.SemaphoreType.DMA((6,)),
+        ],
+        compiler_params=params(58),
+        cost_estimate=cost(0, 1 << 16),
+        name="meet",
+    )(keep, *got)
+
+
+def color_of(chip):
+    return (chip // 16 + chip // 4 + chip) % 2
+
+
+def matching(k):
+    pairs = []
+    for chip in range(CHIPS):
+        if color_of(chip) == 0:
+            at = [chip // 16, chip // 4 % 4, chip % 4]
+            at[k // 2] = (at[k // 2] + (1 if k % 2 == 0 else 3)) % 4
+            mate = (at[0] * 4 + at[1]) * 4 + at[2]
+            pairs += [(chip, mate), (mate, chip)]
+    return pairs
 
 
 def returned_kernel(asked, packed, head_grad, out, returned):
@@ -551,7 +640,12 @@
 ):
     grad[...] = local_grad[...]
     share[...] = jnp.zeros_like(share)
-    packed[...] = jnp.sum(parts[...], axis=0)
+    for half in range(2):
+        total = None
+        for chip in range(CHIPS):
+            if color_of(chip) == half:
+                total = parts[chip] if total is None else total + parts[chip]
+        packed[half * KEPT : (half + 1) * KEPT, :] = total
     unpack66(packed, 0, share, 0)
     for i in range(NEG_DEV):
         at = row(negatives[i])
@@ -614,11 +708,12 @@
     mine, *others, head_grad = gradients(
         heads, grad_at, core.reshape(1), tail_local, neg_acc, h, r, p, back
     )
-    paired = merge(mine, [lax.ppermute(other, "c", [(0, 1), (1, 0)]) for other in others])
-    paired, returned = lax.optimization_barrier((paired, returned))
-    parts = lax.all_to_all(
-        paired.reshape(CHIPS, PACK66, LANES), AXES[:3], split_axis=0, concat_axis=0, tiled=True
-    )
+    color = (lax.axis_index("x") + lax.axis_index("z") + lax.axis_index("y")) % 2
+    got = [lax.ppermute(other, "c", [(0, 1), (1, 0)]) for other in others]
+    merged = merge(color.reshape(1), mine, got)
+    (keep, *sends), returned = lax.optimization_barrier((merged, returned))
+    met = meet(keep, [lax.ppermute(send, AXES[:3], matching(k)) for k, send in enumerate(sends)])
+    parts = lax.all_to_all(met, AXES[:3], split_axis=0, concat_axis=0, tiled=True)
     local_grad = add_returned(asked, returned, head_grad)
     new_table_t, new_state, new_rel_t, new_rel_state = adagrad_step(
         negatives,

time: 360 us -> 334 us (0.928)
  waiting for transfers between devices: 146 us -> 110 us
  starting transfers between devices: 31.5 us -> 39.4 us
  local copies, waits for them, and re-layouts: 8.55 us -> 15 us
    all_to_all x1, waiting for transfers between devices: 87.1 us -> 30.1 us  [local(): lax.all_to_all(met, AXES[:3], split_axis=0, concat_axis=0, tiled=True)]
    ppermute x4 -> x10, waiting for transfers between devices: 10.1 us -> 31 us  [the longest x6 20.8 us: local(): lax.ppermute(send, AXES[:3], matching(k))]
    ppermute x4 -> x10, starting transfers between devices: 1.1 us -> 9.51 us  [the longest x6 8.41 us: local(): lax.ppermute(send, AXES[:3], matching(k))]
    unnamed x27 -> x43, local copies, waits for them, and re-layouts: 6.15 us -> 12.6 us
    pallas_call x1 -> x2, Pallas kernels: 12.9 us -> 12.6 us  [the longest x1 7.78 us: merge(): pl.pallas_call(merge_kernel, out_shape=(blocks(CHIPS, KEPT),) + tuple((bl...]
  transfers between devices with their start and end apart: 8 -> 14, of which waited for: 5 -> 8; matrix products, arithmetic and copies ran while one was open for 1% -> 1% of each run, Pallas kernels for 30% -> 31%
where the time goes in v7:
time: 334 us
  Pallas kernels  139 us (42%)
  waiting for transfers between devices  110 us (33%)
  starting transfers between devices  39.4 us (12%)
  blocking collectives  15.3 us (5%)
  local copies, waits for them, and re-layouts  15 us (4%)
  between operations  14.3 us (4%)
    all_gather x1, waiting for transfers between devices, local(): shared = lax.all_gather(send, AXES, axis=0, tiled=True)  48.4 us
    pallas_call x1, Pallas kernels, queries(): pl.pallas_call(query_kernel, grid=(E_DEV // TILE,), out_shape=(PLANE, PLA...  44 us
    all_to_all x1, waiting for transfers between devices, local(): lax.all_to_all(met, AXES[:3], split_axis=0, concat_axis=0, tiled=True)  30.1 us
    pallas_call x1, Pallas kernels, gradients(): pl.pallas_call(edge_kernel, grid=(E_DEV // TILE,), out_shape=(half, piece...  28.7 us
    pallas_call x1, Pallas kernels, tail_terms(): pl.pallas_call(tail_kernel, grid=(E_DEV // TILE,), out_shape=(PLANE, jax....  25.3 us
    ppermute x6, waiting for transfers between devices, local(): lax.ppermute(send, AXES[:3], matching(k))  20.8 us
    all_to_all x2, starting transfers between devices, exchange(): lax.all_to_all(rows, AXES, split_axis=0, concat_axis=0, tiled=True)  19.7 us
    all_to_all x1, blocking collectives, local(): lax.all_to_all(pull_lists, AXES, split_axis=0, concat_axis=0, tiled=True)  15.3 us
  transfers between devices with their start and end apart: 14, of which 8 were waited for; matrix products, arithmetic and copies ran while one was open for 1% of the time, Pallas kernels for 31%

profile of v7, /device:TPU:102, one launch (start us, length us, event | category | flops | bytes accessed | tf_op | source)
XLA Modules:
  0.0 333.6 jit_solution(17144644806974443698)
XLA Ops:
  7.2 1.0 copy.19
  8.3 0.7 pad_bitcast_fusion.rel_t
  9.0 3.4 %prep.1 = (f32[4096,128]{1,0:T(8,128)}, f32[208,128]{1,0:T(8,128)}) custom-call(s32[8]{0:T(128)} %negatives.3, f32[400,1024]{1,0:T(8,128)} %bitcast.24, f32[400,128]{1,0:T(8,128)} %pad_bitcast_fusion.rel_t), custom_call_target="tpu_custom_call" | custom-call | bytes 8388608 | tf_op jit(solution)/shard_map/prep/pallas_call | solution.py:187
  12.5 15.3 %all_to_all.24 = s32[128,1,16]{2,1,0:T(1,128)S(1)} all-to-all(s32[128,1,16]{2,1,0:T(1,128)S(1)} %bitcast.33), channel_id=1, replica_groups=mesh['x'=4,'z'=4,'y'=4,'c'=2] {'x','z','y','c'}, dimensions={0} | all-to-all | bytes 16384 | tf_op jit(solution)/shard_map/all_to_all | solution.py:697
  27.8 0.5 broadcast.25
  28.3 0.8 reduce.3
  29.2 0.7 reshape.58.asked
  29.8 9.7 %pull_rows.1 = f32[7168,128]{1,0:T(8,128)} custom-call(s32[2048]{0:T(1024)} %reshape.58.asked, f32[4096,128]{1,0:T(8,128)} %get-tuple-element.41.tab4), custom_call_target="tpu_custom_call" | custom-call | bytes 8388608 | tf_op jit(solution)/shard_map/pull_rows/pallas_call | solution.py:214
  39.6 48.4 %all-gather.2.cloned.1.call-done.shared = f32[26624,128]{1,0:T(8,128)} async-done(((f32[208,128]{1,0:T(8,128)}), f32[26624,128]{1,0:T(8,128)}) %all-gather.2.cloned.1.call-update) | async-done | bytes 13631504 | tf_op jit(solution)/shard_map/all_gather | solution.py:696
  88.0 9.5 %all-to-all-start.1 = ((f32[128,56,128]{2,1,0:T(8,128)}), f32[128,56,128]{2,1,0:T(8,128)}, u32[]{:S(2)}, u32[]{:S(2)}) async-start(f32[128,56,128]{2,1,0:T(8,128)} %bitcast.28), calls=%async_computation.1 | async-start | bytes 7340032 | tf_op jit(solution)/shard_map/all_to_all | solution.py:702
  97.5 0.6 multiply_add_fusion
  98.1 44.0 %queries.1 = (f32[4,2048,128]{2,1,0:T(8,128)}, f32[4,2048,128]{2,1,0:T(8,128)}, f32[4,2048,128]{2,1,0:T(8,128)}, f32[4,2048,128]{2,1,0:T(8,128)}, f32[1024,512]{1,0:T(8,128)}) custom-call(s32[2048]{0:T(1024)} %heads.3, s32[2048]{0:T(1024)} %get-tuple-element.90.rel_at, f32[4096,128]{1,0:T(8,128)} %get-tuple-element.41.tab4, ...), custom_call_target="tpu_custom_call" | custom-call | flops 35999997952 | bytes 62914560 | tf_op jit(solution)/shard_map/queries/pallas_call | solution.py:298
  142.2 25.3 %tail_terms.1 = (f32[4,2048,128]{2,1,0:T(8,128)}, f32[4096,128]{1,0:T(8,128)}, f32[7168,128]{1,0:T(8,128)}) custom-call(s32[2048]{0:T(1024)} %tails.1, f32[4096,128]{1,0:T(8,128)} %get-tuple-element.41.tab4, f32[7168,128]{1,0:T(8,128)} %bitcast.6.fetched, f32[4,2048,128]{2,1,0:T(8,128)} %get-tuple-element.45.q_in), custom_call_target="tpu_custom_call" | custom-call | bytes 31457280 | tf_op jit(solution)/shard_map/tail_terms/pallas_call | solution.py:377
  167.5 10.1 %all-to-all-start.2 = ((f32[128,56,128]{2,1,0:T(8,128)}), f32[128,56,128]{2,1,0:T(8,128)}, u32[]{:S(2)}, u32[]{:S(2)}) async-start(f32[128,56,128]{2,1,0:T(8,128)} %bitcast.30), calls=%async_computation.2 | async-start | bytes 7340032 | tf_op jit(solution)/shard_map/all_to_all | solution.py:702
  177.7 28.7 %gradients.1 = (f32[13312,128]{1,0:T(8,128)}, f32[3328,128]{1,0:T(8,128)}, f32[3328,128]{1,0:T(8,128)}, f32[3328,128]{1,0:T(8,128)}, f32[3328,128]{1,0:T(8,128)}, /*index=5*/f32[4096,128]{1,0:T(8,128)}) custom-call(s32[2048]{0:T(1024)} %heads.3, s32[2048]{0:T(1024)} %get-tuple-element.91.grad_at, s32[1]{0:T(128)} %bitcast.2.core, ...), custom_call_target="tpu_custom_call" | custom-call | bytes 1048576 | tf_op jit(solution)/shard_map/gradients/pallas_call | solution.py:464
  206.4 0.2 collective-permute-start.2
  206.6 0.4 collective-permute-start.3
  207.0 0.1 collective-permute-start
  207.2 0.4 collective-permute-start.1
  207.5 2.8 collective-permute-done.2
  210.3 4.9 %collective-permute-done.3 = f32[3328,128]{1,0:T(8,128)S(1)} collective-permute-done((f32[3328,128]{1,0:T(8,128)}, f32[3328,128]{1,0:T(8,128)S(1)}, u32[]{:S(2)}, u32[]{:S(2)}) %collective-permute-start.3) | collective-permute-done | bytes 1703968 | tf_op jit(solution)/shard_map/ppermute | solution.py:712
  215.3 2.4 collective-permute-done.1
  217.8 7.8 %merge.1 = (f32[64,104,128]{2,1,0:T(8,128)}, f32[11,104,128]{2,1,0:T(8,128)}, f32[11,104,128]{2,1,0:T(8,128)}, f32[11,104,128]{2,1,0:T(8,128)}, f32[11,104,128]{...) custom-call(s32[1]{0:T(128)} %bitcast.1.color, f32[64,208,128]{2,1,0:T(8,128)} %bitcast.29, ...), custom_call_target="tpu_custom_call" | custom-call | bytes 65536 | tf_op jit(solution)/shard_map/merge/pallas_call | solution.py:527
  225.6 1.6 collective-permute-start.8
  227.2 1.9 collective-permute-start.4
  229.0 0.3 collective-permute-start.5
  229.4 0.9 collective-permute-start.6
  230.3 0.8 collective-permute-start.7
  231.1 8.9 %collective-permute-done.8.got4 = f32[10,104,128]{2,1,0:T(8,128)S(1)} collective-permute-done((f32[10,104,128]{2,1,0:T(8,128)}, f32[10,104,128]{2,1,0:T(8,128)S(1)}, u32[]{:S(2)}, u32[]{:S(2)}) %collective-permute-start.8) | collective-permute-done | bytes 532512 | tf_op jit(solution)/shard_map/ppermute | solution.py:715
  240.0 2.9 collective-permute-start.9
  242.9 11.9 %collective-permute-done.9.got5 = f32[10,104,128]{2,1,0:T(8,128)S(1)} collective-permute-done((f32[10,104,128]{2,1,0:T(8,128)}, f32[10,104,128]{2,1,0:T(8,128)S(1)}, u32[]{:S(2)}, u32[]{:S(2)}) %collective-permute-start.9) | collective-permute-done | bytes 532512 | tf_op jit(solution)/shard_map/ppermute | solution.py:715
  254.8 0.8 copy-done.16
  255.7 0.2 copy-done.12
  255.9 0.2 copy-done.13
  256.1 0.8 copy-done.14
  256.9 4.8 %meet.1 = f32[64,104,128]{2,1,0:T(8,128)} custom-call(f32[64,104,128]{2,1,0:T(8,128)} %get-tuple-element.67.keep, f32[11,104,128]{2,1,0:T(8,128)} %copy-done.11, f32[11,104,128]{2,1,0:T(8,128)} %copy-done.12, f32[11,104,128]{2,1,0:T(8,128)} %copy-done.13, f32[11,104,128]{2,1,0:T(8,128)} %copy-done.14, f32[10,104,128]{2,1,0:T(8,128)} %copy-done.15, ...), custom_call_target="tpu_custom_call" | custom-call | bytes 65536 | tf_op jit(solution)/shard_map/meet/pallas_call | solution.py:569
  261.8 10.2 %all-to-all-start.3 = ((f32[64,104,128]{2,1,0:T(8,128)}), f32[64,104,128]{2,1,0:T(8,128)S(1)}, u32[]{:S(2)}, u32[]{:S(2)}) async-start(f32[64,104,128]{2,1,0:T(8,128)} %meet.1), calls=%async_computation.3 | async-start | bytes 6815744 | tf_op jit(solution)/shard_map/all_to_all | solution.py:716
  272.0 1.6 copy-done.3
  273.6 11.8 %add_returned.1.local_grad = f32[4096,128]{1,0:T(8,128)S(1)} custom-call(s32[2048]{0:T(1024)S(1)} %copy-done.6, f32[7168,128]{1,0:T(8,128)} %bitcast.13.packed, f32[4096,128]{1,0:T(8,128)S(1)} %copy-done.3), custom_call_target="tpu_custom_call" | custom-call | bytes 10485760 | tf_op jit(solution)/shard_map/add_returned/pallas_call | solution.py:613
  285.4 1.3 copy-done
  286.8 30.1 %all-to-all-done.3.parts = f32[64,104,128]{2,1,0:T(8,128)S(1)} async-done(((f32[64,104,128]{2,1,0:T(8,128)}), f32[64,104,128]{2,1,0:T(8,128)S(1)}, u32[]{:S(2)}, u32[]{:S(2)}) %all-to-all-start.3) | async-done | bytes 3407904 | tf_op jit(solution)/shard_map/all_to_all | solution.py:716
  316.9 1.6 copy-done.1
  318.5 1.4 copy-done.2
  319.9 0.9 copy-done.4
  320.8 3.0 adagrad_step.1
  323.9 0.7 copy-done.5
  324.5 1.7 copy.20
  326.3 0.5 slice_bitcast_fusion
  (41 shorter events, 0.5 us)
Async XLA Ops:
  7.2 5.2 %copy-start.17 = (s32[128,16]{0,1:T(8,128)S(1)}, s32[128,16]{0,1:T(8,128)}, u32[]{:S(2)}) copy-start(s32[128,16]{0,1:T(8,128)} %param.16) | copy-start | bytes 24580
  7.2 80.8 %all-gather.2.cloned.1.call-start = ((), (), s32[]{:S(2)}) async-start(), calls=%async_computation.4 | async-start | bytes 13737984 | tf_op jit(solution)/shard_map/all_gather | solution.py:696
  88.0 9.5 %copy-start.18 = (s32[2048]{0:T(1024)S(1)}, s32[2048]{0:T(1024)}, u32[]{:S(2)}) copy-start(s32[2048]{0:T(1024)} %param.14) | copy-start | bytes 24580
  88.0 54.2 %all-to-all-start.1 = ((f32[128,56,128]{2,1,0:T(8,128)}), f32[128,56,128]{2,1,0:T(8,128)}, u32[]{:S(2)}, u32[]{:S(2)}) async-start(f32[128,56,128]{2,1,0:T(8,128)} %bitcast.28), calls=%async_computation.1 | async-start | bytes 7340032 | tf_op jit(solution)/shard_map/all_to_all | solution.py:702
  167.5 58.0 %all-to-all-start.2 = ((f32[128,56,128]{2,1,0:T(8,128)}), f32[128,56,128]{2,1,0:T(8,128)}, u32[]{:S(2)}, u32[]{:S(2)}) async-start(f32[128,56,128]{2,1,0:T(8,128)} %bitcast.30), calls=%async_computation.2 | async-start | bytes 7340032 | tf_op jit(solution)/shard_map/all_to_all | solution.py:702
  206.4 3.9 %collective-permute-start.2 = (f32[3328,128]{1,0:T(8,128)}, f32[3328,128]{1,0:T(8,128)S(1)}, u32[]{:S(2)}, u32[]{:S(2)}) collective-permute-start(f32[3328,128]{1,0:T(8,128)} %get-tuple-element.55), channel_id=1, source_target_pairs={{0,1},{1,0},{2,3},{3,2},{4,5},{5,4},{6,7},{7,6},{8,9},{9,8},{10,11... | collective-permute-start | bytes 5111816 | tf_op jit(solution)/shard_map/ppermute | solution.py:712
  206.6 8.5 %collective-permute-start.3 = (f32[3328,128]{1,0:T(8,128)}, f32[3328,128]{1,0:T(8,128)S(1)}, u32[]{:S(2)}, u32[]{:S(2)}) collective-permute-start(f32[3328,128]{1,0:T(8,128)} %get-tuple-element.56), channel_id=1, source_target_pairs={{0,1},{1,0},{2,3},{3,2},{4,5},{5,4},{6,7},{7,6},{8,9},{9,8},{10,11... | collective-permute-start | bytes 5111816 | tf_op jit(solution)/shard_map/ppermute | solution.py:712
  207.0 8.3 %collective-permute-start = (f32[3328,128]{1,0:T(8,128)}, f32[3328,128]{1,0:T(8,128)}, u32[]{:S(2)}, u32[]{:S(2)}) collective-permute-start(f32[3328,128]{1,0:T(8,128)} %get-tuple-element.53), channel_id=1, source_target_pairs={{0,1},{1,0},{2,3},{3,2},{4,5},{5,4},{6,7},{7,6},{8,9},{9,8},{10,11... | collective-permute-start | bytes 5111816 | tf_op jit(solution)/shard_map/ppermute | solution.py:712
  207.2 10.6 %collective-permute-start.1 = (f32[3328,128]{1,0:T(8,128)}, f32[3328,128]{1,0:T(8,128)}, u32[]{:S(2)}, u32[]{:S(2)}) collective-permute-start(f32[3328,128]{1,0:T(8,128)} %get-tuple-element.54), channel_id=1, source_target_pairs={{0,1},{1,0},{2,3},{3,2},{4,5},{5,4},{6,7},{7,6},{8,9},{9,8},{10,11... | collective-permute-start | bytes 5111816 | tf_op jit(solution)/shard_map/ppermute | solution.py:712
  210.3 7.4 %copy-start.9 = (f32[3328,128]{1,0:T(8,128)}, f32[3328,128]{1,0:T(8,128)S(1)}, u32[]{:S(2)}) copy-start(f32[3328,128]{1,0:T(8,128)S(1)} %collective-permute-done.2) | copy-start | bytes 5111812
  215.2 2.6 copy-start.10
  225.6 14.4 %collective-permute-start.8 = (f32[10,104,128]{2,1,0:T(8,128)}, f32[10,104,128]{2,1,0:T(8,128)S(1)}, u32[]{:S(2)}, u32[]{:S(2)}) collective-permute-start(f32[10,104,128]{2,1,0:T(8,128)} %get-tuple-element.72), channel_id=1, source_target_pairs={{0,2},{2,0},{4,6},{6,4},{10,12},{12,10},{14,8},{8,14},{16,18},{18,... | collective-permute-start | bytes 1597448 | tf_op jit(solution)/shard_map/ppermute | solution.py:715
  227.2 27.6 %collective-permute-start.4 = (f32[11,104,128]{2,1,0:T(8,128)}, f32[11,104,128]{2,1,0:T(8,128)S(1)}, u32[]{:S(2)}, u32[]{:S(2)}) collective-permute-start(f32[11,104,128]{2,1,0:T(8,128)} %get-tuple-element.68), channel_id=1, source_target_pairs={{0,32},{32,0},{4,36},{36,4},{10,42},{42,10},{14,46},{46,14},{16,48... | collective-permute-start | bytes 1757192 | tf_op jit(solution)/shard_map/ppermute | solution.py:715
  229.0 25.7 %collective-permute-start.5 = (f32[11,104,128]{2,1,0:T(8,128)}, f32[11,104,128]{2,1,0:T(8,128)S(1)}, u32[]{:S(2)}, u32[]{:S(2)}) collective-permute-start(f32[11,104,128]{2,1,0:T(8,128)} %get-tuple-element.69), channel_id=1, source_target_pairs={{0,96},{96,0},{4,100},{100,4},{10,106},{106,10},{14,110},{110,14},... | collective-permute-start | bytes 1757192 | tf_op jit(solution)/shard_map/ppermute | solution.py:715
  229.4 25.4 %collective-permute-start.6 = (f32[11,104,128]{2,1,0:T(8,128)}, f32[11,104,128]{2,1,0:T(8,128)S(1)}, u32[]{:S(2)}, u32[]{:S(2)}) collective-permute-start(f32[11,104,128]{2,1,0:T(8,128)} %get-tuple-element.70), channel_id=1, source_target_pairs={{0,8},{8,0},{4,12},{12,4},{10,18},{18,10},{14,22},{22,14},{16,24},... | collective-permute-start | bytes 1757192 | tf_op jit(solution)/shard_map/ppermute | solution.py:715
  230.3 24.5 %collective-permute-start.7 = (f32[11,104,128]{2,1,0:T(8,128)}, f32[11,104,128]{2,1,0:T(8,128)S(1)}, u32[]{:S(2)}, u32[]{:S(2)}) collective-permute-start(f32[11,104,128]{2,1,0:T(8,128)} %get-tuple-element.71), channel_id=1, source_target_pairs={{0,24},{24,0},{4,28},{28,4},{10,2},{2,10},{14,6},{6,14},{16,8},{8,... | collective-permute-start | bytes 1757192 | tf_op jit(solution)/shard_map/ppermute | solution.py:715
  240.0 14.8 %copy-start.15 = (f32[10,104,128]{2,1,0:T(8,128)}, f32[10,104,128]{2,1,0:T(8,128)S(1)}, u32[]{:S(2)}) copy-start(f32[10,104,128]{2,1,0:T(8,128)S(1)} %collective-permute-done.8.got4) | copy-start | bytes 1597444
  240.0 14.7 %collective-permute-start.9 = (f32[10,104,128]{2,1,0:T(8,128)}, f32[10,104,128]{2,1,0:T(8,128)S(1)}, u32[]{:S(2)}, u32[]{:S(2)}) collective-permute-start(f32[10,104,128]{2,1,0:T(8,128)} %get-tuple-element.73), channel_id=1, source_target_pairs={{0,6},{6,0},{4,2},{2,4},{10,8},{8,10},{14,12},{12,14},{16,22},{22,... | collective-permute-start | bytes 1597448 | tf_op jit(solution)/shard_map/ppermute | solution.py:715
  254.7 0.9 copy-start.16
  254.8 1.0 copy-start.11
  254.8 1.2 copy-start.12
  254.8 1.3 copy-start.13
  256.1 0.8 copy-start.14
  261.7 10.3 %copy-start.19 = (f32[58]{0:T(128)S(1)}, f32[58]{0:T(128)}, u32[]{:S(2)}) copy-start(f32[58]{0:T(128)} %param.12) | copy-start | bytes 700
  261.8 10.3 %copy-start.6 = (s32[2048]{0:T(1024)S(1)}, s32[2048]{0:T(1024)}, u32[]{:S(2)}) copy-start(s32[2048]{0:T(1024)} %reshape.58.asked) | copy-start | bytes 24580
  261.8 55.1 %all-to-all-start.3 = ((f32[64,104,128]{2,1,0:T(8,128)}), f32[64,104,128]{2,1,0:T(8,128)S(1)}, u32[]{:S(2)}, u32[]{:S(2)}) async-start(f32[64,104,128]{2,1,0:T(8,128)} %meet.1), calls=%async_computation.3 | async-start | bytes 6815744 | tf_op jit(solution)/shard_map/all_to_all | solution.py:716
  272.0 1.6 copy-start.3
  273.6 43.3 %copy-start.7 = (f32[1024]{0:T(1024)S(1)}, f32[1024]{0:T(1024)}, u32[]{:S(2)}) copy-start(f32[1024]{0:T(1024)} %param.10) | copy-start | bytes 12292
  273.6 43.3 %copy-start.8 = (s32[8]{0:T(128)S(1)}, s32[8]{0:T(128)}, u32[]{:S(2)}) copy-start(s32[8]{0:T(128)} %negatives.3) | copy-start | bytes 100
  285.4 1.4 copy-start
  316.9 1.6 copy-start.1
  318.5 1.4 copy-start.2
  319.9 0.9 copy-start.4
  323.9 0.7 copy-start.5
Sparse Core Ops, SparseCore 0:
  12.5 75.4 all-gather.1

commit v8 on v7

--- a/solution.py
+++ b/solution.py
@@ -28,7 +28,8 @@
 PACK66 = 208
 PIECES = 4
 KEPT = PACK66 // 2
-GROUPS = (0, 11, 22, 33, 44, 54, 64)
+GROUPS = (0, 13, 26, 39, 52, 64)
+WAYS = len(GROUPS) - 1
 UNROLL = 8
 
 f32 = jnp.float32
@@ -326,70 +327,88 @@
 ):
     step = pl.program_id(0)
     local = ENT_DEV * CHUNKS
+    size = N_DEV * PACK16 // PIECES
+    each = N_DEV // PIECES
 
     @pl.when(step == 0)
     def _():
-        loads = (
-            pltpu.make_async_copy(fetched, packed, sems.at[1]),
-            pltpu.make_async_copy(tab4, ext.at[pl.ds(0, local)], sems.at[0]),
-        )
+        loads = []
+        for i in range(PIECES):
+            here = pl.ds(i * size, size)
+            loads.append(pltpu.make_async_copy(fetched.at[here], packed.at[here], sems.at[i]))
+        loads.append(pltpu.make_async_copy(tab4, ext.at[pl.ds(0, local)], sems.at[PIECES]))
         for load in loads:
             load.start()
         ext_grad[...] = jnp.zeros_like(ext_grad)
-        for load in loads:
-            load.wait()
-        unpack_slots(packed, ext, local)
-
-    base = step * TILE
+        for i in range(PIECES):
+            loads[i].wait()
+
+            def unpack(d, i=i):
+                unpack16(packed, (i * each + d) * PACK16, ext, local + (i * each + d) * CAP * CHUNKS)
+
+            blocks_loop(each, 4, unpack)
+        loads[PIECES].wait()
+
+    base = step * TAIL_TILE
 
     def gather(i):
         tb[row(i), :] = ext[row(tails[base + i]), :]
 
-    rows_loop(TILE, gather)
-    t = [chunk_of(tb, c, TILE) for c in range(CHUNKS)]
+    rows_loop(TAIL_TILE, gather)
+    t = [chunk_of(tb, c, TAIL_TILE) for c in range(CHUNKS)]
     q = [q_in[c] for c in range(CHUNKS)]
     score = (q[0] * t[0] + q[1] * t[1]) + (q[2] * t[2] + q[3] * t[3])
     pos_grad = jax.nn.sigmoid(jnp.sum(score, axis=1, keepdims=True)) - 1.0
     for c in range(CHUNKS):
         p_out[c] = pos_grad * t[c]
-        tb[pl.ds(c, TILE, stride=CHUNKS), :] = pos_grad * q[c]
+        tb[pl.ds(c, TAIL_TILE, stride=CHUNKS), :] = pos_grad * q[c]
 
     def scatter(i):
         at = row(tails[base + i])
         ext_grad[at, :] = ext_grad[at, :] + tb[row(i), :]
 
-    rows_loop(TILE, scatter)
-
-    @pl.when(step == E_DEV // TILE - 1)
+    rows_loop(TAIL_TILE, scatter)
+
+    @pl.when(step == E_DEV // TAIL_TILE - 1)
     def _():
-        stores = (
-            pltpu.make_async_copy(ext_grad.at[pl.ds(0, local)], tail_local, sems.at[0]),
-            pltpu.make_async_copy(packed, outgoing, sems.at[1]),
-        )
-        stores[0].start()
-        pack_slots(ext_grad, local, packed)
-        stores[1].start()
+        stores = []
+        for i in range(PIECES):
+            here = pl.ds(i * size, size)
+            stores.append(pltpu.make_async_copy(packed.at[here], outgoing.at[here], sems.at[i]))
+        stores.append(pltpu.make_async_copy(ext_grad.at[pl.ds(0, local)], tail_local, sems.at[PIECES]))
+        stores[PIECES].start()
+        for i in range(PIECES):
+
+            def pack(d, i=i):
+                pack16(ext_grad, local + (i * each + d) * CAP * CHUNKS, packed, (i * each + d) * PACK16)
+
+            blocks_loop(each, 4, pack)
+            stores[i].start()
         for store in stores:
             store.wait()
 
 
+TAIL_TILE = 512
+
+
 def tail_terms(tails, tab4, fetched, q):
+    block = pl.BlockSpec((CHUNKS, TAIL_TILE, LANES), lambda i: (0, i, 0))
     return pl.pallas_call(
         tail_kernel,
-        grid=(E_DEV // TILE,),
+        grid=(E_DEV // TAIL_TILE,),
         out_shape=(
             PLANE,
             jax.ShapeDtypeStruct((ENT_DEV * CHUNKS, LANES), f32),
             jax.ShapeDtypeStruct((N_DEV * PACK16, LANES), f32),
         ),
-        in_specs=[SMEM, ANY, ANY, BLOCK],
-        out_specs=(BLOCK, HBM, HBM),
+        in_specs=[SMEM, ANY, ANY, block],
+        out_specs=(block, HBM, HBM),
         scratch_shapes=[
             pltpu.VMEM(((ENT_DEV + SLOTS) * CHUNKS, LANES), f32),
             pltpu.VMEM(((ENT_DEV + SLOTS) * CHUNKS, LANES), f32),
             pltpu.VMEM((N_DEV * PACK16, LANES), f32),
-            pltpu.VMEM((TILE * CHUNKS, LANES), f32),
-            pltpu.SemaphoreType.DMA((2,)),
+            pltpu.VMEM((TAIL_TILE * CHUNKS, LANES), f32),
+            pltpu.SemaphoreType.DMA((PIECES + 1,)),
         ],
         compiler_params=params(58),
         cost_estimate=cost(0, 30 << 20),
@@ -482,7 +501,7 @@
 
 def merge_kernel(
     color, mine, got0, got1, got2, got3,
-    keep, send0, send1, send2, send3, send4, send5,
+    keep, send0, send1, send2, send3, send4,
     total, came, sems, came_sems,
 ):
     each = CHIPS // PIECES
@@ -498,10 +517,10 @@
     stores = [
         pltpu.make_async_copy(total.at[pl.ds(first, last - first), theirs], send, sems.at[PIECES + i])
         for i, (first, last, send) in enumerate(
-            zip(GROUPS[:-1], GROUPS[1:], (send0, send1, send2, send3, send4, send5), strict=True)
+            zip(GROUPS[:-1], GROUPS[1:], (send0, send1, send2, send3, send4), strict=True)
         )
     ]
-    stores.append(pltpu.make_async_copy(total.at[:, own], keep, sems.at[PIECES + 6]))
+    stores.append(pltpu.make_async_copy(total.at[:, own], keep, sems.at[PIECES + WAYS]))
     started = 0
     for i in range(PIECES):
         loads[i].wait()
@@ -512,10 +531,10 @@
             return carry
 
         lax.fori_loop(0, each, add, 0)
-        while started < 6 and GROUPS[started + 1] <= (i + 1) * each:
+        while started < WAYS and GROUPS[started + 1] <= (i + 1) * each:
             stores[started].start()
             started += 1
-    stores[6].start()
+    stores[WAYS].start()
     for store in stores:
         store.wait()
 
@@ -528,11 +547,11 @@
         merge_kernel,
         out_shape=(blocks(CHIPS, KEPT),) + tuple(blocks(b - a, KEPT) for a, b in zip(GROUPS[:-1], GROUPS[1:], strict=True)),
         in_specs=[SMEM, ANY] + [ANY] * PIECES,
-        out_specs=(HBM,) * 7,
+        out_specs=(HBM,) * (WAYS + 1),
         scratch_shapes=[
             pltpu.VMEM((CHIPS, PACK66, LANES), f32),
             pltpu.VMEM((CHIPS, PACK66, LANES), f32),
-            pltpu.SemaphoreType.DMA((PIECES + 7,)),
+            pltpu.SemaphoreType.DMA((PIECES + WAYS + 1,)),
             pltpu.SemaphoreType.DMA((PIECES,)),
         ],
         compiler_params=params(58),
@@ -541,22 +560,19 @@
     )(color, mine.reshape(CHIPS, PACK66, LANES), *[x.reshape(CHIPS // PIECES, PACK66, LANES) for x in got])
 
 
-def meet_kernel(keep, got0, got1, got2, got3, got4, got5, out, total, came, sems, came_sems):
-    spans = list(zip(GROUPS[:-1], GROUPS[1:], (got0, got1, got2, got3, got4, got5), strict=True))
-    loads, arrivals, stores = [], [], []
-    for i, (first, last, got) in enumerate(spans):
+def meet_kernel(keep, got0, got1, got2, got3, got4, out, total, sems):
+    spans = list(zip(GROUPS[:-1], GROUPS[1:], (got0, got1, got2, got3, got4), strict=True))
+    loads, stores = [], []
+    for i, (first, last, _) in enumerate(spans):
         here = pl.ds(first, last - first)
         loads.append(pltpu.make_async_copy(keep.at[here], total.at[here], sems.at[i]))
-        stores.append(pltpu.make_async_copy(total.at[here], out.at[here], sems.at[6 + i]))
-        arrivals.append(pltpu.make_async_copy(got, came.at[here], came_sems.at[i]))
+        stores.append(pltpu.make_async_copy(total.at[here], out.at[here], sems.at[WAYS + i]))
         loads[i].start()
-        arrivals[i].start()
-    for i, (first, last, _) in enumerate(spans):
+    for i, (first, last, got) in enumerate(spans):
         loads[i].wait()
-        arrivals[i].wait()
-
-        def add(d, carry, first=first):
-            total[first + d] = total[first + d] + came[first + d]
+
+        def add(d, carry, first=first, got=got):
+            total[first + d] = total[first + d] + got[d]
             return carry
 
         lax.fori_loop(0, last - first, add, 0)
@@ -569,15 +585,10 @@
     return pl.pallas_call(
         meet_kernel,
         out_shape=jax.ShapeDtypeStruct((CHIPS, KEPT, LANES), f32),
-        in_specs=[ANY] * 7,
+        in_specs=[ANY] + [VMEM] * WAYS,
         out_specs=HBM,
-        scratch_shapes=[
-            pltpu.VMEM((CHIPS, KEPT, LANES), f32),
-            pltpu.VMEM((CHIPS, KEPT, LANES), f32),
-            pltpu.SemaphoreType.DMA((12,)),
-            pltpu.SemaphoreType.DMA((6,)),
-        ],
-        compiler_params=params(58),
+        scratch_shapes=[pltpu.VMEM((CHIPS, KEPT, LANES), f32), pltpu.SemaphoreType.DMA((2 * WAYS,))],
+        compiler_params=params(16),
         cost_estimate=cost(0, 1 << 16),
         name="meet",
     )(keep, *got)
@@ -634,24 +645,36 @@
 
 
 def step_kernel(
-    negatives, local_grad, parts, table_t, state, rel_t, rel_state,
+    negatives, local_grad, parts, table_now, state, rel_t, rel_state,
     new_table_t, new_state, new_rel_t, new_rel_state,
-    grad, share, packed,
+    grad, came, table_t, share, packed, sems,
 ):
-    grad[...] = local_grad[...]
+    each = CHIPS // PIECES
+    loads = []
+    for i in range(PIECES):
+        here = pl.ds(i * each, each)
+        loads.append(pltpu.make_async_copy(parts.at[here], came.at[here], sems.at[i]))
+    loads.append(pltpu.make_async_copy(local_grad, grad, sems.at[PIECES]))
+    loads.append(pltpu.make_async_copy(table_now, table_t, sems.at[PIECES + 1]))
+    for load in loads:
+        load.start()
     share[...] = jnp.zeros_like(share)
-    for half in range(2):
-        total = None
-        for chip in range(CHIPS):
-            if color_of(chip) == half:
-                total = parts[chip] if total is None else total + parts[chip]
-        packed[half * KEPT : (half + 1) * KEPT, :] = total
+    totals = [None, None]
+    for i in range(PIECES):
+        loads[i].wait()
+        for chip in range(i * each, (i + 1) * each):
+            half = color_of(chip)
+            totals[half] = came[chip] if totals[half] is None else totals[half] + came[chip]
+    packed[0:KEPT, :] = totals[0]
+    packed[KEPT:PACK66, :] = totals[1]
     unpack66(packed, 0, share, 0)
+    adagrad(share, LANES, rel_t, rel_state, new_rel_t, new_rel_state)
+    loads[PIECES].wait()
     for i in range(NEG_DEV):
         at = row(negatives[i])
         grad[at, :] = grad[at, :] + share[REL4 + CHUNKS * i : REL4 + CHUNKS * (i + 1), :]
+    loads[PIECES + 1].wait()
     adagrad(grad, ENT_DEV, table_t, state, new_table_t, new_state)
-    adagrad(share, LANES, rel_t, rel_state, new_rel_t, new_rel_state)
 
 
 def adagrad_step(negatives, local_grad, parts, table_t, state, rel_t, rel_state):
@@ -661,14 +684,17 @@
     return pl.pallas_call(
         step_kernel,
         out_shape=(like(WIDTH, ENT_DEV), like(1, ENT_DEV), like(WIDTH, LANES), like(1, LANES)),
-        in_specs=[SMEM] + [VMEM] * 6,
+        in_specs=[SMEM, ANY, ANY, ANY] + [VMEM] * 3,
         out_specs=(VMEM,) * 4,
         scratch_shapes=[
             pltpu.VMEM((ENT_DEV * CHUNKS, LANES), f32),
+            pltpu.VMEM((CHIPS, KEPT, LANES), f32),
+            pltpu.VMEM((WIDTH, ENT_DEV), f32),
             pltpu.VMEM((CHUNKS * LANES, LANES), f32),
             pltpu.VMEM((PACK66, LANES), f32),
+            pltpu.SemaphoreType.DMA((PIECES + 2,)),
         ],
-        compiler_params=params(40),
+        compiler_params=params(58),
         cost_estimate=cost(0, 16 << 20),
         name="adagrad_step",
     )(negatives, local_grad, parts, table_t, state, rel_t, rel_state)

time: 334 us -> 322 us (0.964)
  local copies, waits for them, and re-layouts: 15 us -> 9.81 us
  waiting for transfers between devices: 110 us -> 106 us
    unnamed x43 -> x21, local copies, waits for them, and re-layouts: 12.6 us -> 6.23 us
    ppermute x6 -> x5, waiting for transfers between devices: 20.8 us -> 14.8 us  [local(): lax.ppermute(send, AXES[:3], matching(k))]
    ppermute x6 -> x5, starting transfers between devices: 8.41 us -> 5.09 us  [local(): lax.ppermute(send, AXES[:3], matching(k))]
  transfers between devices with their start and end apart: 14 -> 13, of which waited for: 8 -> 9; matrix products, arithmetic and copies ran while one was open for 1% -> 1% of each run, Pallas kernels for 31% -> 32%
where the time goes in v8:
time: 322 us; the launch traced here: 321 us
  Pallas kernels  138 us (43%)
  waiting for transfers between devices  106 us (33%)
  starting transfers between devices  36.9 us (11%)
  blocking collectives  15.3 us (5%)
  between operations  14.2 us (4%)
  local copies, waits for them, and re-layouts  9.81 us (3%)
    all_gather x1, waiting for transfers between devices, local(): shared = lax.all_gather(send, AXES, axis=0, tiled=True)  48.4 us
    pallas_call x1, Pallas kernels, queries(): pl.pallas_call(query_kernel, grid=(E_DEV // TILE,), out_shape=(PLANE, PLA...  44 us
    all_to_all x1, waiting for transfers between devices, local(): lax.all_to_all(met, AXES[:3], split_axis=0, concat_axis=0, tiled=True)  32.3 us
    pallas_call x1, Pallas kernels, gradients(): pl.pallas_call(edge_kernel, grid=(E_DEV // TILE,), out_shape=(half, piece...  28.8 us
    pallas_call x1, Pallas kernels, tail_terms(): pl.pallas_call(tail_kernel, grid=(E_DEV // TAIL_TILE,), out_shape=(PLANE,...  22.7 us
    all_to_all x2, starting transfers between devices, exchange(): lax.all_to_all(rows, AXES, split_axis=0, concat_axis=0, tiled=True)  19.7 us
    all_to_all x1, blocking collectives, local(): lax.all_to_all(pull_lists, AXES, split_axis=0, concat_axis=0, tiled=True)  15.3 us
    ppermute x5, waiting for transfers between devices, local(): lax.ppermute(send, AXES[:3], matching(k))  14.8 us
  transfers between devices with their start and end apart: 13, of which 9 were waited for; matrix products, arithmetic and copies ran while one was open for 1% of the time, Pallas kernels for 32%

profile of v8, /device:TPU:102, one launch (start us, length us, event | category | flops | bytes accessed | tf_op | source)
XLA Modules:
  0.0 321.2 jit_solution(10047444906395584580)
XLA Ops:
  7.2 0.0 all-gather.2.cloned.1.call-start
  7.2 1.0 copy.19
  8.3 0.7 pad_bitcast_fusion.rel_t
  9.0 3.4 %prep.1 = (f32[4096,128]{1,0:T(8,128)}, f32[208,128]{1,0:T(8,128)}) custom-call(s32[8]{0:T(128)} %negatives.3, f32[400,1024]{1,0:T(8,128)} %bitcast.26, f32[400,128]{1,0:T(8,128)} %pad_bitcast_fusion.rel_t), custom_call_target="tpu_custom_call" | custom-call | bytes 8388608 | tf_op jit(solution)/shard_map/prep/pallas_call | solution.py:188
  12.4 0.0 all-gather.2.cloned.1.call-update
  12.4 0.1 copy.18
  12.5 15.3 %all_to_all.24 = s32[128,1,16]{2,1,0:T(1,128)S(1)} all-to-all(s32[128,1,16]{2,1,0:T(1,128)S(1)} %bitcast.31), channel_id=1, replica_groups=mesh['x'=4,'z'=4,'y'=4,'c'=2] {'x','z','y','c'}, dimensions={0} | all-to-all | bytes 16384 | tf_op jit(solution)/shard_map/all_to_all | solution.py:723
  27.8 0.5 broadcast.25
  28.3 0.8 reduce.3
  29.2 0.7 reshape.58.asked
  29.8 9.8 %pull_rows.1 = f32[7168,128]{1,0:T(8,128)} custom-call(s32[2048]{0:T(1024)} %reshape.58.asked, f32[4096,128]{1,0:T(8,128)} %get-tuple-element.39.tab4), custom_call_target="tpu_custom_call" | custom-call | bytes 8388608 | tf_op jit(solution)/shard_map/pull_rows/pallas_call | solution.py:215
  39.6 48.4 %all-gather.2.cloned.1.call-done.shared = f32[26624,128]{1,0:T(8,128)} async-done(((f32[208,128]{1,0:T(8,128)}), f32[26624,128]{1,0:T(8,128)}) %all-gather.2.cloned.1.call-update) | async-done | bytes 13631504 | tf_op jit(solution)/shard_map/all_gather | solution.py:722
  88.0 9.5 %all-to-all-start.1 = ((f32[128,56,128]{2,1,0:T(8,128)}), f32[128,56,128]{2,1,0:T(8,128)}, u32[]{:S(2)}, u32[]{:S(2)}) async-start(f32[128,56,128]{2,1,0:T(8,128)} %bitcast.24), calls=%async_computation.1 | async-start | bytes 7340032 | tf_op jit(solution)/shard_map/all_to_all | solution.py:728
  97.5 0.6 multiply_add_fusion
  98.1 44.0 %queries.1 = (f32[4,2048,128]{2,1,0:T(8,128)}, f32[4,2048,128]{2,1,0:T(8,128)}, f32[4,2048,128]{2,1,0:T(8,128)}, f32[4,2048,128]{2,1,0:T(8,128)}, f32[1024,512]{1,0:T(8,128)}) custom-call(s32[2048]{0:T(1024)} %heads.3, s32[2048]{0:T(1024)} %get-tuple-element.86.rel_at, f32[4096,128]{1,0:T(8,128)} %get-tuple-element.39.tab4, ...), custom_call_target="tpu_custom_call" | custom-call | flops 35999997952 | bytes 62914560 | tf_op jit(solution)/shard_map/queries/pallas_call | solution.py:299
  142.1 0.0 all-to-all-done.1
  142.1 22.7 %tail_terms.1 = (f32[4,2048,128]{2,1,0:T(8,128)}, f32[4096,128]{1,0:T(8,128)}, f32[7168,128]{1,0:T(8,128)}) custom-call(s32[2048]{0:T(1024)} %tails.1, f32[4096,128]{1,0:T(8,128)} %get-tuple-element.39.tab4, f32[7168,128]{1,0:T(8,128)} %bitcast.6.fetched, f32[4,2048,128]{2,1,0:T(8,128)} %get-tuple-element.43.q_in), custom_call_target="tpu_custom_call" | custom-call | bytes 31457280 | tf_op jit(solution)/shard_map/tail_terms/pallas_call | solution.py:396
  164.9 10.1 %all-to-all-start.2 = ((f32[128,56,128]{2,1,0:T(8,128)}), f32[128,56,128]{2,1,0:T(8,128)}, u32[]{:S(2)}, u32[]{:S(2)}) async-start(f32[128,56,128]{2,1,0:T(8,128)} %bitcast.28), calls=%async_computation.2 | async-start | bytes 7340032 | tf_op jit(solution)/shard_map/all_to_all | solution.py:728
  175.0 28.8 %gradients.1 = (f32[13312,128]{1,0:T(8,128)}, f32[3328,128]{1,0:T(8,128)}, f32[3328,128]{1,0:T(8,128)}, f32[3328,128]{1,0:T(8,128)}, f32[3328,128]{1,0:T(8,128)}, /*index=5*/f32[4096,128]{1,0:T(8,128)}) custom-call(s32[2048]{0:T(1024)} %heads.3, s32[2048]{0:T(1024)} %get-tuple-element.87.grad_at, s32[1]{0:T(128)} %bitcast.2.core, ...), custom_call_target="tpu_custom_call" | custom-call | bytes 1048576 | tf_op jit(solution)/shard_map/gradients/pallas_call | solution.py:483
  203.8 0.2 collective-permute-start.2
  204.0 0.4 collective-permute-start.3
  204.4 0.1 collective-permute-start
  204.5 0.4 collective-permute-start.1
  204.9 2.8 collective-permute-done.2
  207.7 4.9 %collective-permute-done.3 = f32[3328,128]{1,0:T(8,128)S(1)} collective-permute-done((f32[3328,128]{1,0:T(8,128)}, f32[3328,128]{1,0:T(8,128)S(1)}, u32[]{:S(2)}, u32[]{:S(2)}) %collective-permute-start.3) | collective-permute-done | bytes 1703968 | tf_op jit(solution)/shard_map/ppermute | solution.py:738
  212.5 0.1 collective-permute-done
  212.7 2.4 collective-permute-done.1
  215.1 8.0 %merge.1 = (f32[64,104,128]{2,1,0:T(8,128)}, f32[13,104,128]{2,1,0:T(8,128)}, f32[13,104,128]{2,1,0:T(8,128)}, f32[13,104,128]{2,1,0:T(8,128)}, f32[13,104,128]{2,1,0:T(8,128)}, /*index=5*/f32[12,104,128]{2,1,0:T(8,128)}) custom-call(s32[1]{0:T(128)} %bitcast.1.color, f32[64,208,128]{2,1,0:T(8,128)} %bitcast.25, f32[16,208,128]{2,1,0:T(8,128)} %bitcast.8.got0, ...), custom_call_target="tpu_custom_call" | custom-call | bytes 65536 | tf_op jit(solution)/shard_map/merge/pallas_call | solution.py:546
  223.1 0.0 all-to-all-done.2
  223.1 0.6 collective-permute-start.4
  223.7 0.9 collective-permute-start.5
  224.6 0.5 collective-permute-start.6
  225.0 0.7 collective-permute-start.7
  225.8 2.4 collective-permute-start.8
  228.2 13.8 %collective-permute-done.8.got4 = f32[12,104,128]{2,1,0:T(8,128)S(1)} collective-permute-done((f32[12,104,128]{2,1,0:T(8,128)}, f32[12,104,128]{2,1,0:T(8,128)S(1)}, u32[]{:S(2)}, u32[]{:S(2)}) %collective-permute-start.8) | collective-permute-done | bytes 639008 | tf_op jit(solution)/shard_map/ppermute | solution.py:741
  242.0 0.2 collective-permute-done.4.got0
  242.2 0.8 collective-permute-done.6.got2
  243.0 2.0 copy-done.1
  245.0 3.2 meet.1
  248.2 0.0 copy-start.8
  248.2 11.0 %all-to-all-start.3 = ((f32[64,104,128]{2,1,0:T(8,128)}), f32[64,104,128]{2,1,0:T(8,128)}, u32[]{:S(2)}, u32[]{:S(2)}) async-start(f32[64,104,128]{2,1,0:T(8,128)} %meet.1), calls=%async_computation.3 | async-start | bytes 6815744 | tf_op jit(solution)/shard_map/all_to_all | solution.py:742
  259.3 0.5 pad_bitcast_fusion.1.rel_state
  259.8 11.8 %add_returned.1.local_grad = f32[4096,128]{1,0:T(8,128)S(1)} custom-call(s32[2048]{0:T(1024)S(1)} %copy-done.3, f32[7168,128]{1,0:T(8,128)} %bitcast.13.packed, f32[4096,128]{1,0:T(8,128)S(1)} %copy-done.2), custom_call_target="tpu_custom_call" | custom-call | bytes 10485760 | tf_op jit(solution)/shard_map/add_returned/pallas_call | solution.py:624
  271.6 1.4 copy-done
  273.0 32.3 %all-to-all-done.3.parts = f32[64,104,128]{2,1,0:T(8,128)} async-done(((f32[64,104,128]{2,1,0:T(8,128)}), f32[64,104,128]{2,1,0:T(8,128)}, u32[]{:S(2)}, u32[]{:S(2)}) %all-to-all-start.3) | async-done | bytes 3407904 | tf_op jit(solution)/shard_map/all_to_all | solution.py:742
  305.2 6.2 %adagrad_step.1 = (f32[400,1024]{1,0:T(8,128)}, f32[1,1024]{1,0:T(1,128)}, f32[400,128]{1,0:T(8,128)}, f32[1,128]{1,0:T(1,128)}) custom-call(s32[8]{0:T(128)} %negatives.3, f32[4096,128]{1,0:T(8,128)} %copy-done, f32[64,104,128]{2,1,0:T(8,128)} %all-to-all-done.3.parts, f32[400,1024]{1,0:T(8,128)} %bitcast.27, f32[1,1024]{1,0:T(1,128)} %bitcast.33, ...), custom_call_target="tpu_custom_call" | custom-call | bytes 16777216 | tf_op jit(solution)/shard_map/adagrad_step/pallas_call | solution.py:684
  311.5 1.7 copy.20
  313.2 1.2 slice_bitcast_fusion
  (17 shorter events, 0.0 us)
Async XLA Ops:
  7.2 5.2 %copy-start.6 = (s32[128,16]{0,1:T(8,128)S(1)}, s32[128,16]{0,1:T(8,128)}, u32[]{:S(2)}) copy-start(s32[128,16]{0,1:T(8,128)} %param.16) | copy-start | bytes 24580
  7.2 80.8 %all-gather.2.cloned.1.call-start = ((), (), s32[]{:S(2)}) async-start(), calls=%async_computation.4 | async-start | bytes 13737984 | tf_op jit(solution)/shard_map/all_gather | solution.py:722
  88.0 9.5 %copy-start.7 = (s32[2048]{0:T(1024)S(1)}, s32[2048]{0:T(1024)}, u32[]{:S(2)}) copy-start(s32[2048]{0:T(1024)} %param.14) | copy-start | bytes 24580
  88.0 54.2 %all-to-all-start.1 = ((f32[128,56,128]{2,1,0:T(8,128)}), f32[128,56,128]{2,1,0:T(8,128)}, u32[]{:S(2)}, u32[]{:S(2)}) async-start(f32[128,56,128]{2,1,0:T(8,128)} %bitcast.24), calls=%async_computation.1 | async-start | bytes 7340032 | tf_op jit(solution)/shard_map/all_to_all | solution.py:728
  164.9 58.2 %all-to-all-start.2 = ((f32[128,56,128]{2,1,0:T(8,128)}), f32[128,56,128]{2,1,0:T(8,128)}, u32[]{:S(2)}, u32[]{:S(2)}) async-start(f32[128,56,128]{2,1,0:T(8,128)} %bitcast.28), calls=%async_computation.2 | async-start | bytes 7340032 | tf_op jit(solution)/shard_map/all_to_all | solution.py:728
  203.8 3.9 %collective-permute-start.2 = (f32[3328,128]{1,0:T(8,128)}, f32[3328,128]{1,0:T(8,128)S(1)}, u32[]{:S(2)}, u32[]{:S(2)}) collective-permute-start(f32[3328,128]{1,0:T(8,128)} %get-tuple-element.53), channel_id=1, source_target_pairs={{0,1},{1,0},{2,3},{3,2},{4,5},{5,4},{6,7},{7,6},{8,9},{9,8},{10,11... | collective-permute-start | bytes 5111816 | tf_op jit(solution)/shard_map/ppermute | solution.py:738
  204.0 8.5 %collective-permute-start.3 = (f32[3328,128]{1,0:T(8,128)}, f32[3328,128]{1,0:T(8,128)S(1)}, u32[]{:S(2)}, u32[]{:S(2)}) collective-permute-start(f32[3328,128]{1,0:T(8,128)} %get-tuple-element.54), channel_id=1, source_target_pairs={{0,1},{1,0},{2,3},{3,2},{4,5},{5,4},{6,7},{7,6},{8,9},{9,8},{10,11... | collective-permute-start | bytes 5111816 | tf_op jit(solution)/shard_map/ppermute | solution.py:738
  204.4 8.3 %collective-permute-start = (f32[3328,128]{1,0:T(8,128)}, f32[3328,128]{1,0:T(8,128)}, u32[]{:S(2)}, u32[]{:S(2)}) collective-permute-start(f32[3328,128]{1,0:T(8,128)} %get-tuple-element.51), channel_id=1, source_target_pairs={{0,1},{1,0},{2,3},{3,2},{4,5},{5,4},{6,7},{7,6},{8,9},{9,8},{10,11... | collective-permute-start | bytes 5111816 | tf_op jit(solution)/shard_map/ppermute | solution.py:738
  204.5 10.6 %collective-permute-start.1 = (f32[3328,128]{1,0:T(8,128)}, f32[3328,128]{1,0:T(8,128)}, u32[]{:S(2)}, u32[]{:S(2)}) collective-permute-start(f32[3328,128]{1,0:T(8,128)} %get-tuple-element.52), channel_id=1, source_target_pairs={{0,1},{1,0},{2,3},{3,2},{4,5},{5,4},{6,7},{7,6},{8,9},{9,8},{10,11... | collective-permute-start | bytes 5111816 | tf_op jit(solution)/shard_map/ppermute | solution.py:738
  207.7 7.4 %copy-start.4 = (f32[3328,128]{1,0:T(8,128)}, f32[3328,128]{1,0:T(8,128)S(1)}, u32[]{:S(2)}) copy-start(f32[3328,128]{1,0:T(8,128)S(1)} %collective-permute-done.2) | copy-start | bytes 5111812
  212.5 2.6 copy-start.5
  223.1 19.1 %collective-permute-start.4 = (f32[13,104,128]{2,1,0:T(8,128)}, f32[13,104,128]{2,1,0:T(8,128)S(1)}, u32[]{:S(2)}, u32[]{:S(2)}) collective-permute-start(f32[13,104,128]{2,1,0:T(8,128)} %get-tuple-element.65), channel_id=1, source_target_pairs={{0,32},{32,0},{4,36},{36,4},{10,42},{42,10},{14,46},{46,14},{16,48... | collective-permute-start | bytes 2076680 | tf_op jit(solution)/shard_map/ppermute | solution.py:741
  223.7 18.5 %collective-permute-start.5 = (f32[13,104,128]{2,1,0:T(8,128)}, f32[13,104,128]{2,1,0:T(8,128)S(1)}, u32[]{:S(2)}, u32[]{:S(2)}) collective-permute-start(f32[13,104,128]{2,1,0:T(8,128)} %get-tuple-element.66), channel_id=1, source_target_pairs={{0,96},{96,0},{4,100},{100,4},{10,106},{106,10},{14,110},{110,14},... | collective-permute-start | bytes 2076680 | tf_op jit(solution)/shard_map/ppermute | solution.py:741
  224.6 18.4 %collective-permute-start.6 = (f32[13,104,128]{2,1,0:T(8,128)}, f32[13,104,128]{2,1,0:T(8,128)S(1)}, u32[]{:S(2)}, u32[]{:S(2)}) collective-permute-start(f32[13,104,128]{2,1,0:T(8,128)} %get-tuple-element.67), channel_id=1, source_target_pairs={{0,8},{8,0},{4,12},{12,4},{10,18},{18,10},{14,22},{22,14},{16,24},... | collective-permute-start | bytes 2076680 | tf_op jit(solution)/shard_map/ppermute | solution.py:741
  225.0 17.9 %collective-permute-start.7 = (f32[13,104,128]{2,1,0:T(8,128)}, f32[13,104,128]{2,1,0:T(8,128)S(1)}, u32[]{:S(2)}, u32[]{:S(2)}) collective-permute-start(f32[13,104,128]{2,1,0:T(8,128)} %get-tuple-element.68), channel_id=1, source_target_pairs={{0,24},{24,0},{4,28},{28,4},{10,2},{2,10},{14,6},{6,14},{16,8},{8,... | collective-permute-start | bytes 2076680 | tf_op jit(solution)/shard_map/ppermute | solution.py:741
  225.8 16.2 %collective-permute-start.8 = (f32[12,104,128]{2,1,0:T(8,128)}, f32[12,104,128]{2,1,0:T(8,128)S(1)}, u32[]{:S(2)}, u32[]{:S(2)}) collective-permute-start(f32[12,104,128]{2,1,0:T(8,128)} %get-tuple-element.69), channel_id=1, source_target_pairs={{0,2},{2,0},{4,6},{6,4},{10,12},{12,10},{14,8},{8,14},{16,18},{18,... | collective-permute-start | bytes 1916936 | tf_op jit(solution)/shard_map/ppermute | solution.py:741
  243.0 2.0 copy-start.1
  248.2 11.1 %copy-start.8 = (f32[58]{0:T(128)S(1)}, f32[58]{0:T(128)}, u32[]{:S(2)}) copy-start(f32[58]{0:T(128)} %param.12) | copy-start | bytes 700
  248.2 11.6 %copy-start.2 = (f32[4096,128]{1,0:T(8,128)S(1)}, f32[4096,128]{1,0:T(8,128)}, u32[]{:S(2)}) copy-start(f32[4096,128]{1,0:T(8,128)} %get-tuple-element.63.head_grad) | copy-start | bytes 6291460
  248.2 11.6 %copy-start.3 = (s32[2048]{0:T(1024)S(1)}, s32[2048]{0:T(1024)}, u32[]{:S(2)}) copy-start(s32[2048]{0:T(1024)} %reshape.58.asked) | copy-start | bytes 24580
  248.2 57.0 %all-to-all-start.3 = ((f32[64,104,128]{2,1,0:T(8,128)}), f32[64,104,128]{2,1,0:T(8,128)}, u32[]{:S(2)}, u32[]{:S(2)}) async-start(f32[64,104,128]{2,1,0:T(8,128)} %meet.1), calls=%async_computation.3 | async-start | bytes 6815744 | tf_op jit(solution)/shard_map/all_to_all | solution.py:742
  271.6 1.4 copy-start
Sparse Core Ops, SparseCore 0:
  12.5 75.4 all-gather.1

commit v9 on v8

--- a/solution.py
+++ b/solution.py
@@ -176,7 +176,14 @@
         dst[pl.ds(c, n, stride=CHUNKS), :] = piece.T
 
 
-def prep_kernel(negatives, table_t, rel_t, tab4, send, rel4):
+def turn_relations(rel, wide, rel_t):
+    wide[...] = jnp.zeros_like(wide)
+    wide[0:REL_DEV, 0:WIDTH] = rel[...]
+    rel_t[...] = wide[...].T
+
+
+def prep_kernel(negatives, table_t, rel, tab4, send, rel4, wide, rel_t):
+    turn_relations(rel, wide, rel_t)
     to_chunks(table_t, tab4, ENT_DEV)
     to_chunks(rel_t, rel4, LANES)
     for i in range(NEG_DEV):
@@ -184,7 +191,7 @@
     pack66(rel4, 0, send, 0)
 
 
-def prep(negatives, table_t, rel_t):
+def prep(negatives, table_t, rel):
     return pl.pallas_call(
         prep_kernel,
         out_shape=(
@@ -193,11 +200,15 @@
         ),
         in_specs=[SMEM, VMEM, VMEM],
         out_specs=(VMEM, VMEM),
-        scratch_shapes=[pltpu.VMEM((LANES * CHUNKS, LANES), f32)],
+        scratch_shapes=[
+            pltpu.VMEM((LANES * CHUNKS, LANES), f32),
+            pltpu.VMEM((LANES, CHUNKS * LANES), f32),
+            pltpu.VMEM((CHUNKS * LANES, LANES), f32),
+        ],
         compiler_params=params(58),
         cost_estimate=cost(0, 8 << 20),
         name="prep",
-    )(negatives, table_t, rel_t)
+    )(negatives, table_t, rel)
 
 
 def pull_kernel(asked, tab4, out, picked, packed, sem):
@@ -430,12 +441,12 @@
         rel_grad[...] = jnp.zeros_like(rel_grad)
         start.wait()
 
-    base = step * TILE
+    base = step * EDGE_TILE
     g = [p_in[c] + back_in[c] for c in range(CHUNKS)]
     for k in range(2):
         for buf, src in ((hb, r_in), (rb, h_in)):
-            buf[pl.ds(k, TILE, stride=CHUNKS), :] = g[k] * src[k] + g[k + 2] * src[k + 2]
-            buf[pl.ds(k + 2, TILE, stride=CHUNKS), :] = g[k + 2] * src[k] - g[k] * src[k + 2]
+            buf[pl.ds(k, EDGE_TILE, stride=CHUNKS), :] = g[k] * src[k] + g[k + 2] * src[k + 2]
+            buf[pl.ds(k + 2, EDGE_TILE, stride=CHUNKS), :] = g[k + 2] * src[k] - g[k] * src[k + 2]
 
     def scatter(i):
         at = row(heads[base + i])
@@ -443,9 +454,9 @@
         head_grad[at, :] = head_grad[at, :] + hb[row(i), :]
         rel_grad[rel, :] = rel_grad[rel, :] + rb[row(i), :]
 
-    rows_loop(TILE, scatter)
-
-    @pl.when(step == E_DEV // TILE - 1)
+    rows_loop(EDGE_TILE, scatter)
+
+    @pl.when(step == E_DEV // EDGE_TILE - 1)
     def _():
         def place(d, carry):
             spot = ((d % 2) * CHIPS + d // 2) * PER + REL4
@@ -476,21 +487,25 @@
             store.wait()
 
 
+EDGE_TILE = 512
+
+
 def gradients(heads, grad_at, core, tail_local, neg_acc, h, r, p, back):
     half = jax.ShapeDtypeStruct((CHIPS * PACK66, LANES), f32)
     piece = jax.ShapeDtypeStruct((CHIPS * PACK66 // PIECES, LANES), f32)
+    block = pl.BlockSpec((CHUNKS, EDGE_TILE, LANES), lambda i: (0, i, 0))
     whole = pl.BlockSpec((ENT_DEV * CHUNKS, LANES), lambda i: (0, 0))
     return pl.pallas_call(
         edge_kernel,
-        grid=(E_DEV // TILE,),
+        grid=(E_DEV // EDGE_TILE,),
         out_shape=(half, piece, piece, piece, piece, jax.ShapeDtypeStruct((ENT_DEV * CHUNKS, LANES), f32)),
-        in_specs=[SMEM, SMEM, SMEM, ANY, pl.BlockSpec((NEG, CHUNKS * LANES), lambda i: (0, 0)), BLOCK, BLOCK, BLOCK, BLOCK],
+        in_specs=[SMEM, SMEM, SMEM, ANY, pl.BlockSpec((NEG, CHUNKS * LANES), lambda i: (0, 0)), block, block, block, block],
         out_specs=(HBM,) * 5 + (whole,),
         scratch_shapes=[
             pltpu.VMEM((N_DEV * PER, LANES), f32),
             pltpu.VMEM((N_DEV * PACK66, LANES), f32),
-            pltpu.VMEM((TILE * CHUNKS, LANES), f32),
-            pltpu.VMEM((TILE * CHUNKS, LANES), f32),
+            pltpu.VMEM((EDGE_TILE * CHUNKS, LANES), f32),
+            pltpu.VMEM((EDGE_TILE * CHUNKS, LANES), f32),
             pltpu.SemaphoreType.DMA((PIECES + 1,)),
         ],
         compiler_params=params(58),
@@ -588,7 +603,7 @@
         in_specs=[ANY] + [VMEM] * WAYS,
         out_specs=HBM,
         scratch_shapes=[pltpu.VMEM((CHIPS, KEPT, LANES), f32), pltpu.SemaphoreType.DMA((2 * WAYS,))],
-        compiler_params=params(16),
+        compiler_params=params(47),
         cost_estimate=cost(0, 1 << 16),
         name="meet",
     )(keep, *got)
@@ -645,9 +660,9 @@
 
 
 def step_kernel(
-    negatives, local_grad, parts, table_now, state, rel_t, rel_state,
-    new_table_t, new_state, new_rel_t, new_rel_state,
-    grad, came, table_t, share, packed, sems,
+    negatives, local_grad, parts, table_now, state, rel, rel_state,
+    new_table_t, new_state, new_rel, new_rel_state,
+    grad, came, table_t, share, packed, wide, rel_t, new_rel_t, states, new_states, sems,
 ):
     each = CHIPS // PIECES
     loads = []
@@ -659,6 +674,10 @@
     for load in loads:
         load.start()
     share[...] = jnp.zeros_like(share)
+    turn_relations(rel, wide, rel_t)
+    new_rel_t[...] = jnp.zeros_like(new_rel_t)
+    states[...] = jnp.zeros_like(states)
+    states[:, 0:REL_DEV] = rel_state[...]
     totals = [None, None]
     for i in range(PIECES):
         loads[i].wait()
@@ -668,7 +687,9 @@
     packed[0:KEPT, :] = totals[0]
     packed[KEPT:PACK66, :] = totals[1]
     unpack66(packed, 0, share, 0)
-    adagrad(share, LANES, rel_t, rel_state, new_rel_t, new_rel_state)
+    adagrad(share, LANES, rel_t, states, new_rel_t, new_states)
+    new_rel[...] = new_rel_t[...].T[0:REL_DEV, 0:WIDTH]
+    new_rel_state[...] = new_states[:, 0:REL_DEV]
     loads[PIECES].wait()
     for i in range(NEG_DEV):
         at = row(negatives[i])
@@ -677,13 +698,13 @@
     adagrad(grad, ENT_DEV, table_t, state, new_table_t, new_state)
 
 
-def adagrad_step(negatives, local_grad, parts, table_t, state, rel_t, rel_state):
+def adagrad_step(negatives, local_grad, parts, table_t, state, rel, rel_state):
     def like(*shape):
         return jax.ShapeDtypeStruct(shape, f32)
 
     return pl.pallas_call(
         step_kernel,
-        out_shape=(like(WIDTH, ENT_DEV), like(1, ENT_DEV), like(WIDTH, LANES), like(1, LANES)),
+        out_shape=(like(WIDTH, ENT_DEV), like(1, ENT_DEV), like(REL_DEV, WIDTH), like(1, REL_DEV)),
         in_specs=[SMEM, ANY, ANY, ANY] + [VMEM] * 3,
         out_specs=(VMEM,) * 4,
         scratch_shapes=[
@@ -692,12 +713,17 @@
             pltpu.VMEM((WIDTH, ENT_DEV), f32),
             pltpu.VMEM((CHUNKS * LANES, LANES), f32),
             pltpu.VMEM((PACK66, LANES), f32),
+            pltpu.VMEM((LANES, CHUNKS * LANES), f32),
+            pltpu.VMEM((CHUNKS * LANES, LANES), f32),
+            pltpu.VMEM((CHUNKS * LANES, LANES), f32),
+            pltpu.VMEM((1, LANES), f32),
+            pltpu.VMEM((1, LANES), f32),
             pltpu.SemaphoreType.DMA((PIECES + 2,)),
         ],
         compiler_params=params(58),
         cost_estimate=cost(0, 16 << 20),
         name="adagrad_step",
-    )(negatives, local_grad, parts, table_t, state, rel_t, rel_state)
+    )(negatives, local_grad, parts, table_t, state, rel, rel_state)
 
 
 def local(
@@ -712,13 +738,12 @@
     negatives,
 ):
     table_t = entity_table.T
-    rel_t = jnp.pad(relation_table, ((0, LANES - REL_DEV), (0, 0))).T
     owner, place = relations // REL_DEV, relations % REL_DEV
     rel_at = owner * (REL_DEV + NEG_DEV) + place
     grad_at = ((owner % 2) * CHIPS + owner // 2) * (REL_DEV + NEG_DEV) + place
     core = lax.axis_index("c")
 
-    tab4, send = prep(negatives, table_t, rel_t)
+    tab4, send = prep(negatives, table_t, relation_table)
     shared = lax.all_gather(send, AXES, axis=0, tiled=True)
     asked = lax.all_to_all(pull_lists, AXES, split_axis=0, concat_axis=0, tiled=True).reshape(SLOTS)
     rows_out, shared = lax.optimization_barrier((pull_rows(asked, tab4), shared))
@@ -741,20 +766,20 @@
     met = meet(keep, [lax.ppermute(send, AXES[:3], matching(k)) for k, send in enumerate(sends)])
     parts = lax.all_to_all(met, AXES[:3], split_axis=0, concat_axis=0, tiled=True)
     local_grad = add_returned(asked, returned, head_grad)
-    new_table_t, new_state, new_rel_t, new_rel_state = adagrad_step(
+    new_table_t, new_state, new_rel, new_rel_state = adagrad_step(
         negatives,
         local_grad,
         parts,
         table_t,
         entity_state.reshape(1, ENT_DEV),
-        rel_t,
-        jnp.pad(relation_state, (0, LANES - REL_DEV)).reshape(1, LANES),
+        relation_table,
+        relation_state.reshape(1, REL_DEV),
     )
     return (
         new_table_t.T,
         new_state.reshape(ENT_DEV),
-        new_rel_t.T[:REL_DEV],
-        new_rel_state.reshape(LANES)[:REL_DEV],
+        new_rel,
+        new_rel_state.reshape(REL_DEV),
     )
 
 

time: 322 us -> 317 us (0.984)
  local copies, waits for them, and re-layouts: 9.81 us -> 3.4 us
    unnamed x21 -> x13, local copies, waits for them, and re-layouts: 6.23 us -> 2.22 us
  transfers between devices with their start and end apart: 13 -> 13, of which waited for: 9 -> 9; matrix products, arithmetic and copies ran while one was open for 1% -> 1% of each run, Pallas kernels for 32% -> 33%
where the time goes in v9:
time: 317 us; the launch traced here: 316 us
  Pallas kernels  139 us (44%)
  waiting for transfers between devices  106 us (33%)
  starting transfers between devices  36.9 us (12%)
  blocking collectives  15.3 us (5%)
  between operations  14.2 us (4%)
  local copies, waits for them, and re-layouts  3.4 us (1%)
    all_gather x1, waiting for transfers between devices, local(): shared = lax.all_gather(send, AXES, axis=0, tiled=True)  48.4 us
    pallas_call x1, Pallas kernels, queries(): pl.pallas_call(query_kernel, grid=(E_DEV // TILE,), out_shape=(PLANE, PLA...  44.1 us
    all_to_all x1, waiting for transfers between devices, local(): lax.all_to_all(met, AXES[:3], split_axis=0, concat_axis=0, tiled=True)  32.8 us
    pallas_call x1, Pallas kernels, gradients(): pl.pallas_call(edge_kernel, grid=(E_DEV // EDGE_TILE,), out_shape=(half,...  29.7 us
    pallas_call x1, Pallas kernels, tail_terms(): pl.pallas_call(tail_kernel, grid=(E_DEV // TAIL_TILE,), out_shape=(PLANE,...  22.7 us
    all_to_all x2, starting transfers between devices, exchange(): lax.all_to_all(rows, AXES, split_axis=0, concat_axis=0, tiled=True)  19.7 us
    all_to_all x1, blocking collectives, local(): lax.all_to_all(pull_lists, AXES, split_axis=0, concat_axis=0, tiled=True)  15.3 us
    ppermute x5, waiting for transfers between devices, local(): lax.ppermute(send, AXES[:3], matching(k))  14.8 us
  transfers between devices with their start and end apart: 13, of which 9 were waited for; matrix products, arithmetic and copies ran while one was open for 1% of the time, Pallas kernels for 33%

profile of v9, /device:TPU:102, one launch (start us, length us, event | category | flops | bytes accessed | tf_op | source)
XLA Modules:
  0.0 316.3 jit_solution(1838145731821299394)
XLA Ops:
  7.2 0.0 all-gather.2.cloned.1.call-start
  7.2 3.5 %prep.1 = (f32[4096,128]{1,0:T(8,128)}, f32[208,128]{1,0:T(8,128)}) custom-call(s32[8]{0:T(128)} %negatives.3, f32[400,1024]{1,0:T(8,128)} %bitcast.20, f32[58,400]{1,0:T(8,128)} %rel.3), custom_call_target="tpu_custom_call" | custom-call | bytes 8388608 | tf_op jit(solution)/shard_map/prep/pallas_call | solution.py:195
  10.7 0.0 all-gather.2.cloned.1.call-update
  10.7 0.8 copy.14
  11.5 15.3 %all_to_all.24 = s32[128,1,16]{2,1,0:T(1,128)S(1)} all-to-all(s32[128,1,16]{2,1,0:T(1,128)S(1)} %bitcast.25), channel_id=1, replica_groups=mesh['x'=4,'z'=4,'y'=4,'c'=2] {'x','z','y','c'}, dimensions={0} | all-to-all | bytes 16384 | tf_op jit(solution)/shard_map/all_to_all | solution.py:748
  26.8 0.5 broadcast.21
  27.3 0.8 reduce.3
  28.2 0.7 reshape.59.asked
  28.8 9.8 %pull_rows.1 = f32[7168,128]{1,0:T(8,128)} custom-call(s32[2048]{0:T(1024)} %reshape.59.asked, f32[4096,128]{1,0:T(8,128)} %get-tuple-element.39.tab4), custom_call_target="tpu_custom_call" | custom-call | bytes 8388608 | tf_op jit(solution)/shard_map/pull_rows/pallas_call | solution.py:226
  38.6 48.4 %all-gather.2.cloned.1.call-done.shared = f32[26624,128]{1,0:T(8,128)} async-done(((f32[208,128]{1,0:T(8,128)}), f32[26624,128]{1,0:T(8,128)}) %all-gather.2.cloned.1.call-update) | async-done | bytes 13631504 | tf_op jit(solution)/shard_map/all_gather | solution.py:747
  87.0 9.5 %all-to-all-start.1 = ((f32[128,56,128]{2,1,0:T(8,128)}), f32[128,56,128]{2,1,0:T(8,128)}, u32[]{:S(2)}, u32[]{:S(2)}) async-start(f32[128,56,128]{2,1,0:T(8,128)} %bitcast.18), calls=%async_computation.1 | async-start | bytes 7340032 | tf_op jit(solution)/shard_map/all_to_all | solution.py:753
  96.6 0.0 copy-done.5
  96.6 0.6 multiply_add_fusion
  97.2 44.1 %queries.1 = (f32[4,2048,128]{2,1,0:T(8,128)}, f32[4,2048,128]{2,1,0:T(8,128)}, f32[4,2048,128]{2,1,0:T(8,128)}, f32[4,2048,128]{2,1,0:T(8,128)}, f32[1024,512]{1,0:T(8,128)}) custom-call(s32[2048]{0:T(1024)} %heads.3, s32[2048]{0:T(1024)} %get-tuple-element.74.rel_at, f32[4096,128]{1,0:T(8,128)} %get-tuple-element.39.tab4, ...), custom_call_target="tpu_custom_call" | custom-call | flops 35999997952 | bytes 62914560 | tf_op jit(solution)/shard_map/queries/pallas_call | solution.py:310
  141.3 0.0 all-to-all-done.1
  141.3 22.7 %tail_terms.1 = (f32[4,2048,128]{2,1,0:T(8,128)}, f32[4096,128]{1,0:T(8,128)}, f32[7168,128]{1,0:T(8,128)}) custom-call(s32[2048]{0:T(1024)} %tails.1, f32[4096,128]{1,0:T(8,128)} %get-tuple-element.39.tab4, f32[7168,128]{1,0:T(8,128)} %bitcast.5.fetched, f32[4,2048,128]{2,1,0:T(8,128)} %get-tuple-element.43.q_in), custom_call_target="tpu_custom_call" | custom-call | bytes 31457280 | tf_op jit(solution)/shard_map/tail_terms/pallas_call | solution.py:407
  164.0 10.1 %all-to-all-start.2 = ((f32[128,56,128]{2,1,0:T(8,128)}), f32[128,56,128]{2,1,0:T(8,128)}, u32[]{:S(2)}, u32[]{:S(2)}) async-start(f32[128,56,128]{2,1,0:T(8,128)} %bitcast.22), calls=%async_computation.2 | async-start | bytes 7340032 | tf_op jit(solution)/shard_map/all_to_all | solution.py:753
  174.2 29.7 %gradients.1 = (f32[13312,128]{1,0:T(8,128)}, f32[3328,128]{1,0:T(8,128)}, f32[3328,128]{1,0:T(8,128)}, f32[3328,128]{1,0:T(8,128)}, f32[3328,128]{1,0:T(8,128)}, /*index=5*/f32[4096,128]{1,0:T(8,128)}) custom-call(s32[2048]{0:T(1024)} %heads.3, s32[2048]{0:T(1024)} %get-tuple-element.75.grad_at, s32[1]{0:T(128)} %bitcast.2.core, ...), custom_call_target="tpu_custom_call" | custom-call | bytes 1048576 | tf_op jit(solution)/shard_map/gradients/pallas_call | solution.py:498
  203.9 0.2 collective-permute-start
  204.2 0.4 collective-permute-start.1
  204.5 0.1 collective-permute-start.2
  204.7 0.4 collective-permute-start.3
  205.0 2.8 collective-permute-done
  207.8 4.9 %collective-permute-done.1 = f32[3328,128]{1,0:T(8,128)S(1)} collective-permute-done((f32[3328,128]{1,0:T(8,128)}, f32[3328,128]{1,0:T(8,128)S(1)}, u32[]{:S(2)}, u32[]{:S(2)}) %collective-permute-start.1) | collective-permute-done | bytes 1703968 | tf_op jit(solution)/shard_map/ppermute | solution.py:763
  212.7 0.1 collective-permute-done.2
  212.8 2.4 collective-permute-done.3
  215.3 0.0 copy-done.3
  215.3 0.0 copy-done.4
  215.3 7.9 %merge.1 = (f32[64,104,128]{2,1,0:T(8,128)}, f32[13,104,128]{2,1,0:T(8,128)}, f32[13,104,128]{2,1,0:T(8,128)}, f32[13,104,128]{2,1,0:T(8,128)}, f32[13,104,128]{2,1,0:T(8,128)}, /*index=5*/f32[12,104,128]{2,1,0:T(8,128)}) custom-call(s32[1]{0:T(128)} %bitcast.1.color, f32[64,208,128]{2,1,0:T(8,128)} %bitcast.19, f32[16,208,128]{2,1,0:T(8,128)} %bitcast.23, ...), custom_call_target="tpu_custom_call" | custom-call | bytes 65536 | tf_op jit(solution)/shard_map/merge/pallas_call | solution.py:561
  223.2 0.0 all-to-all-done.2
  223.2 0.6 collective-permute-start.4
  223.8 0.9 collective-permute-start.5
  224.7 0.5 collective-permute-start.6
  225.1 0.7 collective-permute-start.7
  225.9 2.4 collective-permute-start.8
  228.3 13.8 %collective-permute-done.8.got4 = f32[12,104,128]{2,1,0:T(8,128)S(1)} collective-permute-done((f32[12,104,128]{2,1,0:T(8,128)}, f32[12,104,128]{2,1,0:T(8,128)S(1)}, u32[]{:S(2)}, u32[]{:S(2)}) %collective-permute-start.8) | collective-permute-done | bytes 639008 | tf_op jit(solution)/shard_map/ppermute | solution.py:766
  242.1 0.2 collective-permute-done.4.got0
  242.3 0.0 collective-permute-done.5.got1
  242.3 0.8 collective-permute-done.6.got2
  243.1 0.0 collective-permute-done.7.got3
  243.1 3.1 meet.1
  246.2 11.0 %all-to-all-start.3 = ((f32[64,104,128]{2,1,0:T(8,128)}), f32[64,104,128]{2,1,0:T(8,128)}, u32[]{:S(2)}, u32[]{:S(2)}) async-start(f32[64,104,128]{2,1,0:T(8,128)} %meet.1), calls=%async_computation.3 | async-start | bytes 6815744 | tf_op jit(solution)/shard_map/all_to_all | solution.py:767
  257.3 0.0 copy-done.1
  257.3 0.0 copy-done.2
  257.3 11.8 %add_returned.1.local_grad = f32[4096,128]{1,0:T(8,128)S(1)} custom-call(s32[2048]{0:T(1024)S(1)} %copy-done.2, f32[7168,128]{1,0:T(8,128)} %bitcast.12.packed, f32[4096,128]{1,0:T(8,128)S(1)} %copy-done.1), custom_call_target="tpu_custom_call" | custom-call | bytes 10485760 | tf_op jit(solution)/shard_map/add_returned/pallas_call | solution.py:639
  269.1 1.4 copy-done
  270.5 32.8 %all-to-all-done.3.parts = f32[64,104,128]{2,1,0:T(8,128)} async-done(((f32[64,104,128]{2,1,0:T(8,128)}), f32[64,104,128]{2,1,0:T(8,128)}, u32[]{:S(2)}, u32[]{:S(2)}) %all-to-all-start.3) | async-done | bytes 3407904 | tf_op jit(solution)/shard_map/all_to_all | solution.py:767
  303.2 6.2 %adagrad_step.1 = (f32[400,1024]{1,0:T(8,128)}, f32[1,1024]{1,0:T(1,128)}, f32[58,400]{1,0:T(8,128)}, f32[1,58]{1,0:T(1,128)}) custom-call(s32[8]{0:T(128)} %negatives.3, f32[4096,128]{1,0:T(8,128)} %copy-done, f32[64,104,128]{2,1,0:T(8,128)} %all-to-all-done.3.parts, f32[400,1024]{1,0:T(8,128)} %bitcast.21, f32[1,1024]{1,0:T(1,128)} %bitcast.26, ...), custom_call_target="tpu_custom_call" | custom-call | bytes 16777216 | tf_op jit(solution)/shard_map/adagrad_step/pallas_call | solution.py:705
  (6 shorter events, 0.0 us)
Async XLA Ops:
  7.2 79.9 %all-gather.2.cloned.1.call-start = ((), (), s32[]{:S(2)}) async-start(), calls=%async_computation.4 | async-start | bytes 13737984 | tf_op jit(solution)/shard_map/all_gather | solution.py:747
  87.0 9.5 %copy-start.5 = (s32[2048]{0:T(1024)S(1)}, s32[2048]{0:T(1024)}, u32[]{:S(2)}) copy-start(s32[2048]{0:T(1024)} %param.14) | copy-start | bytes 24580
  87.0 54.3 %all-to-all-start.1 = ((f32[128,56,128]{2,1,0:T(8,128)}), f32[128,56,128]{2,1,0:T(8,128)}, u32[]{:S(2)}, u32[]{:S(2)}) async-start(f32[128,56,128]{2,1,0:T(8,128)} %bitcast.18), calls=%async_computation.1 | async-start | bytes 7340032 | tf_op jit(solution)/shard_map/all_to_all | solution.py:753
  164.0 59.2 %all-to-all-start.2 = ((f32[128,56,128]{2,1,0:T(8,128)}), f32[128,56,128]{2,1,0:T(8,128)}, u32[]{:S(2)}, u32[]{:S(2)}) async-start(f32[128,56,128]{2,1,0:T(8,128)} %bitcast.22), calls=%async_computation.2 | async-start | bytes 7340032 | tf_op jit(solution)/shard_map/all_to_all | solution.py:753
  203.9 3.9 %collective-permute-start = (f32[3328,128]{1,0:T(8,128)}, f32[3328,128]{1,0:T(8,128)S(1)}, u32[]{:S(2)}, u32[]{:S(2)}) collective-permute-start(f32[3328,128]{1,0:T(8,128)} %get-tuple-element.51), channel_id=1, source_target_pairs={{0,1},{1,0},{2,3},{3,2},{4,5},{5,4},{6,7},{7,6},{8,9},{9,8},{10,11... | collective-permute-start | bytes 5111816 | tf_op jit(solution)/shard_map/ppermute | solution.py:763
  204.2 8.5 %collective-permute-start.1 = (f32[3328,128]{1,0:T(8,128)}, f32[3328,128]{1,0:T(8,128)S(1)}, u32[]{:S(2)}, u32[]{:S(2)}) collective-permute-start(f32[3328,128]{1,0:T(8,128)} %get-tuple-element.52), channel_id=1, source_target_pairs={{0,1},{1,0},{2,3},{3,2},{4,5},{5,4},{6,7},{7,6},{8,9},{9,8},{10,11... | collective-permute-start | bytes 5111816 | tf_op jit(solution)/shard_map/ppermute | solution.py:763
  204.5 8.3 %collective-permute-start.2 = (f32[3328,128]{1,0:T(8,128)}, f32[3328,128]{1,0:T(8,128)}, u32[]{:S(2)}, u32[]{:S(2)}) collective-permute-start(f32[3328,128]{1,0:T(8,128)} %get-tuple-element.53), channel_id=1, source_target_pairs={{0,1},{1,0},{2,3},{3,2},{4,5},{5,4},{6,7},{7,6},{8,9},{9,8},{10,11... | collective-permute-start | bytes 5111816 | tf_op jit(solution)/shard_map/ppermute | solution.py:763
  204.7 10.6 %collective-permute-start.3 = (f32[3328,128]{1,0:T(8,128)}, f32[3328,128]{1,0:T(8,128)}, u32[]{:S(2)}, u32[]{:S(2)}) collective-permute-start(f32[3328,128]{1,0:T(8,128)} %get-tuple-element.54), channel_id=1, source_target_pairs={{0,1},{1,0},{2,3},{3,2},{4,5},{5,4},{6,7},{7,6},{8,9},{9,8},{10,11... | collective-permute-start | bytes 5111816 | tf_op jit(solution)/shard_map/ppermute | solution.py:763
  207.8 7.4 %copy-start.3 = (f32[3328,128]{1,0:T(8,128)}, f32[3328,128]{1,0:T(8,128)S(1)}, u32[]{:S(2)}) copy-start(f32[3328,128]{1,0:T(8,128)S(1)} %collective-permute-done) | copy-start | bytes 5111812
  212.7 2.6 copy-start.4
  223.2 19.1 %collective-permute-start.4 = (f32[13,104,128]{2,1,0:T(8,128)}, f32[13,104,128]{2,1,0:T(8,128)S(1)}, u32[]{:S(2)}, u32[]{:S(2)}) collective-permute-start(f32[13,104,128]{2,1,0:T(8,128)} %get-tuple-element.65), channel_id=1, source_target_pairs={{0,32},{32,0},{4,36},{36,4},{10,42},{42,10},{14,46},{46,14},{16,48... | collective-permute-start | bytes 2076680 | tf_op jit(solution)/shard_map/ppermute | solution.py:766
  223.8 18.5 %collective-permute-start.5 = (f32[13,104,128]{2,1,0:T(8,128)}, f32[13,104,128]{2,1,0:T(8,128)S(1)}, u32[]{:S(2)}, u32[]{:S(2)}) collective-permute-start(f32[13,104,128]{2,1,0:T(8,128)} %get-tuple-element.66), channel_id=1, source_target_pairs={{0,96},{96,0},{4,100},{100,4},{10,106},{106,10},{14,110},{110,14},... | collective-permute-start | bytes 2076680 | tf_op jit(solution)/shard_map/ppermute | solution.py:766
  224.7 18.4 %collective-permute-start.6 = (f32[13,104,128]{2,1,0:T(8,128)}, f32[13,104,128]{2,1,0:T(8,128)S(1)}, u32[]{:S(2)}, u32[]{:S(2)}) collective-permute-start(f32[13,104,128]{2,1,0:T(8,128)} %get-tuple-element.67), channel_id=1, source_target_pairs={{0,8},{8,0},{4,12},{12,4},{10,18},{18,10},{14,22},{22,14},{16,24},... | collective-permute-start | bytes 2076680 | tf_op jit(solution)/shard_map/ppermute | solution.py:766
  225.1 17.9 %collective-permute-start.7 = (f32[13,104,128]{2,1,0:T(8,128)}, f32[13,104,128]{2,1,0:T(8,128)S(1)}, u32[]{:S(2)}, u32[]{:S(2)}) collective-permute-start(f32[13,104,128]{2,1,0:T(8,128)} %get-tuple-element.68), channel_id=1, source_target_pairs={{0,24},{24,0},{4,28},{28,4},{10,2},{2,10},{14,6},{6,14},{16,8},{8,... | collective-permute-start | bytes 2076680 | tf_op jit(solution)/shard_map/ppermute | solution.py:766
  225.9 16.2 %collective-permute-start.8 = (f32[12,104,128]{2,1,0:T(8,128)}, f32[12,104,128]{2,1,0:T(8,128)S(1)}, u32[]{:S(2)}, u32[]{:S(2)}) collective-permute-start(f32[12,104,128]{2,1,0:T(8,128)} %get-tuple-element.69), channel_id=1, source_target_pairs={{0,2},{2,0},{4,6},{6,4},{10,12},{12,10},{14,8},{8,14},{16,18},{18,... | collective-permute-start | bytes 1916936 | tf_op jit(solution)/shard_map/ppermute | solution.py:766
  246.2 11.1 %copy-start.1 = (f32[4096,128]{1,0:T(8,128)S(1)}, f32[4096,128]{1,0:T(8,128)}, u32[]{:S(2)}) copy-start(f32[4096,128]{1,0:T(8,128)} %get-tuple-element.63.head_grad) | copy-start | bytes 6291460
  246.2 11.1 %copy-start.2 = (s32[2048]{0:T(1024)S(1)}, s32[2048]{0:T(1024)}, u32[]{:S(2)}) copy-start(s32[2048]{0:T(1024)} %reshape.59.asked) | copy-start | bytes 24580
  246.2 57.0 %all-to-all-start.3 = ((f32[64,104,128]{2,1,0:T(8,128)}), f32[64,104,128]{2,1,0:T(8,128)}, u32[]{:S(2)}, u32[]{:S(2)}) async-start(f32[64,104,128]{2,1,0:T(8,128)} %meet.1), calls=%async_computation.3 | async-start | bytes 6815744 | tf_op jit(solution)/shard_map/all_to_all | solution.py:767
  269.1 1.4 copy-start
Sparse Core Ops, SparseCore 0:
  11.6 75.4 all-gather.1

commit v10 on v9

--- a/solution.py
+++ b/solution.py
@@ -79,6 +79,12 @@
     lax.fori_loop(0, n // UNROLL, step, 0)
 
 
+def add_two(acc, a, b, first, second):
+    old_a, old_b = acc[row(a), :], acc[row(b), :]
+    acc[row(a), :] = old_a + first
+    acc[row(b), :] = (old_b + second) + jnp.where(a == b, first, jnp.zeros_like(first))
+
+
 def lane(n):
     return lax.broadcasted_iota(jnp.int32, (n, LANES), 1)
 
@@ -374,11 +380,11 @@
         p_out[c] = pos_grad * t[c]
         tb[pl.ds(c, TAIL_TILE, stride=CHUNKS), :] = pos_grad * q[c]
 
-    def scatter(i):
-        at = row(tails[base + i])
-        ext_grad[at, :] = ext_grad[at, :] + tb[row(i), :]
-
-    rows_loop(TAIL_TILE, scatter)
+    def scatter(pair):
+        i = pair * 2
+        add_two(ext_grad, tails[base + i], tails[base + i + 1], tb[row(i), :], tb[row(i + 1), :])
+
+    rows_loop(TAIL_TILE // 2, scatter)
 
     @pl.when(step == E_DEV // TAIL_TILE - 1)
     def _():
@@ -448,13 +454,12 @@
             buf[pl.ds(k, EDGE_TILE, stride=CHUNKS), :] = g[k] * src[k] + g[k + 2] * src[k + 2]
             buf[pl.ds(k + 2, EDGE_TILE, stride=CHUNKS), :] = g[k + 2] * src[k] - g[k] * src[k + 2]
 
-    def scatter(i):
-        at = row(heads[base + i])
-        rel = row(grad_at[base + i])
-        head_grad[at, :] = head_grad[at, :] + hb[row(i), :]
-        rel_grad[rel, :] = rel_grad[rel, :] + rb[row(i), :]
-
-    rows_loop(EDGE_TILE, scatter)
+    def scatter(pair):
+        i = pair * 2
+        add_two(head_grad, heads[base + i], heads[base + i + 1], hb[row(i), :], hb[row(i + 1), :])
+        add_two(rel_grad, grad_at[base + i], grad_at[base + i + 1], rb[row(i), :], rb[row(i + 1), :])
+
+    rows_loop(EDGE_TILE // 2, scatter)
 
     @pl.when(step == E_DEV // EDGE_TILE - 1)
     def _():
@@ -487,7 +492,7 @@
             store.wait()
 
 
-EDGE_TILE = 512
+EDGE_TILE = 256
 
 
 def gradients(heads, grad_at, core, tail_local, neg_acc, h, r, p, back):
@@ -628,11 +633,11 @@
     out[...] = head_grad[...]
     unpack_slots(packed, returned, 0)
 
-    def body(i):
-        at = row(asked[i])
-        out[at, :] = out[at, :] + returned[row(i), :]
-
-    rows_loop(SLOTS, body)
+    def body(pair):
+        i = pair * 2
+        add_two(out, asked[i], asked[i + 1], returned[row(i), :], returned[row(i + 1), :])
+
+    rows_loop(SLOTS // 2, body)
 
 
 def add_returned(asked, returned, head_grad):

time: 317 us -> 312 us (0.984)
  Pallas kernels: 139 us -> 132 us
  transfers between devices with their start and end apart: 13 -> 13, of which waited for: 9 -> 9; matrix products, arithmetic and copies ran while one was open for 1% -> 1% of each run, Pallas kernels for 33% -> 32%
where the time goes in v10:
time: 312 us; the launch traced here: 311 us
  Pallas kernels  132 us (42%)
  waiting for transfers between devices  108 us (35%)
  starting transfers between devices  36.9 us (12%)
  blocking collectives  15.3 us (5%)
  between operations  14.2 us (5%)
  local copies, waits for them, and re-layouts  3.4 us (1%)
    all_gather x1, waiting for transfers between devices, local(): shared = lax.all_gather(send, AXES, axis=0, tiled=True)  48.4 us
    pallas_call x1, Pallas kernels, queries(): pl.pallas_call(query_kernel, grid=(E_DEV // TILE,), out_shape=(PLANE, PLA...  44.1 us
    all_to_all x1, waiting for transfers between devices, local(): lax.all_to_all(met, AXES[:3], split_axis=0, concat_axis=0, tiled=True)  34.1 us
    pallas_call x1, Pallas kernels, gradients(): pl.pallas_call(edge_kernel, grid=(E_DEV // EDGE_TILE,), out_shape=(half,...  27 us
    pallas_call x1, Pallas kernels, tail_terms(): pl.pallas_call(tail_kernel, grid=(E_DEV // TAIL_TILE,), out_shape=(PLANE,...  20.5 us
    all_to_all x2, starting transfers between devices, exchange(): lax.all_to_all(rows, AXES, split_axis=0, concat_axis=0, tiled=True)  19.7 us
    all_to_all x1, blocking collectives, local(): lax.all_to_all(pull_lists, AXES, split_axis=0, concat_axis=0, tiled=True)  15.3 us
    ppermute x5, waiting for transfers between devices, local(): lax.ppermute(send, AXES[:3], matching(k))  14.8 us
  transfers between devices with their start and end apart: 13, of which 9 were waited for; matrix products, arithmetic and copies ran while one was open for 1% of the time, Pallas kernels for 32%

profile of v10, /device:TPU:102, one launch (start us, length us, event | category | flops | bytes accessed | tf_op | source)
XLA Modules:
  0.0 311.4 jit_solution(3630157956509499695)
XLA Ops:
  7.2 0.0 all-gather.2.cloned.1.call-start
  7.2 3.5 %prep.1 = (f32[4096,128]{1,0:T(8,128)}, f32[208,128]{1,0:T(8,128)}) custom-call(s32[8]{0:T(128)} %negatives.3, f32[400,1024]{1,0:T(8,128)} %bitcast.20, f32[58,400]{1,0:T(8,128)} %rel.3), custom_call_target="tpu_custom_call" | custom-call | bytes 8388608 | tf_op jit(solution)/shard_map/prep/pallas_call | solution.py:201
  10.7 0.0 all-gather.2.cloned.1.call-update
  10.7 0.8 copy.14
  11.5 15.3 %all_to_all.24 = s32[128,1,16]{2,1,0:T(1,128)S(1)} all-to-all(s32[128,1,16]{2,1,0:T(1,128)S(1)} %bitcast.25), channel_id=1, replica_groups=mesh['x'=4,'z'=4,'y'=4,'c'=2] {'x','z','y','c'}, dimensions={0} | all-to-all | bytes 16384 | tf_op jit(solution)/shard_map/all_to_all | solution.py:753
  26.8 0.5 broadcast.21
  27.3 0.8 reduce.3
  28.2 0.7 reshape.59.asked
  28.8 9.8 %pull_rows.1 = f32[7168,128]{1,0:T(8,128)} custom-call(s32[2048]{0:T(1024)} %reshape.59.asked, f32[4096,128]{1,0:T(8,128)} %get-tuple-element.39.tab4), custom_call_target="tpu_custom_call" | custom-call | bytes 8388608 | tf_op jit(solution)/shard_map/pull_rows/pallas_call | solution.py:232
  38.6 48.4 %all-gather.2.cloned.1.call-done.shared = f32[26624,128]{1,0:T(8,128)} async-done(((f32[208,128]{1,0:T(8,128)}), f32[26624,128]{1,0:T(8,128)}) %all-gather.2.cloned.1.call-update) | async-done | bytes 13631504 | tf_op jit(solution)/shard_map/all_gather | solution.py:752
  87.0 9.5 %all-to-all-start.1 = ((f32[128,56,128]{2,1,0:T(8,128)}), f32[128,56,128]{2,1,0:T(8,128)}, u32[]{:S(2)}, u32[]{:S(2)}) async-start(f32[128,56,128]{2,1,0:T(8,128)} %bitcast.18), calls=%async_computation.1 | async-start | bytes 7340032 | tf_op jit(solution)/shard_map/all_to_all | solution.py:758
  96.6 0.0 copy-done.5
  96.6 0.6 multiply_add_fusion
  97.2 44.1 %queries.1 = (f32[4,2048,128]{2,1,0:T(8,128)}, f32[4,2048,128]{2,1,0:T(8,128)}, f32[4,2048,128]{2,1,0:T(8,128)}, f32[4,2048,128]{2,1,0:T(8,128)}, f32[1024,512]{1,0:T(8,128)}) custom-call(s32[2048]{0:T(1024)} %heads.3, s32[2048]{0:T(1024)} %get-tuple-element.74.rel_at, f32[4096,128]{1,0:T(8,128)} %get-tuple-element.39.tab4, ...), custom_call_target="tpu_custom_call" | custom-call | flops 35999997952 | bytes 62914560 | tf_op jit(solution)/shard_map/queries/pallas_call | solution.py:316
  141.3 0.0 all-to-all-done.1
  141.3 20.5 %tail_terms.1 = (f32[4,2048,128]{2,1,0:T(8,128)}, f32[4096,128]{1,0:T(8,128)}, f32[7168,128]{1,0:T(8,128)}) custom-call(s32[2048]{0:T(1024)} %tails.1, f32[4096,128]{1,0:T(8,128)} %get-tuple-element.39.tab4, f32[7168,128]{1,0:T(8,128)} %bitcast.5.fetched, f32[4,2048,128]{2,1,0:T(8,128)} %get-tuple-element.43.q_in), custom_call_target="tpu_custom_call" | custom-call | bytes 31457280 | tf_op jit(solution)/shard_map/tail_terms/pallas_call | solution.py:413
  161.8 10.1 %all-to-all-start.2 = ((f32[128,56,128]{2,1,0:T(8,128)}), f32[128,56,128]{2,1,0:T(8,128)}, u32[]{:S(2)}, u32[]{:S(2)}) async-start(f32[128,56,128]{2,1,0:T(8,128)} %bitcast.22), calls=%async_computation.2 | async-start | bytes 7340032 | tf_op jit(solution)/shard_map/all_to_all | solution.py:758
  172.0 27.0 %gradients.1 = (f32[13312,128]{1,0:T(8,128)}, f32[3328,128]{1,0:T(8,128)}, f32[3328,128]{1,0:T(8,128)}, f32[3328,128]{1,0:T(8,128)}, f32[3328,128]{1,0:T(8,128)}, /*index=5*/f32[4096,128]{1,0:T(8,128)}) custom-call(s32[2048]{0:T(1024)} %heads.3, s32[2048]{0:T(1024)} %get-tuple-element.75.grad_at, s32[1]{0:T(128)} %bitcast.2.core, ...), custom_call_target="tpu_custom_call" | custom-call | bytes 1048576 | tf_op jit(solution)/shard_map/gradients/pallas_call | solution.py:503
  199.0 0.2 collective-permute-start
  199.2 0.4 collective-permute-start.1
  199.6 0.1 collective-permute-start.2
  199.7 0.4 collective-permute-start.3
  200.1 2.8 collective-permute-done
  202.9 4.9 %collective-permute-done.1 = f32[3328,128]{1,0:T(8,128)S(1)} collective-permute-done((f32[3328,128]{1,0:T(8,128)}, f32[3328,128]{1,0:T(8,128)S(1)}, u32[]{:S(2)}, u32[]{:S(2)}) %collective-permute-start.1) | collective-permute-done | bytes 1703968 | tf_op jit(solution)/shard_map/ppermute | solution.py:768
  207.7 0.1 collective-permute-done.2
  207.9 2.4 collective-permute-done.3
  210.3 0.0 copy-done.3
  210.3 0.0 copy-done.4
  210.3 7.9 %merge.1 = (f32[64,104,128]{2,1,0:T(8,128)}, f32[13,104,128]{2,1,0:T(8,128)}, f32[13,104,128]{2,1,0:T(8,128)}, f32[13,104,128]{2,1,0:T(8,128)}, f32[13,104,128]{2,1,0:T(8,128)}, /*index=5*/f32[12,104,128]{2,1,0:T(8,128)}) custom-call(s32[1]{0:T(128)} %bitcast.1.color, f32[64,208,128]{2,1,0:T(8,128)} %bitcast.19, f32[16,208,128]{2,1,0:T(8,128)} %bitcast.23, ...), custom_call_target="tpu_custom_call" | custom-call | bytes 65536 | tf_op jit(solution)/shard_map/merge/pallas_call | solution.py:566
  218.2 0.0 all-to-all-done.2
  218.2 0.6 collective-permute-start.4
  218.8 0.9 collective-permute-start.5
  219.7 0.7 collective-permute-start.6
  220.4 0.5 collective-permute-start.7
  220.9 2.4 collective-permute-start.8
  223.3 13.8 %collective-permute-done.8.got4 = f32[12,104,128]{2,1,0:T(8,128)S(1)} collective-permute-done((f32[12,104,128]{2,1,0:T(8,128)}, f32[12,104,128]{2,1,0:T(8,128)S(1)}, u32[]{:S(2)}, u32[]{:S(2)}) %collective-permute-start.8) | collective-permute-done | bytes 639008 | tf_op jit(solution)/shard_map/ppermute | solution.py:771
  237.1 0.2 collective-permute-done.4.got0
  237.3 0.0 collective-permute-done.5.got1
  237.3 0.8 collective-permute-done.6.got2
  238.1 0.0 collective-permute-done.7.got3
  238.1 3.1 meet.1
  241.2 0.0 copy-start.1
  241.3 0.0 copy-start.2
  241.3 11.0 %all-to-all-start.3 = ((f32[64,104,128]{2,1,0:T(8,128)}), f32[64,104,128]{2,1,0:T(8,128)}, u32[]{:S(2)}, u32[]{:S(2)}) async-start(f32[64,104,128]{2,1,0:T(8,128)} %meet.1), calls=%async_computation.3 | async-start | bytes 6815744 | tf_op jit(solution)/shard_map/all_to_all | solution.py:772
  252.3 10.4 %add_returned.1.local_grad = f32[4096,128]{1,0:T(8,128)S(1)} custom-call(s32[2048]{0:T(1024)S(1)} %copy-done.2, f32[7168,128]{1,0:T(8,128)} %bitcast.12.packed, f32[4096,128]{1,0:T(8,128)S(1)} %copy-done.1), custom_call_target="tpu_custom_call" | custom-call | bytes 10485760 | tf_op jit(solution)/shard_map/add_returned/pallas_call | solution.py:644
  262.8 1.4 copy-done
  264.2 34.1 %all-to-all-done.3.parts = f32[64,104,128]{2,1,0:T(8,128)} async-done(((f32[64,104,128]{2,1,0:T(8,128)}), f32[64,104,128]{2,1,0:T(8,128)}, u32[]{:S(2)}, u32[]{:S(2)}) %all-to-all-start.3) | async-done | bytes 3407904 | tf_op jit(solution)/shard_map/all_to_all | solution.py:772
  298.3 6.2 %adagrad_step.1 = (f32[400,1024]{1,0:T(8,128)}, f32[1,1024]{1,0:T(1,128)}, f32[58,400]{1,0:T(8,128)}, f32[1,58]{1,0:T(1,128)}) custom-call(s32[8]{0:T(128)} %negatives.3, f32[4096,128]{1,0:T(8,128)} %copy-done, f32[64,104,128]{2,1,0:T(8,128)} %all-to-all-done.3.parts, f32[400,1024]{1,0:T(8,128)} %bitcast.21, f32[1,1024]{1,0:T(1,128)} %bitcast.26, ...), custom_call_target="tpu_custom_call" | custom-call | bytes 16777216 | tf_op jit(solution)/shard_map/adagrad_step/pallas_call | solution.py:710
  (6 shorter events, 0.0 us)
Async XLA Ops:
  7.2 79.9 %all-gather.2.cloned.1.call-start = ((), (), s32[]{:S(2)}) async-start(), calls=%async_computation.4 | async-start | bytes 13737984 | tf_op jit(solution)/shard_map/all_gather | solution.py:752
  87.0 9.5 %copy-start.5 = (s32[2048]{0:T(1024)S(1)}, s32[2048]{0:T(1024)}, u32[]{:S(2)}) copy-start(s32[2048]{0:T(1024)} %param.14) | copy-start | bytes 24580
  87.0 54.3 %all-to-all-start.1 = ((f32[128,56,128]{2,1,0:T(8,128)}), f32[128,56,128]{2,1,0:T(8,128)}, u32[]{:S(2)}, u32[]{:S(2)}) async-start(f32[128,56,128]{2,1,0:T(8,128)} %bitcast.18), calls=%async_computation.1 | async-start | bytes 7340032 | tf_op jit(solution)/shard_map/all_to_all | solution.py:758
  161.8 56.4 %all-to-all-start.2 = ((f32[128,56,128]{2,1,0:T(8,128)}), f32[128,56,128]{2,1,0:T(8,128)}, u32[]{:S(2)}, u32[]{:S(2)}) async-start(f32[128,56,128]{2,1,0:T(8,128)} %bitcast.22), calls=%async_computation.2 | async-start | bytes 7340032 | tf_op jit(solution)/shard_map/all_to_all | solution.py:758
  199.0 3.9 %collective-permute-start = (f32[3328,128]{1,0:T(8,128)}, f32[3328,128]{1,0:T(8,128)S(1)}, u32[]{:S(2)}, u32[]{:S(2)}) collective-permute-start(f32[3328,128]{1,0:T(8,128)} %get-tuple-element.51), channel_id=1, source_target_pairs={{0,1},{1,0},{2,3},{3,2},{4,5},{5,4},{6,7},{7,6},{8,9},{9,8},{10,11... | collective-permute-start | bytes 5111816 | tf_op jit(solution)/shard_map/ppermute | solution.py:768
  199.2 8.5 %collective-permute-start.1 = (f32[3328,128]{1,0:T(8,128)}, f32[3328,128]{1,0:T(8,128)S(1)}, u32[]{:S(2)}, u32[]{:S(2)}) collective-permute-start(f32[3328,128]{1,0:T(8,128)} %get-tuple-element.52), channel_id=1, source_target_pairs={{0,1},{1,0},{2,3},{3,2},{4,5},{5,4},{6,7},{7,6},{8,9},{9,8},{10,11... | collective-permute-start | bytes 5111816 | tf_op jit(solution)/shard_map/ppermute | solution.py:768
  199.6 8.3 %collective-permute-start.2 = (f32[3328,128]{1,0:T(8,128)}, f32[3328,128]{1,0:T(8,128)}, u32[]{:S(2)}, u32[]{:S(2)}) collective-permute-start(f32[3328,128]{1,0:T(8,128)} %get-tuple-element.53), channel_id=1, source_target_pairs={{0,1},{1,0},{2,3},{3,2},{4,5},{5,4},{6,7},{7,6},{8,9},{9,8},{10,11... | collective-permute-start | bytes 5111816 | tf_op jit(solution)/shard_map/ppermute | solution.py:768
  199.7 10.6 %collective-permute-start.3 = (f32[3328,128]{1,0:T(8,128)}, f32[3328,128]{1,0:T(8,128)}, u32[]{:S(2)}, u32[]{:S(2)}) collective-permute-start(f32[3328,128]{1,0:T(8,128)} %get-tuple-element.54), channel_id=1, source_target_pairs={{0,1},{1,0},{2,3},{3,2},{4,5},{5,4},{6,7},{7,6},{8,9},{9,8},{10,11... | collective-permute-start | bytes 5111816 | tf_op jit(solution)/shard_map/ppermute | solution.py:768
  202.9 7.4 %copy-start.3 = (f32[3328,128]{1,0:T(8,128)}, f32[3328,128]{1,0:T(8,128)S(1)}, u32[]{:S(2)}) copy-start(f32[3328,128]{1,0:T(8,128)S(1)} %collective-permute-done) | copy-start | bytes 5111812
  207.7 2.6 copy-start.4
  218.2 19.1 %collective-permute-start.4 = (f32[13,104,128]{2,1,0:T(8,128)}, f32[13,104,128]{2,1,0:T(8,128)S(1)}, u32[]{:S(2)}, u32[]{:S(2)}) collective-permute-start(f32[13,104,128]{2,1,0:T(8,128)} %get-tuple-element.65), channel_id=1, source_target_pairs={{0,32},{32,0},{4,36},{36,4},{10,42},{42,10},{14,46},{46,14},{16,48... | collective-permute-start | bytes 2076680 | tf_op jit(solution)/shard_map/ppermute | solution.py:771
  218.8 18.5 %collective-permute-start.5 = (f32[13,104,128]{2,1,0:T(8,128)}, f32[13,104,128]{2,1,0:T(8,128)S(1)}, u32[]{:S(2)}, u32[]{:S(2)}) collective-permute-start(f32[13,104,128]{2,1,0:T(8,128)} %get-tuple-element.66), channel_id=1, source_target_pairs={{0,96},{96,0},{4,100},{100,4},{10,106},{106,10},{14,110},{110,14},... | collective-permute-start | bytes 2076680 | tf_op jit(solution)/shard_map/ppermute | solution.py:771
  219.7 18.4 %collective-permute-start.6 = (f32[13,104,128]{2,1,0:T(8,128)}, f32[13,104,128]{2,1,0:T(8,128)S(1)}, u32[]{:S(2)}, u32[]{:S(2)}) collective-permute-start(f32[13,104,128]{2,1,0:T(8,128)} %get-tuple-element.67), channel_id=1, source_target_pairs={{0,8},{8,0},{4,12},{12,4},{10,18},{18,10},{14,22},{22,14},{16,24},... | collective-permute-start | bytes 2076680 | tf_op jit(solution)/shard_map/ppermute | solution.py:771
  220.4 17.7 %collective-permute-start.7 = (f32[13,104,128]{2,1,0:T(8,128)}, f32[13,104,128]{2,1,0:T(8,128)S(1)}, u32[]{:S(2)}, u32[]{:S(2)}) collective-permute-start(f32[13,104,128]{2,1,0:T(8,128)} %get-tuple-element.68), channel_id=1, source_target_pairs={{0,24},{24,0},{4,28},{28,4},{10,2},{2,10},{14,6},{6,14},{16,8},{8,... | collective-permute-start | bytes 2076680 | tf_op jit(solution)/shard_map/ppermute | solution.py:771
  220.9 16.2 %collective-permute-start.8 = (f32[12,104,128]{2,1,0:T(8,128)}, f32[12,104,128]{2,1,0:T(8,128)S(1)}, u32[]{:S(2)}, u32[]{:S(2)}) collective-permute-start(f32[12,104,128]{2,1,0:T(8,128)} %get-tuple-element.69), channel_id=1, source_target_pairs={{0,2},{2,0},{4,6},{6,4},{10,12},{12,10},{14,8},{8,14},{16,18},{18,... | collective-permute-start | bytes 1916936 | tf_op jit(solution)/shard_map/ppermute | solution.py:771
  241.2 11.1 %copy-start.1 = (f32[4096,128]{1,0:T(8,128)S(1)}, f32[4096,128]{1,0:T(8,128)}, u32[]{:S(2)}) copy-start(f32[4096,128]{1,0:T(8,128)} %get-tuple-element.63.head_grad) | copy-start | bytes 6291460
  241.3 11.1 %copy-start.2 = (s32[2048]{0:T(1024)S(1)}, s32[2048]{0:T(1024)}, u32[]{:S(2)}) copy-start(s32[2048]{0:T(1024)} %reshape.59.asked) | copy-start | bytes 24580
  241.3 57.0 %all-to-all-start.3 = ((f32[64,104,128]{2,1,0:T(8,128)}), f32[64,104,128]{2,1,0:T(8,128)}, u32[]{:S(2)}, u32[]{:S(2)}) async-start(f32[64,104,128]{2,1,0:T(8,128)} %meet.1), calls=%async_computation.3 | async-start | bytes 6815744 | tf_op jit(solution)/shard_map/all_to_all | solution.py:772
  262.8 1.4 copy-start
Sparse Core Ops, SparseCore 0:
  11.6 75.4 all-gather.1

commit v11 on v10

--- a/solution.py
+++ b/solution.py
@@ -30,7 +30,7 @@
 KEPT = PACK66 // 2
 GROUPS = (0, 13, 26, 39, 52, 64)
 WAYS = len(GROUPS) - 1
-UNROLL = 8
+UNROLL = 16
 
 f32 = jnp.float32
 bf16 = jnp.bfloat16
@@ -139,11 +139,11 @@
 
 
 def pack_slots(src, src_base, dst):
-    blocks_loop(N_DEV, 4, lambda d: pack16(src, src_base + d * CAP * CHUNKS, dst, d * PACK16))
+    blocks_loop(N_DEV, 8, lambda d: pack16(src, src_base + d * CAP * CHUNKS, dst, d * PACK16))
 
 
 def unpack_slots(src, dst, dst_base):
-    blocks_loop(N_DEV, 4, lambda d: unpack16(src, d * PACK16, dst, dst_base + d * CAP * CHUNKS))
+    blocks_loop(N_DEV, 8, lambda d: unpack16(src, d * PACK16, dst, dst_base + d * CAP * CHUNKS))
 
 
 def pack66(src, src_base, dst, dst_base):
@@ -363,7 +363,7 @@
             def unpack(d, i=i):
                 unpack16(packed, (i * each + d) * PACK16, ext, local + (i * each + d) * CAP * CHUNKS)
 
-            blocks_loop(each, 4, unpack)
+            blocks_loop(each, 8, unpack)
         loads[PIECES].wait()
 
     base = step * TAIL_TILE
@@ -399,7 +399,7 @@
             def pack(d, i=i):
                 pack16(ext_grad, local + (i * each + d) * CAP * CHUNKS, packed, (i * each + d) * PACK16)
 
-            blocks_loop(each, 4, pack)
+            blocks_loop(each, 8, pack)
             stores[i].start()
         for store in stores:
             store.wait()

time: 312 us -> 310 us (level)
  Pallas kernels: 132 us -> 128 us
  transfers between devices with their start and end apart: 13 -> 13, of which waited for: 9 -> 9; matrix products, arithmetic and copies ran while one was open for 1% -> 1% of each run, Pallas kernels for 32% -> 31%
where the time goes in v11:
time: 310 us; the launch traced here: 309 us
  Pallas kernels  128 us (41%)
  waiting for transfers between devices  109 us (35%)
  starting transfers between devices  37 us (12%)
  blocking collectives  15.3 us (5%)
  between operations  14.2 us (5%)
  local copies, waits for them, and re-layouts  3.4 us (1%)
    all_gather x1, waiting for transfers between devices, local(): shared = lax.all_gather(send, AXES, axis=0, tiled=True)  50.4 us
    pallas_call x1, Pallas kernels, queries(): pl.pallas_call(query_kernel, grid=(E_DEV // TILE,), out_shape=(PLANE, PLA...  43.5 us
    all_to_all x1, waiting for transfers between devices, local(): lax.all_to_all(met, AXES[:3], split_axis=0, concat_axis=0, tiled=True)  34 us
    pallas_call x1, Pallas kernels, gradients(): pl.pallas_call(edge_kernel, grid=(E_DEV // EDGE_TILE,), out_shape=(half,...  26.8 us
    all_to_all x2, starting transfers between devices, exchange(): lax.all_to_all(rows, AXES, split_axis=0, concat_axis=0, tiled=True)  19.7 us
    pallas_call x1, Pallas kernels, tail_terms(): pl.pallas_call(tail_kernel, grid=(E_DEV // TAIL_TILE,), out_shape=(PLANE,...  18.9 us
    all_to_all x1, blocking collectives, local(): lax.all_to_all(pull_lists, AXES, split_axis=0, concat_axis=0, tiled=True)  15.3 us
    ppermute x5, waiting for transfers between devices, local(): lax.ppermute(send, AXES[:3], matching(k))  14.8 us
  transfers between devices with their start and end apart: 13, of which 9 were waited for; matrix products, arithmetic and copies ran while one was open for 1% of the time, Pallas kernels for 31%

profile of v11, /device:TPU:102, one launch (start us, length us, event | category | flops | bytes accessed | tf_op | source)
XLA Modules:
  0.0 308.9 jit_solution(5348954469697730194)
XLA Ops:
  7.2 0.0 all-gather.2.cloned.1.call-start
  7.2 3.5 %prep.1 = (f32[4096,128]{1,0:T(8,128)}, f32[208,128]{1,0:T(8,128)}) custom-call(s32[8]{0:T(128)} %negatives.3, f32[400,1024]{1,0:T(8,128)} %bitcast.20, f32[58,400]{1,0:T(8,128)} %rel.3), custom_call_target="tpu_custom_call" | custom-call | bytes 8388608 | tf_op jit(solution)/shard_map/prep/pallas_call | solution.py:201
  10.7 0.0 all-gather.2.cloned.1.call-update
  10.7 0.8 copy.14
  11.5 15.3 %all_to_all.24 = s32[128,1,16]{2,1,0:T(1,128)S(1)} all-to-all(s32[128,1,16]{2,1,0:T(1,128)S(1)} %bitcast.25), channel_id=1, replica_groups=mesh['x'=4,'z'=4,'y'=4,'c'=2] {'x','z','y','c'}, dimensions={0} | all-to-all | bytes 16384 | tf_op jit(solution)/shard_map/all_to_all | solution.py:753
  26.8 0.5 broadcast.21
  27.3 0.8 reduce.3
  28.2 0.7 reshape.59.asked
  28.8 7.8 %pull_rows.1 = f32[7168,128]{1,0:T(8,128)} custom-call(s32[2048]{0:T(1024)} %reshape.59.asked, f32[4096,128]{1,0:T(8,128)} %get-tuple-element.39.tab4), custom_call_target="tpu_custom_call" | custom-call | bytes 8388608 | tf_op jit(solution)/shard_map/pull_rows/pallas_call | solution.py:232
  36.6 50.4 %all-gather.2.cloned.1.call-done.shared = f32[26624,128]{1,0:T(8,128)} async-done(((f32[208,128]{1,0:T(8,128)}), f32[26624,128]{1,0:T(8,128)}) %all-gather.2.cloned.1.call-update) | async-done | bytes 13631504 | tf_op jit(solution)/shard_map/all_gather | solution.py:752
  87.0 9.5 %all-to-all-start.1 = ((f32[128,56,128]{2,1,0:T(8,128)}), f32[128,56,128]{2,1,0:T(8,128)}, u32[]{:S(2)}, u32[]{:S(2)}) async-start(f32[128,56,128]{2,1,0:T(8,128)} %bitcast.18), calls=%async_computation.1 | async-start | bytes 7340032 | tf_op jit(solution)/shard_map/all_to_all | solution.py:758
  96.5 0.0 copy-done.5
  96.6 0.6 multiply_add_fusion
  97.2 43.5 %queries.1 = (f32[4,2048,128]{2,1,0:T(8,128)}, f32[4,2048,128]{2,1,0:T(8,128)}, f32[4,2048,128]{2,1,0:T(8,128)}, f32[4,2048,128]{2,1,0:T(8,128)}, f32[1024,512]{1,0:T(8,128)}) custom-call(s32[2048]{0:T(1024)} %heads.3, s32[2048]{0:T(1024)} %get-tuple-element.74.rel_at, f32[4096,128]{1,0:T(8,128)} %get-tuple-element.39.tab4, ...), custom_call_target="tpu_custom_call" | custom-call | flops 35999997952 | bytes 62914560 | tf_op jit(solution)/shard_map/queries/pallas_call | solution.py:316
  140.7 0.0 all-to-all-done.1
  140.7 18.9 %tail_terms.1 = (f32[4,2048,128]{2,1,0:T(8,128)}, f32[4096,128]{1,0:T(8,128)}, f32[7168,128]{1,0:T(8,128)}) custom-call(s32[2048]{0:T(1024)} %tails.1, f32[4096,128]{1,0:T(8,128)} %get-tuple-element.39.tab4, f32[7168,128]{1,0:T(8,128)} %bitcast.5.fetched, f32[4,2048,128]{2,1,0:T(8,128)} %get-tuple-element.43.q_in), custom_call_target="tpu_custom_call" | custom-call | bytes 31457280 | tf_op jit(solution)/shard_map/tail_terms/pallas_call | solution.py:413
  159.5 10.2 %all-to-all-start.2 = ((f32[128,56,128]{2,1,0:T(8,128)}), f32[128,56,128]{2,1,0:T(8,128)}, u32[]{:S(2)}, u32[]{:S(2)}) async-start(f32[128,56,128]{2,1,0:T(8,128)} %bitcast.22), calls=%async_computation.2 | async-start | bytes 7340032 | tf_op jit(solution)/shard_map/all_to_all | solution.py:758
  169.7 26.8 %gradients.1 = (f32[13312,128]{1,0:T(8,128)}, f32[3328,128]{1,0:T(8,128)}, f32[3328,128]{1,0:T(8,128)}, f32[3328,128]{1,0:T(8,128)}, f32[3328,128]{1,0:T(8,128)}, /*index=5*/f32[4096,128]{1,0:T(8,128)}) custom-call(s32[2048]{0:T(1024)} %heads.3, s32[2048]{0:T(1024)} %get-tuple-element.75.grad_at, s32[1]{0:T(128)} %bitcast.2.core, ...), custom_call_target="tpu_custom_call" | custom-call | bytes 1048576 | tf_op jit(solution)/shard_map/gradients/pallas_call | solution.py:503
  196.5 0.2 collective-permute-start
  196.7 0.4 collective-permute-start.1
  197.1 0.1 collective-permute-start.2
  197.2 0.4 collective-permute-start.3
  197.6 2.8 collective-permute-done
  200.4 4.9 %collective-permute-done.1 = f32[3328,128]{1,0:T(8,128)S(1)} collective-permute-done((f32[3328,128]{1,0:T(8,128)}, f32[3328,128]{1,0:T(8,128)S(1)}, u32[]{:S(2)}, u32[]{:S(2)}) %collective-permute-start.1) | collective-permute-done | bytes 1703968 | tf_op jit(solution)/shard_map/ppermute | solution.py:768
  205.3 0.1 collective-permute-done.2
  205.4 2.4 collective-permute-done.3
  207.8 0.0 copy-done.3
  207.8 0.0 copy-done.4
  207.8 7.9 %merge.1 = (f32[64,104,128]{2,1,0:T(8,128)}, f32[13,104,128]{2,1,0:T(8,128)}, f32[13,104,128]{2,1,0:T(8,128)}, f32[13,104,128]{2,1,0:T(8,128)}, f32[13,104,128]{2,1,0:T(8,128)}, /*index=5*/f32[12,104,128]{2,1,0:T(8,128)}) custom-call(s32[1]{0:T(128)} %bitcast.1.color, f32[64,208,128]{2,1,0:T(8,128)} %bitcast.19, f32[16,208,128]{2,1,0:T(8,128)} %bitcast.23, ...), custom_call_target="tpu_custom_call" | custom-call | bytes 65536 | tf_op jit(solution)/shard_map/merge/pallas_call | solution.py:566
  215.8 0.0 all-to-all-done.2
  215.8 0.6 collective-permute-start.4
  216.4 0.9 collective-permute-start.5
  217.2 0.9 collective-permute-start.6
  218.2 0.2 collective-permute-start.7
  218.4 2.4 collective-permute-start.8
  220.9 13.8 %collective-permute-done.8.got4 = f32[12,104,128]{2,1,0:T(8,128)S(1)} collective-permute-done((f32[12,104,128]{2,1,0:T(8,128)}, f32[12,104,128]{2,1,0:T(8,128)S(1)}, u32[]{:S(2)}, u32[]{:S(2)}) %collective-permute-start.8) | collective-permute-done | bytes 639008 | tf_op jit(solution)/shard_map/ppermute | solution.py:771
  234.6 0.2 collective-permute-done.4.got0
  234.8 0.0 collective-permute-done.5.got1
  234.8 0.8 collective-permute-done.6.got2
  235.7 0.0 collective-permute-done.7.got3
  235.7 3.1 %meet.1 = f32[64,104,128]{2,1,0:T(8,128)} custom-call(f32[64,104,128]{2,1,0:T(8,128)} %get-tuple-element.64.keep, f32[13,104,128]{2,1,0:T(8,128)S(1)} %collective-permute-done.4.got0, f32[13,104,128]{2,1,0:T(8,128)S(1)} %collective-permute-done.5.got1, f32[13,104,128]{2,1,0:T(8,128)S(1)} %collective-permute-done.6.got2, ...), custom_call_target="tpu_custom_call" | custom-call | bytes 65536 | tf_op jit(solution)/shard_map/meet/pallas_call | solution.py:605
  238.8 0.0 copy-start.1
  238.8 0.0 copy-start.2
  238.8 11.0 %all-to-all-start.3 = ((f32[64,104,128]{2,1,0:T(8,128)}), f32[64,104,128]{2,1,0:T(8,128)}, u32[]{:S(2)}, u32[]{:S(2)}) async-start(f32[64,104,128]{2,1,0:T(8,128)} %meet.1), calls=%async_computation.3 | async-start | bytes 6815744 | tf_op jit(solution)/shard_map/all_to_all | solution.py:772
  249.9 10.6 %add_returned.1.local_grad = f32[4096,128]{1,0:T(8,128)S(1)} custom-call(s32[2048]{0:T(1024)S(1)} %copy-done.2, f32[7168,128]{1,0:T(8,128)} %bitcast.12.packed, f32[4096,128]{1,0:T(8,128)S(1)} %copy-done.1), custom_call_target="tpu_custom_call" | custom-call | bytes 10485760 | tf_op jit(solution)/shard_map/add_returned/pallas_call | solution.py:644
  260.4 1.4 copy-done
  261.8 34.0 %all-to-all-done.3.parts = f32[64,104,128]{2,1,0:T(8,128)} async-done(((f32[64,104,128]{2,1,0:T(8,128)}), f32[64,104,128]{2,1,0:T(8,128)}, u32[]{:S(2)}, u32[]{:S(2)}) %all-to-all-start.3) | async-done | bytes 3407904 | tf_op jit(solution)/shard_map/all_to_all | solution.py:772
  295.8 6.2 %adagrad_step.1 = (f32[400,1024]{1,0:T(8,128)}, f32[1,1024]{1,0:T(1,128)}, f32[58,400]{1,0:T(8,128)}, f32[1,58]{1,0:T(1,128)}) custom-call(s32[8]{0:T(128)} %negatives.3, f32[4096,128]{1,0:T(8,128)} %copy-done, f32[64,104,128]{2,1,0:T(8,128)} %all-to-all-done.3.parts, f32[400,1024]{1,0:T(8,128)} %bitcast.21, f32[1,1024]{1,0:T(1,128)} %bitcast.26, ...), custom_call_target="tpu_custom_call" | custom-call | bytes 16777216 | tf_op jit(solution)/shard_map/adagrad_step/pallas_call | solution.py:710
  (6 shorter events, 0.0 us)
Async XLA Ops:
  7.2 79.8 %all-gather.2.cloned.1.call-start = ((), (), s32[]{:S(2)}) async-start(), calls=%async_computation.4 | async-start | bytes 13737984 | tf_op jit(solution)/shard_map/all_gather | solution.py:752
  87.0 9.5 %copy-start.5 = (s32[2048]{0:T(1024)S(1)}, s32[2048]{0:T(1024)}, u32[]{:S(2)}) copy-start(s32[2048]{0:T(1024)} %param.14) | copy-start | bytes 24580
  87.0 53.7 %all-to-all-start.1 = ((f32[128,56,128]{2,1,0:T(8,128)}), f32[128,56,128]{2,1,0:T(8,128)}, u32[]{:S(2)}, u32[]{:S(2)}) async-start(f32[128,56,128]{2,1,0:T(8,128)} %bitcast.18), calls=%async_computation.1 | async-start | bytes 7340032 | tf_op jit(solution)/shard_map/all_to_all | solution.py:758
  159.5 56.2 %all-to-all-start.2 = ((f32[128,56,128]{2,1,0:T(8,128)}), f32[128,56,128]{2,1,0:T(8,128)}, u32[]{:S(2)}, u32[]{:S(2)}) async-start(f32[128,56,128]{2,1,0:T(8,128)} %bitcast.22), calls=%async_computation.2 | async-start | bytes 7340032 | tf_op jit(solution)/shard_map/all_to_all | solution.py:758
  196.5 3.9 %collective-permute-start = (f32[3328,128]{1,0:T(8,128)}, f32[3328,128]{1,0:T(8,128)S(1)}, u32[]{:S(2)}, u32[]{:S(2)}) collective-permute-start(f32[3328,128]{1,0:T(8,128)} %get-tuple-element.51), channel_id=1, source_target_pairs={{0,1},{1,0},{2,3},{3,2},{4,5},{5,4},{6,7},{7,6},{8,9},{9,8},{10,11... | collective-permute-start | bytes 5111816 | tf_op jit(solution)/shard_map/ppermute | solution.py:768
  196.7 8.5 %collective-permute-start.1 = (f32[3328,128]{1,0:T(8,128)}, f32[3328,128]{1,0:T(8,128)S(1)}, u32[]{:S(2)}, u32[]{:S(2)}) collective-permute-start(f32[3328,128]{1,0:T(8,128)} %get-tuple-element.52), channel_id=1, source_target_pairs={{0,1},{1,0},{2,3},{3,2},{4,5},{5,4},{6,7},{7,6},{8,9},{9,8},{10,11... | collective-permute-start | bytes 5111816 | tf_op jit(solution)/shard_map/ppermute | solution.py:768
  197.1 8.3 %collective-permute-start.2 = (f32[3328,128]{1,0:T(8,128)}, f32[3328,128]{1,0:T(8,128)}, u32[]{:S(2)}, u32[]{:S(2)}) collective-permute-start(f32[3328,128]{1,0:T(8,128)} %get-tuple-element.53), channel_id=1, source_target_pairs={{0,1},{1,0},{2,3},{3,2},{4,5},{5,4},{6,7},{7,6},{8,9},{9,8},{10,11... | collective-permute-start | bytes 5111816 | tf_op jit(solution)/shard_map/ppermute | solution.py:768
  197.2 10.6 %collective-permute-start.3 = (f32[3328,128]{1,0:T(8,128)}, f32[3328,128]{1,0:T(8,128)}, u32[]{:S(2)}, u32[]{:S(2)}) collective-permute-start(f32[3328,128]{1,0:T(8,128)} %get-tuple-element.54), channel_id=1, source_target_pairs={{0,1},{1,0},{2,3},{3,2},{4,5},{5,4},{6,7},{7,6},{8,9},{9,8},{10,11... | collective-permute-start | bytes 5111816 | tf_op jit(solution)/shard_map/ppermute | solution.py:768
  200.4 7.4 %copy-start.3 = (f32[3328,128]{1,0:T(8,128)}, f32[3328,128]{1,0:T(8,128)S(1)}, u32[]{:S(2)}) copy-start(f32[3328,128]{1,0:T(8,128)S(1)} %collective-permute-done) | copy-start | bytes 5111812
  205.3 2.6 copy-start.4
  215.8 19.1 %collective-permute-start.4 = (f32[13,104,128]{2,1,0:T(8,128)}, f32[13,104,128]{2,1,0:T(8,128)S(1)}, u32[]{:S(2)}, u32[]{:S(2)}) collective-permute-start(f32[13,104,128]{2,1,0:T(8,128)} %get-tuple-element.65), channel_id=1, source_target_pairs={{0,32},{32,0},{4,36},{36,4},{10,42},{42,10},{14,46},{46,14},{16,48... | collective-permute-start | bytes 2076680 | tf_op jit(solution)/shard_map/ppermute | solution.py:771
  216.4 18.5 %collective-permute-start.5 = (f32[13,104,128]{2,1,0:T(8,128)}, f32[13,104,128]{2,1,0:T(8,128)S(1)}, u32[]{:S(2)}, u32[]{:S(2)}) collective-permute-start(f32[13,104,128]{2,1,0:T(8,128)} %get-tuple-element.66), channel_id=1, source_target_pairs={{0,96},{96,0},{4,100},{100,4},{10,106},{106,10},{14,110},{110,14},... | collective-permute-start | bytes 2076680 | tf_op jit(solution)/shard_map/ppermute | solution.py:771
  217.2 18.4 %collective-permute-start.6 = (f32[13,104,128]{2,1,0:T(8,128)}, f32[13,104,128]{2,1,0:T(8,128)S(1)}, u32[]{:S(2)}, u32[]{:S(2)}) collective-permute-start(f32[13,104,128]{2,1,0:T(8,128)} %get-tuple-element.67), channel_id=1, source_target_pairs={{0,8},{8,0},{4,12},{12,4},{10,18},{18,10},{14,22},{22,14},{16,24},... | collective-permute-start | bytes 2076680 | tf_op jit(solution)/shard_map/ppermute | solution.py:771
  218.2 17.5 %collective-permute-start.7 = (f32[13,104,128]{2,1,0:T(8,128)}, f32[13,104,128]{2,1,0:T(8,128)S(1)}, u32[]{:S(2)}, u32[]{:S(2)}) collective-permute-start(f32[13,104,128]{2,1,0:T(8,128)} %get-tuple-element.68), channel_id=1, source_target_pairs={{0,24},{24,0},{4,28},{28,4},{10,2},{2,10},{14,6},{6,14},{16,8},{8,... | collective-permute-start | bytes 2076680 | tf_op jit(solution)/shard_map/ppermute | solution.py:771
  218.4 16.2 %collective-permute-start.8 = (f32[12,104,128]{2,1,0:T(8,128)}, f32[12,104,128]{2,1,0:T(8,128)S(1)}, u32[]{:S(2)}, u32[]{:S(2)}) collective-permute-start(f32[12,104,128]{2,1,0:T(8,128)} %get-tuple-element.69), channel_id=1, source_target_pairs={{0,2},{2,0},{4,6},{6,4},{10,12},{12,10},{14,8},{8,14},{16,18},{18,... | collective-permute-start | bytes 1916936 | tf_op jit(solution)/shard_map/ppermute | solution.py:771
  238.8 11.1 %copy-start.1 = (f32[4096,128]{1,0:T(8,128)S(1)}, f32[4096,128]{1,0:T(8,128)}, u32[]{:S(2)}) copy-start(f32[4096,128]{1,0:T(8,128)} %get-tuple-element.63.head_grad) | copy-start | bytes 6291460
  238.8 11.1 %copy-start.2 = (s32[2048]{0:T(1024)S(1)}, s32[2048]{0:T(1024)}, u32[]{:S(2)}) copy-start(s32[2048]{0:T(1024)} %reshape.59.asked) | copy-start | bytes 24580
  238.8 57.0 %all-to-all-start.3 = ((f32[64,104,128]{2,1,0:T(8,128)}), f32[64,104,128]{2,1,0:T(8,128)}, u32[]{:S(2)}, u32[]{:S(2)}) async-start(f32[64,104,128]{2,1,0:T(8,128)} %meet.1), calls=%async_computation.3 | async-start | bytes 6815744 | tf_op jit(solution)/shard_map/all_to_all | solution.py:772
  260.4 1.4 copy-start
Sparse Core Ops, SparseCore 0:
  11.6 75.3 all-gather.1

commit v12 on v11

--- a/solution.py
+++ b/solution.py
@@ -85,6 +85,15 @@
     acc[row(b), :] = (old_b + second) + jnp.where(a == b, first, jnp.zeros_like(first))
 
 
+def add_four(acc, spots, terms):
+    sums = [acc[row(spot), :] + term for spot, term in zip(spots, terms, strict=True)]
+    for j in range(4):
+        total = sums[j]
+        for m in range(j):
+            total = total + jnp.where(spots[m] == spots[j], terms[m], jnp.zeros_like(total))
+        acc[row(spots[j]), :] = total
+
+
 def lane(n):
     return lax.broadcasted_iota(jnp.int32, (n, LANES), 1)
 
@@ -380,11 +389,11 @@
         p_out[c] = pos_grad * t[c]
         tb[pl.ds(c, TAIL_TILE, stride=CHUNKS), :] = pos_grad * q[c]
 
-    def scatter(pair):
-        i = pair * 2
-        add_two(ext_grad, tails[base + i], tails[base + i + 1], tb[row(i), :], tb[row(i + 1), :])
-
-    rows_loop(TAIL_TILE // 2, scatter)
+    def scatter(group):
+        i = group * 4
+        add_four(ext_grad, [tails[base + i + k] for k in range(4)], [tb[row(i + k), :] for k in range(4)])
+
+    blocks_loop(TAIL_TILE // 4, 8, scatter)
 
     @pl.when(step == E_DEV // TAIL_TILE - 1)
     def _():

time: 310 us -> 309 us (level)
  no operation moved by 1% of the time
where the time goes in v12:
time: 309 us; the launch traced here: 308 us
  Pallas kernels  127 us (41%)
  waiting for transfers between devices  109 us (35%)
  starting transfers between devices  37 us (12%)
  blocking collectives  15.3 us (5%)
  between operations  14.2 us (5%)
  local copies, waits for them, and re-layouts  3.4 us (1%)
    all_gather x1, waiting for transfers between devices, local(): shared = lax.all_gather(send, AXES, axis=0, tiled=True)  50.4 us
    pallas_call x1, Pallas kernels, queries(): pl.pallas_call(query_kernel, grid=(E_DEV // TILE,), out_shape=(PLANE, PLA...  43.5 us
    all_to_all x1, waiting for transfers between devices, local(): lax.all_to_all(met, AXES[:3], split_axis=0, concat_axis=0, tiled=True)  34 us
    pallas_call x1, Pallas kernels, gradients(): pl.pallas_call(edge_kernel, grid=(E_DEV // EDGE_TILE,), out_shape=(half,...  26.8 us
    all_to_all x2, starting transfers between devices, exchange(): lax.all_to_all(rows, AXES, split_axis=0, concat_axis=0, tiled=True)  19.7 us
    pallas_call x1, Pallas kernels, tail_terms(): pl.pallas_call(tail_kernel, grid=(E_DEV // TAIL_TILE,), out_shape=(PLANE,...  17.7 us
    all_to_all x1, blocking collectives, local(): lax.all_to_all(pull_lists, AXES, split_axis=0, concat_axis=0, tiled=True)  15.3 us
    ppermute x5, waiting for transfers between devices, local(): lax.ppermute(send, AXES[:3], matching(k))  14.8 us
  transfers between devices with their start and end apart: 13, of which 9 were waited for; matrix products, arithmetic and copies ran while one was open for 1% of the time, Pallas kernels for 31%

profile of v12, /device:TPU:102, one launch (start us, length us, event | category | flops | bytes accessed | tf_op | source)
XLA Modules:
  0.0 307.8 jit_solution(16093111783198855534)
XLA Ops:
  7.2 0.0 all-gather.2.cloned.1.call-start
  7.2 3.5 %prep.1 = (f32[4096,128]{1,0:T(8,128)}, f32[208,128]{1,0:T(8,128)}) custom-call(s32[8]{0:T(128)} %negatives.3, f32[400,1024]{1,0:T(8,128)} %bitcast.20, f32[58,400]{1,0:T(8,128)} %rel.3), custom_call_target="tpu_custom_call" | custom-call | bytes 8388608 | tf_op jit(solution)/shard_map/prep/pallas_call | solution.py:210
  10.7 0.0 all-gather.2.cloned.1.call-update
  10.7 0.8 copy.14
  11.5 15.3 %all_to_all.24 = s32[128,1,16]{2,1,0:T(1,128)S(1)} all-to-all(s32[128,1,16]{2,1,0:T(1,128)S(1)} %bitcast.25), channel_id=1, replica_groups=mesh['x'=4,'z'=4,'y'=4,'c'=2] {'x','z','y','c'}, dimensions={0} | all-to-all | bytes 16384 | tf_op jit(solution)/shard_map/all_to_all | solution.py:762
  26.8 0.5 broadcast.21
  27.3 0.8 reduce.3
  28.2 0.7 reshape.59.asked
  28.8 7.8 %pull_rows.1 = f32[7168,128]{1,0:T(8,128)} custom-call(s32[2048]{0:T(1024)} %reshape.59.asked, f32[4096,128]{1,0:T(8,128)} %get-tuple-element.39.tab4), custom_call_target="tpu_custom_call" | custom-call | bytes 8388608 | tf_op jit(solution)/shard_map/pull_rows/pallas_call | solution.py:241
  36.6 50.4 %all-gather.2.cloned.1.call-done.shared = f32[26624,128]{1,0:T(8,128)} async-done(((f32[208,128]{1,0:T(8,128)}), f32[26624,128]{1,0:T(8,128)}) %all-gather.2.cloned.1.call-update) | async-done | bytes 13631504 | tf_op jit(solution)/shard_map/all_gather | solution.py:761
  87.0 9.5 %all-to-all-start.1 = ((f32[128,56,128]{2,1,0:T(8,128)}), f32[128,56,128]{2,1,0:T(8,128)}, u32[]{:S(2)}, u32[]{:S(2)}) async-start(f32[128,56,128]{2,1,0:T(8,128)} %bitcast.18), calls=%async_computation.1 | async-start | bytes 7340032 | tf_op jit(solution)/shard_map/all_to_all | solution.py:767
  96.5 0.0 copy-done.5
  96.6 0.6 multiply_add_fusion
  97.2 43.5 %queries.1 = (f32[4,2048,128]{2,1,0:T(8,128)}, f32[4,2048,128]{2,1,0:T(8,128)}, f32[4,2048,128]{2,1,0:T(8,128)}, f32[4,2048,128]{2,1,0:T(8,128)}, f32[1024,512]{1,0:T(8,128)}) custom-call(s32[2048]{0:T(1024)} %heads.3, s32[2048]{0:T(1024)} %get-tuple-element.74.rel_at, f32[4096,128]{1,0:T(8,128)} %get-tuple-element.39.tab4, ...), custom_call_target="tpu_custom_call" | custom-call | flops 35999997952 | bytes 62914560 | tf_op jit(solution)/shard_map/queries/pallas_call | solution.py:325
  140.7 0.0 all-to-all-done.1
  140.7 17.7 %tail_terms.1 = (f32[4,2048,128]{2,1,0:T(8,128)}, f32[4096,128]{1,0:T(8,128)}, f32[7168,128]{1,0:T(8,128)}) custom-call(s32[2048]{0:T(1024)} %tails.1, f32[4096,128]{1,0:T(8,128)} %get-tuple-element.39.tab4, f32[7168,128]{1,0:T(8,128)} %bitcast.5.fetched, f32[4,2048,128]{2,1,0:T(8,128)} %get-tuple-element.43.q_in), custom_call_target="tpu_custom_call" | custom-call | bytes 31457280 | tf_op jit(solution)/shard_map/tail_terms/pallas_call | solution.py:422
  158.4 10.2 %all-to-all-start.2 = ((f32[128,56,128]{2,1,0:T(8,128)}), f32[128,56,128]{2,1,0:T(8,128)}, u32[]{:S(2)}, u32[]{:S(2)}) async-start(f32[128,56,128]{2,1,0:T(8,128)} %bitcast.22), calls=%async_computation.2 | async-start | bytes 7340032 | tf_op jit(solution)/shard_map/all_to_all | solution.py:767
  168.6 26.8 %gradients.1 = (f32[13312,128]{1,0:T(8,128)}, f32[3328,128]{1,0:T(8,128)}, f32[3328,128]{1,0:T(8,128)}, f32[3328,128]{1,0:T(8,128)}, f32[3328,128]{1,0:T(8,128)}, /*index=5*/f32[4096,128]{1,0:T(8,128)}) custom-call(s32[2048]{0:T(1024)} %heads.3, s32[2048]{0:T(1024)} %get-tuple-element.75.grad_at, s32[1]{0:T(128)} %bitcast.2.core, ...), custom_call_target="tpu_custom_call" | custom-call | bytes 1048576 | tf_op jit(solution)/shard_map/gradients/pallas_call | solution.py:512
  195.4 0.2 collective-permute-start
  195.6 0.4 collective-permute-start.1
  196.0 0.1 collective-permute-start.2
  196.2 0.4 collective-permute-start.3
  196.5 2.8 collective-permute-done
  199.3 4.9 %collective-permute-done.1 = f32[3328,128]{1,0:T(8,128)S(1)} collective-permute-done((f32[3328,128]{1,0:T(8,128)}, f32[3328,128]{1,0:T(8,128)S(1)}, u32[]{:S(2)}, u32[]{:S(2)}) %collective-permute-start.1) | collective-permute-done | bytes 1703968 | tf_op jit(solution)/shard_map/ppermute | solution.py:777
  204.2 0.1 collective-permute-done.2
  204.3 2.4 collective-permute-done.3
  206.7 0.0 copy-done.3
  206.7 0.0 copy-done.4
  206.8 7.9 %merge.1 = (f32[64,104,128]{2,1,0:T(8,128)}, f32[13,104,128]{2,1,0:T(8,128)}, f32[13,104,128]{2,1,0:T(8,128)}, f32[13,104,128]{2,1,0:T(8,128)}, f32[13,104,128]{2,1,0:T(8,128)}, /*index=5*/f32[12,104,128]{2,1,0:T(8,128)}) custom-call(s32[1]{0:T(128)} %bitcast.1.color, f32[64,208,128]{2,1,0:T(8,128)} %bitcast.19, f32[16,208,128]{2,1,0:T(8,128)} %bitcast.23, ...), custom_call_target="tpu_custom_call" | custom-call | bytes 65536 | tf_op jit(solution)/shard_map/merge/pallas_call | solution.py:575
  214.7 0.0 all-to-all-done.2
  214.7 0.6 collective-permute-start.4
  215.3 0.9 collective-permute-start.5
  216.1 0.9 collective-permute-start.6
  217.1 0.2 collective-permute-start.7
  217.3 2.4 collective-permute-start.8
  219.8 13.8 %collective-permute-done.8.got4 = f32[12,104,128]{2,1,0:T(8,128)S(1)} collective-permute-done((f32[12,104,128]{2,1,0:T(8,128)}, f32[12,104,128]{2,1,0:T(8,128)S(1)}, u32[]{:S(2)}, u32[]{:S(2)}) %collective-permute-start.8) | collective-permute-done | bytes 639008 | tf_op jit(solution)/shard_map/ppermute | solution.py:780
  233.6 0.2 collective-permute-done.4.got0
  233.8 0.0 collective-permute-done.5.got1
  233.8 0.8 collective-permute-done.6.got2
  234.6 0.0 collective-permute-done.7.got3
  234.6 3.1 %meet.1 = f32[64,104,128]{2,1,0:T(8,128)} custom-call(f32[64,104,128]{2,1,0:T(8,128)} %get-tuple-element.64.keep, f32[13,104,128]{2,1,0:T(8,128)S(1)} %collective-permute-done.4.got0, f32[13,104,128]{2,1,0:T(8,128)S(1)} %collective-permute-done.5.got1, f32[13,104,128]{2,1,0:T(8,128)S(1)} %collective-permute-done.6.got2, ...), custom_call_target="tpu_custom_call" | custom-call | bytes 65536 | tf_op jit(solution)/shard_map/meet/pallas_call | solution.py:614
  237.7 0.0 copy-start.1
  237.7 0.0 copy-start.2
  237.7 11.0 %all-to-all-start.3 = ((f32[64,104,128]{2,1,0:T(8,128)}), f32[64,104,128]{2,1,0:T(8,128)}, u32[]{:S(2)}, u32[]{:S(2)}) async-start(f32[64,104,128]{2,1,0:T(8,128)} %meet.1), calls=%async_computation.3 | async-start | bytes 6815744 | tf_op jit(solution)/shard_map/all_to_all | solution.py:781
  248.8 10.6 %add_returned.1.local_grad = f32[4096,128]{1,0:T(8,128)S(1)} custom-call(s32[2048]{0:T(1024)S(1)} %copy-done.2, f32[7168,128]{1,0:T(8,128)} %bitcast.12.packed, f32[4096,128]{1,0:T(8,128)S(1)} %copy-done.1), custom_call_target="tpu_custom_call" | custom-call | bytes 10485760 | tf_op jit(solution)/shard_map/add_returned/pallas_call | solution.py:653
  259.4 1.4 copy-done
  260.8 34.0 %all-to-all-done.3.parts = f32[64,104,128]{2,1,0:T(8,128)} async-done(((f32[64,104,128]{2,1,0:T(8,128)}), f32[64,104,128]{2,1,0:T(8,128)}, u32[]{:S(2)}, u32[]{:S(2)}) %all-to-all-start.3) | async-done | bytes 3407904 | tf_op jit(solution)/shard_map/all_to_all | solution.py:781
  294.7 6.2 %adagrad_step.1 = (f32[400,1024]{1,0:T(8,128)}, f32[1,1024]{1,0:T(1,128)}, f32[58,400]{1,0:T(8,128)}, f32[1,58]{1,0:T(1,128)}) custom-call(s32[8]{0:T(128)} %negatives.3, f32[4096,128]{1,0:T(8,128)} %copy-done, f32[64,104,128]{2,1,0:T(8,128)} %all-to-all-done.3.parts, f32[400,1024]{1,0:T(8,128)} %bitcast.21, f32[1,1024]{1,0:T(1,128)} %bitcast.26, ...), custom_call_target="tpu_custom_call" | custom-call | bytes 16777216 | tf_op jit(solution)/shard_map/adagrad_step/pallas_call | solution.py:719
  (6 shorter events, 0.0 us)
Async XLA Ops:
  7.2 79.8 %all-gather.2.cloned.1.call-start = ((), (), s32[]{:S(2)}) async-start(), calls=%async_computation.4 | async-start | bytes 13737984 | tf_op jit(solution)/shard_map/all_gather | solution.py:761
  87.0 9.5 %copy-start.5 = (s32[2048]{0:T(1024)S(1)}, s32[2048]{0:T(1024)}, u32[]{:S(2)}) copy-start(s32[2048]{0:T(1024)} %param.14) | copy-start | bytes 24580
  87.0 53.7 %all-to-all-start.1 = ((f32[128,56,128]{2,1,0:T(8,128)}), f32[128,56,128]{2,1,0:T(8,128)}, u32[]{:S(2)}, u32[]{:S(2)}) async-start(f32[128,56,128]{2,1,0:T(8,128)} %bitcast.18), calls=%async_computation.1 | async-start | bytes 7340032 | tf_op jit(solution)/shard_map/all_to_all | solution.py:767
  158.4 56.2 %all-to-all-start.2 = ((f32[128,56,128]{2,1,0:T(8,128)}), f32[128,56,128]{2,1,0:T(8,128)}, u32[]{:S(2)}, u32[]{:S(2)}) async-start(f32[128,56,128]{2,1,0:T(8,128)} %bitcast.22), calls=%async_computation.2 | async-start | bytes 7340032 | tf_op jit(solution)/shard_map/all_to_all | solution.py:767
  195.4 3.9 %collective-permute-start = (f32[3328,128]{1,0:T(8,128)}, f32[3328,128]{1,0:T(8,128)S(1)}, u32[]{:S(2)}, u32[]{:S(2)}) collective-permute-start(f32[3328,128]{1,0:T(8,128)} %get-tuple-element.51), channel_id=1, source_target_pairs={{0,1},{1,0},{2,3},{3,2},{4,5},{5,4},{6,7},{7,6},{8,9},{9,8},{10,11... | collective-permute-start | bytes 5111816 | tf_op jit(solution)/shard_map/ppermute | solution.py:777
  195.6 8.5 %collective-permute-start.1 = (f32[3328,128]{1,0:T(8,128)}, f32[3328,128]{1,0:T(8,128)S(1)}, u32[]{:S(2)}, u32[]{:S(2)}) collective-permute-start(f32[3328,128]{1,0:T(8,128)} %get-tuple-element.52), channel_id=1, source_target_pairs={{0,1},{1,0},{2,3},{3,2},{4,5},{5,4},{6,7},{7,6},{8,9},{9,8},{10,11... | collective-permute-start | bytes 5111816 | tf_op jit(solution)/shard_map/ppermute | solution.py:777
  196.0 8.3 %collective-permute-start.2 = (f32[3328,128]{1,0:T(8,128)}, f32[3328,128]{1,0:T(8,128)}, u32[]{:S(2)}, u32[]{:S(2)}) collective-permute-start(f32[3328,128]{1,0:T(8,128)} %get-tuple-element.53), channel_id=1, source_target_pairs={{0,1},{1,0},{2,3},{3,2},{4,5},{5,4},{6,7},{7,6},{8,9},{9,8},{10,11... | collective-permute-start | bytes 5111816 | tf_op jit(solution)/shard_map/ppermute | solution.py:777
  196.2 10.6 %collective-permute-start.3 = (f32[3328,128]{1,0:T(8,128)}, f32[3328,128]{1,0:T(8,128)}, u32[]{:S(2)}, u32[]{:S(2)}) collective-permute-start(f32[3328,128]{1,0:T(8,128)} %get-tuple-element.54), channel_id=1, source_target_pairs={{0,1},{1,0},{2,3},{3,2},{4,5},{5,4},{6,7},{7,6},{8,9},{9,8},{10,11... | collective-permute-start | bytes 5111816 | tf_op jit(solution)/shard_map/ppermute | solution.py:777
  199.3 7.4 %copy-start.3 = (f32[3328,128]{1,0:T(8,128)}, f32[3328,128]{1,0:T(8,128)S(1)}, u32[]{:S(2)}) copy-start(f32[3328,128]{1,0:T(8,128)S(1)} %collective-permute-done) | copy-start | bytes 5111812
  204.2 2.6 copy-start.4
  214.7 19.1 %collective-permute-start.4 = (f32[13,104,128]{2,1,0:T(8,128)}, f32[13,104,128]{2,1,0:T(8,128)S(1)}, u32[]{:S(2)}, u32[]{:S(2)}) collective-permute-start(f32[13,104,128]{2,1,0:T(8,128)} %get-tuple-element.65), channel_id=1, source_target_pairs={{0,32},{32,0},{4,36},{36,4},{10,42},{42,10},{14,46},{46,14},{16,48... | collective-permute-start | bytes 2076680 | tf_op jit(solution)/shard_map/ppermute | solution.py:780
  215.3 18.5 %collective-permute-start.5 = (f32[13,104,128]{2,1,0:T(8,128)}, f32[13,104,128]{2,1,0:T(8,128)S(1)}, u32[]{:S(2)}, u32[]{:S(2)}) collective-permute-start(f32[13,104,128]{2,1,0:T(8,128)} %get-tuple-element.66), channel_id=1, source_target_pairs={{0,96},{96,0},{4,100},{100,4},{10,106},{106,10},{14,110},{110,14},... | collective-permute-start | bytes 2076680 | tf_op jit(solution)/shard_map/ppermute | solution.py:780
  216.1 18.4 %collective-permute-start.6 = (f32[13,104,128]{2,1,0:T(8,128)}, f32[13,104,128]{2,1,0:T(8,128)S(1)}, u32[]{:S(2)}, u32[]{:S(2)}) collective-permute-start(f32[13,104,128]{2,1,0:T(8,128)} %get-tuple-element.67), channel_id=1, source_target_pairs={{0,8},{8,0},{4,12},{12,4},{10,18},{18,10},{14,22},{22,14},{16,24},... | collective-permute-start | bytes 2076680 | tf_op jit(solution)/shard_map/ppermute | solution.py:780
  217.1 17.5 %collective-permute-start.7 = (f32[13,104,128]{2,1,0:T(8,128)}, f32[13,104,128]{2,1,0:T(8,128)S(1)}, u32[]{:S(2)}, u32[]{:S(2)}) collective-permute-start(f32[13,104,128]{2,1,0:T(8,128)} %get-tuple-element.68), channel_id=1, source_target_pairs={{0,24},{24,0},{4,28},{28,4},{10,2},{2,10},{14,6},{6,14},{16,8},{8,... | collective-permute-start | bytes 2076680 | tf_op jit(solution)/shard_map/ppermute | solution.py:780
  217.3 16.2 %collective-permute-start.8 = (f32[12,104,128]{2,1,0:T(8,128)}, f32[12,104,128]{2,1,0:T(8,128)S(1)}, u32[]{:S(2)}, u32[]{:S(2)}) collective-permute-start(f32[12,104,128]{2,1,0:T(8,128)} %get-tuple-element.69), channel_id=1, source_target_pairs={{0,2},{2,0},{4,6},{6,4},{10,12},{12,10},{14,8},{8,14},{16,18},{18,... | collective-permute-start | bytes 1916936 | tf_op jit(solution)/shard_map/ppermute | solution.py:780
  237.7 11.1 %copy-start.1 = (f32[4096,128]{1,0:T(8,128)S(1)}, f32[4096,128]{1,0:T(8,128)}, u32[]{:S(2)}) copy-start(f32[4096,128]{1,0:T(8,128)} %get-tuple-element.63.head_grad) | copy-start | bytes 6291460
  237.7 11.1 %copy-start.2 = (s32[2048]{0:T(1024)S(1)}, s32[2048]{0:T(1024)}, u32[]{:S(2)}) copy-start(s32[2048]{0:T(1024)} %reshape.59.asked) | copy-start | bytes 24580
  237.7 57.0 %all-to-all-start.3 = ((f32[64,104,128]{2,1,0:T(8,128)}), f32[64,104,128]{2,1,0:T(8,128)}, u32[]{:S(2)}, u32[]{:S(2)}) async-start(f32[64,104,128]{2,1,0:T(8,128)} %meet.1), calls=%async_computation.3 | async-start | bytes 6815744 | tf_op jit(solution)/shard_map/all_to_all | solution.py:781
  259.3 1.4 copy-start
Sparse Core Ops, SparseCore 0:
  11.6 75.3 all-gather.1
